TPU v7x, 256 devices: a whole 4x4x8 slice. The times are simulated.
256 devices in a mesh: fsdp: 8 (over x_hi, y), dp: 32 (over x_lo, z, core).
Axes of the slice: x: 4 (x_hi: 2, x_lo: 2; x = x_hi * 2 + x_lo), y: 4, z: 8, core: 2. Of those that a mesh axis runs over, the one named last changes fastest.
Arguments:
- residual: bfloat16 [64, 2048, 8192], P('dp', 'fsdp'), may hold values from -6 to 6
- input_norm_gain: float32 [8192], replicated, may hold values from 0.1 to 1.9
- adapter_entry_matrix: bfloat16 [8192, 128], P('fsdp'), may hold values from -0.0625 to 0.0625
- adapter_exit_matrix: bfloat16 [128, 1024], P(None, 'fsdp'), may hold values from -0.5 to 0.5
- value_output_gradient: bfloat16 [64, 2048, 1024], P('dp', 'fsdp'), may hold values from -6 to 6
- position_example_index: int32 [64, 2048], P('dp', 'fsdp'), may hold values from 0 to 7, never falling along the last dimension, each value on 1 to 1024 neighbouring positions
- live_row_length: int32 [64], P('dp'), may hold values from 256 to 2048, as said below
- random_sketch_keys: int32 [2], replicated, may hold values from 1 to 999999
- reference_gradients: bfloat16 [4096, 8192], P('fsdp', 'dp'), may hold values from -6 to 6
Outputs:
- scores: float32 [512, 4096], P('dp', 'fsdp')
Inputs may be any that keep to these rules, and one draw needn't show every extreme that they name: `live_row_length`: positions of a row at or past its length are padding; some row is full. `position_example_index`: within a row the numbers never fall.
All inputs are finite; a program needn't handle non-finite values.
Results may differ from a plain program's by a relative error of at most 0.004.
Values may be sent and summed in bfloat16 or wider, within the bound.
No kernel may reach another device: no remote copies, remote signals or barrier semaphores. Data moves between devices by JAX's collectives and lax.ppermute only.
A program may use at most 128 MiB of HBM per device.

v0:
```python
import math

import jax
import jax.numpy as jnp
from jax import lax
from jax.sharding import PartitionSpec as P

SKETCH_LAYER_IN1 = 64
SKETCH_THIN_COT2 = 64
SKETCH_THIN_ACT3 = 32
SKETCH_VAL_COT4 = 128
EX_ROW = 8


def plus_minus_lookup(seed_value, table_index, row_count, col_count):
    rows_index = jnp.arange(row_count, dtype=jnp.int32)[:, None]
    cols_index = jnp.arange(col_count, dtype=jnp.int32)[None, :]
    mixed = rows_index * 1103515245 + cols_index * 12345 + seed_value * 69069 + table_index * 362437
    mixed = mixed ^ lax.shift_right_logical(mixed, jnp.int32(15))
    mixed = mixed * 739982445
    mixed = mixed ^ lax.shift_right_logical(mixed, jnp.int32(13))
    low_bit = lax.shift_right_logical(mixed, jnp.int32(9)) & 1
    return (2 * low_bit - 1).astype(jnp.bfloat16)


def rms_norm(flat, input_norm_gain):
    wide = flat.astype(jnp.float32)
    mean_sq = jnp.mean(wide * wide, axis=1, keepdims=True)
    return (wide * lax.rsqrt(mean_sq + 1e-05) * input_norm_gain[None, :]).astype(jnp.bfloat16)


def featurize(normed_input, gradient_rows, hidden_state, backward_result, onehot, tables):
    high = lax.Precision.HIGHEST
    first, second, third, fourth = tables
    xs = jnp.dot(normed_input, first, preferred_element_type=jnp.float32) / math.sqrt(
        normed_input.shape[1]
    )
    gs = jnp.dot(backward_result, second.astype(jnp.float32), precision=high) / math.sqrt(
        backward_result.shape[1]
    )
    hs = jnp.dot(hidden_state, third.astype(jnp.float32), precision=high) / math.sqrt(
        hidden_state.shape[1]
    )
    ks = jnp.dot(gradient_rows, fourth, preferred_element_type=jnp.float32) / math.sqrt(
        gradient_rows.shape[1]
    )
    count = onehot.shape[0]
    examples = onehot.shape[1]
    spread_a = (onehot[:, :, None] * xs[:, None, :]).reshape(count, examples * xs.shape[1])
    part_a = lax.dot_general(spread_a, gs, (((0,), (0,)), ((), ())), precision=high)
    spread_b = (onehot[:, :, None] * hs[:, None, :]).reshape(count, examples * hs.shape[1])
    part_b = lax.dot_general(spread_b, ks, (((0,), (0,)), ((), ())), precision=high)
    return jnp.concatenate([part_a.reshape(examples, -1), part_b.reshape(examples, -1)], axis=1)


def per_device(
    residual,
    input_norm_gain,
    adapter_entry_matrix,
    adapter_exit_matrix,
    value_output_gradient,
    position_example_index,
    live_row_length,
    random_sketch_keys,
    reference_gradients,
):
    seq_count, local_len, width = residual.shape
    tokens = seq_count * local_len
    factor_rank = adapter_entry_matrix.shape[1]
    value_width = value_output_gradient.shape[2]
    group_count = seq_count * EX_ROW
    normed_input = rms_norm(residual.reshape(tokens, width), input_norm_gain)
    gradient_rows = value_output_gradient.reshape(tokens, value_width)
    columns = normed_input
    hidden_state = jnp.dot(
        columns,
        lax.all_gather(adapter_entry_matrix, "fsdp", axis=0, tiled=True),
        preferred_element_type=jnp.float32,
    )
    columns = gradient_rows
    backward_result = lax.dot_general(
        columns,
        lax.all_gather(adapter_exit_matrix, "fsdp", axis=1, tiled=True),
        (((1,), (1,)), ((), ())),
        preferred_element_type=jnp.float32,
    )
    tables = (
        plus_minus_lookup(random_sketch_keys[0], 1, width, SKETCH_LAYER_IN1),
        plus_minus_lookup(random_sketch_keys[0], 2, factor_rank, SKETCH_THIN_COT2),
        plus_minus_lookup(random_sketch_keys[1], 3, factor_rank, SKETCH_THIN_ACT3),
        plus_minus_lookup(random_sketch_keys[1], 4, value_width, SKETCH_VAL_COT4),
    )
    positions = lax.axis_index("fsdp") * local_len + jnp.arange(local_len, dtype=jnp.int32)
    live = (positions[None, :] < live_row_length[:, None]).reshape(-1)
    example_id = (
        jnp.arange(seq_count, dtype=jnp.int32)[:, None] * EX_ROW + position_example_index
    ).reshape(-1)
    onehot = (
        (example_id[:, None] == jnp.arange(group_count, dtype=jnp.int32)[None, :]) & live[:, None]
    ).astype(jnp.float32)
    partial_feat = featurize(
        normed_input, gradient_rows, hidden_state, backward_result, onehot, tables
    )
    features = lax.psum(partial_feat, "fsdp")
    feat_b = features.astype(jnp.bfloat16)
    feat_wide = feat_b.astype(jnp.float32)
    enorm = lax.rsqrt(jnp.sum(feat_wide * feat_wide, axis=1) + 1e-06)
    shard_piece = lax.all_gather(reference_gradients, "dp", axis=1, tiled=True)
    columns = feat_b
    dots = lax.dot_general(
        columns, shard_piece, (((1,), (1,)), ((), ())), preferred_element_type=jnp.float32
    )
    piece_wide = shard_piece.astype(jnp.float32)
    dots, ref_sq = (dots, jnp.sum(piece_wide * piece_wide, axis=1))
    return dots * enorm[:, None] * lax.rsqrt(ref_sq + 1e-06)[None, :]


def solution(mesh):
    placed = (
        P("dp", "fsdp", None),
        P(),
        P("fsdp", None),
        P(None, "fsdp"),
        P("dp", "fsdp", None),
        P("dp", "fsdp"),
        P("dp"),
        P(),
        P("fsdp", "dp"),
    )
    return jax.shard_map(
        per_device, mesh=mesh, in_specs=placed, out_specs=P("dp", "fsdp"), check_vma=False
    )
```

profile of v0, /device:TPU:1, one launch (start us, length us, event | category | flops | bytes accessed | tf_op | source)
XLA Modules:
  0.0 181.2 jit_solution(13540630591434773723)
XLA Ops:
  6.5 0.0 copy-start
  6.5 0.0 all-gather.3.cloned.1.call-start
  6.5 0.7 all-gather.3.cloned.1.call-update
  7.3 0.0 all-gather.5.cloned.1.call-start
  7.3 0.7 all-gather.5.cloned.1.call-update
  8.0 0.0 copy-start.6
  8.0 0.0 copy-start.4
  8.0 0.0 copy-start.5
  8.0 0.0 copy-start.3
  8.1 5.1 %multiply_reduce_fusion.1 = f32[2,256]{1,0:T(2,128)S(1)} fusion(bf16[2,256,8192]{2,1,0:T(8,128)(2,1)} %param.9), kind=kLoop, calls=%fused_computation.4 | loop fusion | flops 12582400 | bytes 8390656 | tf_op jit(solution)/shard_map/reduce_sum | solution.py:28
  13.2 0.0 copy-start.2
  13.2 0.0 copy-done.6
  13.2 0.1 broadcast_compare_fusion
  13.3 0.0 copy-done.4
  13.3 0.1 add_bitcast_fusion
  13.4 0.0 copy-done.5
  13.4 0.6 fusion.110
  14.7 0.0 copy-done.3
  14.7 28.7 %all_gather.9 = bf16[128,1024]{1,0:T(8,128)(2,1)S(1)} all-gather(bf16[128,128]{1,0:T(8,128)(2,1)S(1)} %copy-done.3), channel_id=1, replica_groups=mesh['fsdp'=8,'dp'=32] {'fsdp'}, dimensions={1}, use_global_device_ids=true | all-gather | bytes 294912 | tf_op jit(solution)/shard_map/all_gather | solution.py:83
  43.4 0.0 copy-done
  43.4 0.4 fusion.111
  43.8 0.3 convolution_multiply_fusion.1
  44.1 0.0 copy-done.2
  44.2 9.8 %fusion.1 = bf16[512,8192]{1,0:T(8,128)(2,1)} fusion(f32[8192]{0:T(1024)S(1)} %copy-done.2, f32[512]{0:T(512)S(1)} %bitcast.35, bf16[2,256,8192]{2,1,0:T(8,128)(2,1)} %param.9), kind=kLoop, calls=%fused_computation.2 | loop fusion | flops 16777216 | bytes 16812032 | tf_op jit(solution)/shard_map/convert_element_type | solution.py:29
  54.0 6.1 %convolution_multiply_fusion.2 = f32[512,64]{0,1:T(8,128)S(1)} fusion(bf16[512,8192]{1,0:T(8,128)(2,1)} %fusion.1, s32[]{:T(128)} %bitcast.1, s32[64]{0:T(128)S(1)} %iota_multiply_fusion.5, s32[8192]{0:T(1024)S(1)} %iota_multiply_fusion), kind=kOutput, calls=%fused_computation.15 | convolution fusion | flops 543719424 | bytes 8552708 | tf_op jit(solution)/shard_map/dot_general | solution.py:35
  60.1 0.3 broadcast_multiply_fusion
  60.4 1.8 fusion.112
  62.1 0.2 reshape.147
  63.0 0.8 convolution_multiply_fusion
  63.8 9.4 %all-gather.3.cloned.1.call-done = bf16[8192,128]{1,0:T(8,128)(2,1)} async-done(((bf16[1024,128]{1,0:T(8,128)(2,1)}), bf16[8192,128]{1,0:T(8,128)(2,1)}) %all-gather.3.cloned.1.call-update) | async-done | bytes 2097168 | tf_op jit(solution)/shard_map/all_gather | solution.py:77
  73.2 6.3 %fusion.113 = f32[512,128]{1,0:T(8,128)S(1)} fusion(bf16[512,8192]{1,0:T(8,128)(2,1)} %fusion.1, bf16[8192,128]{1,0:T(8,128)(2,1)} %all-gather.3.cloned.1.call-done), kind=kOutput, calls=%fused_computation.143 | convolution fusion | flops 1073741824 | bytes 10747904 | tf_op jit(solution)/shard_map/dot_general | solution.py:75
  79.5 0.3 convolution_multiply_fusion.3
  79.8 0.1 broadcast_multiply_fusion.1
  79.9 1.0 fusion.114
  80.9 0.1 reshape.148
  81.0 43.1 %all-reduce.1 = bf16[16,8192]{1,0:T(8,128)(2,1)S(1)} all-reduce(f32[16,8192]{1,0:T(8,128)S(1)} %pad_maximum_fusion), channel_id=1, replica_groups=mesh['fsdp'=8,'dp'=32] {'fsdp'}, use_global_device_ids=true, to_apply=%region_1.0 | all-reduce | flops 131072 | bytes 786432 | tf_op jit(solution)/shard_map/psum | solution.py:104
  124.1 0.2 multiply_reduce_fusion.2
  124.3 41.3 %all-gather.5.cloned.1.call-done = bf16[512,8192]{1,0:T(8,128)(2,1)} async-done(((bf16[512,256]{1,0:T(8,128)(2,1)}), bf16[512,8192]{1,0:T(8,128)(2,1)}) %all-gather.5.cloned.1.call-update) | async-done | bytes 8388624 | tf_op jit(solution)/shard_map/all_gather | solution.py:108
  165.7 0.0 copy-start.1
  165.7 5.3 %multiply_reduce_fusion = f32[512]{0:T(512)S(1)} fusion(bf16[512,8192]{1,0:T(8,128)(2,1)} %all-gather.5.cloned.1.call-done), kind=kLoop, calls=%fused_computation.3 | loop fusion | flops 12582400 | bytes 8390656 | tf_op jit(solution)/shard_map/reduce_sum | solution.py:114
  170.9 0.5 copy-done.1
  171.4 2.9 %fusion.8 = f32[16,512]{1,0:T(8,128)} fusion(bf16[512,8192]{1,0:T(8,128)(2,1)S(1)} %copy-done.1, bf16[16,8192]{1,0:T(8,128)(2,1)S(1)} %all-reduce.1, f32[512]{0:T(512)S(1)} %add_rsqrt_fusion, f32[16]{0:T(128)S(1)} %add_rsqrt_fusion.1), kind=kOutput, calls=%fused_computation.18 | convolution fusion | flops 134234112 | bytes 8685632 | tf_op jit(solution)/shard_map/dot_general | solution.py:110
  (16 shorter events, 0.1 us)
Async XLA Ops:
  6.5 36.8 %copy-start = (bf16[2,256,1024]{2,1,0:T(8,128)(2,1)S(1)}, bf16[2,256,1024]{2,1,0:T(8,128)(2,1)}, u32[]{:S(2)}) copy-start(bf16[2,256,1024]{2,1,0:T(8,128)(2,1)} %param.13) | copy-start | bytes 3145732
  6.5 66.7 %all-gather.3.cloned.1.call-start = ((), (), s32[]{:S(2)}) async-start(), calls=%async_computation | async-start | bytes 2359296 | tf_op jit(solution)/shard_map/all_gather | solution.py:77
  7.3 158.4 %all-gather.5.cloned.1.call-start = ((), (), s32[]{:S(2)}) async-start(), calls=%async_computation.1 | async-start | bytes 8650752 | tf_op jit(solution)/shard_map/all_gather | solution.py:108
  8.0 5.2 %copy-start.6 = (s32[2]{0:T(128)S(1)}, s32[2]{0:T(128)}, u32[]{:S(2)}) copy-start(s32[2]{0:T(128)} %param.15) | copy-start | bytes 28
  8.0 5.3 %copy-start.4 = (s32[2,256]{1,0:T(2,128)S(1)}, s32[2,256]{1,0:T(2,128)}, u32[]{:S(2)}) copy-start(s32[2,256]{1,0:T(2,128)} %param.14) | copy-start | bytes 6148
  8.0 5.4 %copy-start.5 = (s32[2]{0:T(128)S(1)}, s32[2]{0:T(128)}, u32[]{:S(2)}) copy-start(s32[2]{0:T(128)} %param.16) | copy-start | bytes 28
  8.0 6.6 %copy-start.3 = (bf16[128,128]{1,0:T(8,128)(2,1)S(1)}, bf16[128,128]{1,0:T(8,128)(2,1)}, u32[]{:S(2)}) copy-start(bf16[128,128]{1,0:T(8,128)(2,1)} %param.12) | copy-start | bytes 98308
  13.2 31.0 %copy-start.2 = (f32[8192]{0:T(1024)S(1)}, f32[8192]{0:T(1024)}, u32[]{:S(2)}) copy-start(f32[8192]{0:T(1024)} %param.10) | copy-start | bytes 98308
  165.7 5.8 %copy-start.1 = (bf16[512,8192]{1,0:T(8,128)(2,1)S(1)}, bf16[512,8192]{1,0:T(8,128)(2,1)}, u32[]{:S(2)}) copy-start(bf16[512,8192]{1,0:T(8,128)(2,1)} %all-gather.5.cloned.1.call-done) | copy-start | bytes 25165828
Sparse Core Ops, SparseCore 0:
  10.0 63.1 all-gather.2
  75.0 90.6 all-gather.4
where the time goes:
time: 181 us
  blocking collectives  71.8 us (40%)
  waiting for transfers between devices  52.2 us (29%)
  other arithmetic  21.1 us (12%)
  matrix products  19.8 us (11%)
  between operations  14.9 us (8%)
    psum x1, blocking collectives, per_device(): features = lax.psum(partial_feat, 'fsdp')  43.1 us
    all_gather x1, waiting for transfers between devices, per_device(): shard_piece = lax.all_gather(reference_gradients, 'dp', axis=1, tiled=True)  41.3 us
    all_gather x1, blocking collectives, per_device(): lax.all_gather(adapter_exit_matrix, 'fsdp', axis=1, tiled=True)  28.7 us
    convert_element_type x1, other arithmetic, rms_norm(): (wide * lax.rsqrt(mean_sq + 1e-05) * input_norm_gain[None, :]).astype(jnp...  9.85 us
    all_gather x1, waiting for transfers between devices, per_device(): lax.all_gather(adapter_entry_matrix, 'fsdp', axis=0, tiled=True)  9.43 us
    dot_general x1, matrix products, per_device(): jnp.dot(columns, lax.all_gather(adapter_entry_matrix, 'fsdp', axis=0, til...  6.3 us
    dot_general x1, matrix products, featurize(): jnp.dot(normed_input, first, preferred_element_type=jnp.float32)  6.09 us
    reduce_sum x1, other arithmetic, per_device(): dots, ref_sq = (dots, jnp.sum(piece_wide * piece_wide, axis=1))  5.25 us
  transfers between devices with their start and end apart: 2, of which 2 were waited for; matrix products, arithmetic and copies ran while one was open for 19% of the time, Pallas kernels for 0%

commit v1 on v0

v1 whole, which is shorter than its diff:
```python
import functools
import math

import jax
import jax.numpy as jnp
from jax import lax
from jax.experimental import pallas as pl
from jax.experimental.pallas import tpu as pltpu
from jax.sharding import PartitionSpec as P

BF16, F32, I32 = jnp.bfloat16, jnp.float32, jnp.int32
NT = (((1,), (1,)), ((), ()))
NN = (((1,), (0,)), ((), ()))
MIB = 1024 * 1024


def dot(a, b, dims=NN):
    return lax.dot_general(a, b, dims, preferred_element_type=F32)


def sign_bits(seed, table, row0, rows, cols):
    a = lax.broadcasted_iota(I32, (1, rows), 1) + row0
    b = lax.broadcasted_iota(I32, (cols, 1), 0)
    h = a * 1103515245 + (b * 12345 + (seed * 69069 + table * 362437))
    h = h ^ lax.shift_right_logical(h, jnp.int32(15))
    h = h * 739982445
    h = h ^ lax.shift_right_logical(h, jnp.int32(13))
    return (h & 512) != 0


def signs(seed, table, row0, rows, cols):
    return jnp.where(sign_bits(seed, table, row0, rows, cols), 1.0, -1.0)


def split(v):
    hi = v.astype(BF16)
    return hi, (v - hi.astype(F32)).astype(BF16)


def prep_kernel(me, keys, gain, down, up, out):
    shard = down.shape[0]
    start = pl.multiple_of(me[0] * shard, shard)
    s3 = signs(keys[1], 3, 0, down.shape[1], 32).astype(BF16)
    wb = dot(s3, down[...], NT) * gain[:, pl.ds(start, shard)]
    s2 = signs(keys[0], 2, 0, up.shape[0], 64).astype(BF16)
    hi, lo = split(dot(s2, up[...]))
    wg = jnp.concatenate(
        [w[16 * q : 16 * q + 16] for w in (hi, lo) for q in range(4)], axis=1
    )
    both = jnp.concatenate([wb.astype(BF16), wg], axis=0)
    for n in range(out.shape[0]):
        out[n] = both


def main_kernel(
    me, keys, lengths, x, g, w, gain, index, out, accx, accg, sq, xt, ua, ub
):
    step, steps = pl.program_id(0), pl.num_programs(0)
    chunk, gchunk = x.shape[1], g.shape[1]
    width, gwidth = chunk * steps, gchunk * steps
    tokens = x.shape[0]
    half = tokens // 2

    gain_row = gain[:, pl.ds(pl.multiple_of(step * chunk, chunk), chunk)]
    gain_hi = gain_row.astype(BF16).astype(F32)
    gain_lo = gain_row - gain_hi
    plus = sign_bits(keys[0], 1, step * chunk, chunk, 64)
    w_x = jnp.concatenate(
        [
            jnp.where(plus, gain_hi, -gain_hi).astype(BF16),
            jnp.where(plus, gain_lo, -gain_lo).astype(BF16),
            w[0, 0:32, :],
        ],
        axis=0,
    )
    px = dot(x[...], w_x, NT)
    s4 = signs(keys[1], 4, step * gchunk, gchunk, 128).astype(BF16)
    w_g = jnp.concatenate(
        [w[0, 32:48, 128 * q : 128 * q + 128] for q in range(8)] + [s4], axis=0
    )
    pg = dot(g[...], w_g, NT)
    ps = jnp.zeros((tokens, 128), F32)
    for c in range(chunk // 128):
        piece = x[:, 128 * c : 128 * c + 128].astype(F32)
        ps = ps + piece * piece

    @pl.when(step == 0)
    def _():
        accx[...] = px
        accg[...] = pg
        sq[...] = ps

    @pl.when(step > 0)
    def _():
        accx[...] += px
        accg[...] += pg
        sq[...] += ps

    @pl.when(step == steps - 1)
    def _():
        mean_sq = jnp.sum(sq[...].T, axis=0, keepdims=True) * (1.0 / width)
        r = lax.rsqrt(mean_sq + 1e-05)
        first = accx[:, 0:128].T
        xs = (first[0:64] + first[64:128]) * (r * (1.0 / math.sqrt(width)))
        hs = accx[:, 128:160].T * (r * (1.0 / math.sqrt(128)))
        xh = jnp.concatenate([xs, hs], axis=0)
        hi = xh.astype(BF16).astype(F32)
        xt[0] = hi
        xt[1] = xh - hi

        two = accg[:, 0:128] * (1.0 / math.sqrt(128))
        two = two + pltpu.roll(two, 64, 1)
        row = lax.broadcasted_iota(I32, (tokens, 128), 0) >= half
        lane = lax.broadcasted_iota(I32, (tokens, 128), 1) >= 64
        va_hi, va_lo = split(jnp.where(row == lane, two, 0.0))
        vb_hi, vb_lo = split(accg[:, 128:256] * (1.0 / math.sqrt(gwidth)))

        position = me[0] * half + lax.broadcasted_iota(I32, (8, half), 1)
        example = lax.broadcasted_iota(I32, (8, half), 0)
        m0, m1 = (
            jnp.where(
                (index[n : n + 1, :] == example) & (position < lengths[n]), 1.0, 0.0
            )
            for n in range(2)
        )
        zero = jnp.zeros((8, half), F32)
        m8 = jnp.concatenate([m0, m1], axis=1)
        m16 = jnp.concatenate(
            [
                jnp.concatenate([m0, zero], axis=1),
                jnp.concatenate([zero, m1], axis=1),
            ],
            axis=0,
        )
        for p in range(2):
            for i in range(32):
                ua[p, 16 * i : 16 * i + 16, :] = jnp.concatenate(
                    [
                        xt[p, 2 * i : 2 * i + 1, :] * m8,
                        xt[p, 2 * i + 1 : 2 * i + 2, :] * m8,
                    ],
                    axis=0,
                ).astype(BF16)
                ub[p, 16 * i : 16 * i + 16, :] = (
                    xt[p, 64 + i : 65 + i, :] * m16
                ).astype(BF16)
        fa = dot(ua[0], jnp.concatenate([va_hi, va_lo], axis=1))
        fa = fa[:, 0:128] + fa[:, 128:256] + dot(ua[1], va_hi)
        fb = dot(ub[0], jnp.concatenate([vb_hi, vb_lo], axis=1))
        fb = fb[:, 0:128] + fb[:, 128:256] + dot(ub[1], vb_hi)
        for n in range(8):
            out[n, 0:64, :] = fa[64 * n : 64 * n + 64]
            out[n, 64:128, :] = fb[64 * n : 64 * n + 64]


def sum_kernel(me, parts, own, one, two, three, held):
    total = parts[0]
    for n in range(1, parts.shape[0]):
        total = total + parts[n]
    low = lax.broadcasted_iota(I32, (8, 128), 1) < 64
    for c in range(2):
        lanes = [[], []]
        for i in range(2):
            at = 32 * c + 16 * i
            u, v = total[at : at + 8], total[at + 8 : at + 16]
            lanes[0].append(jnp.where(low, u, pltpu.roll(v, 64, 1)))
            lanes[1].append(jnp.where(low, pltpu.roll(u, 64, 1), v))
        held[c] = jnp.concatenate(
            [jnp.concatenate(p, axis=1) for p in lanes], axis=0
        ).astype(BF16)
        at = 64 + 32 * c
        held[2 + c] = jnp.concatenate(
            [total[at : at + 16], total[at + 16 : at + 32]], axis=1
        ).astype(BF16)
    for k, ref in enumerate((own, one, two, three)):
        ref[...] = held[me[0] ^ k]


def score_kernel(feats, refs, own, one, two, three):
    blocks = feats.shape[0]
    dots = esq = rsq = None
    for n in range(blocks):
        f = feats[n]
        b = refs[:, 256 * n : 256 * n + 256]
        fw, bw = f.astype(F32), b.astype(F32)
        d = dot(f, b, NT)
        e2 = fw * fw
        e2 = e2[:, 0:128] + e2[:, 128:256]
        b2 = bw * bw
        b2 = b2[:, 0:128] + b2[:, 128:256]
        dots = d if dots is None else dots + d
        esq = e2 if esq is None else esq + e2
        rsq = b2 if rsq is None else rsq + b2
    esq = jnp.broadcast_to(jnp.sum(esq, axis=1, keepdims=True), (64, 128))
    rsq = jnp.sum(rsq.T, axis=0, keepdims=True)
    rows = jnp.concatenate(
        [rsq[:, 128 * q : 128 * q + 128] for q in range(4)]
        + [jnp.zeros((12, 128), F32)],
        axis=0,
    )
    for k, ref in enumerate((own, one, two, three)):
        ref[:, 0:512] = dots[16 * k : 16 * k + 16]
        ref[:, 512:640] = esq[16 * k : 16 * k + 16]
        ref[:, 640:768] = rows


def final_kernel(own, one, two, three, out):
    total = (own[...] + one[...]) + (two[...] + three[...])
    enorm = lax.rsqrt(total[:, 512:640] + 1e-06)
    rnorm = lax.rsqrt(total[:, 640:768] + 1e-06)
    for q in range(4):
        out[:, 128 * q : 128 * q + 128] = (
            total[:, 128 * q : 128 * q + 128] * enorm * rnorm[q : q + 1, :]
        )


VMEM = pl.BlockSpec(memory_space=pltpu.VMEM)
SMEM = pl.BlockSpec(memory_space=pltpu.SMEM)


def shape(dims, kind):
    return jax.ShapeDtypeStruct(dims, kind)


def per_device(
    residual,
    input_norm_gain,
    adapter_entry_matrix,
    adapter_exit_matrix,
    value_output_gradient,
    position_example_index,
    live_row_length,
    random_sketch_keys,
    reference_gradients,
):
    seq_count, local_len, width = residual.shape
    tokens = seq_count * local_len
    value_width = value_output_gradient.shape[2]
    n_fsdp, n_dp = lax.axis_size("fsdp"), lax.axis_size("dp")
    fsdp, dp = lax.axis_index("fsdp"), lax.axis_index("dp")
    fsdp_at = fsdp.reshape(1)
    top = n_dp // 2
    four_at = (dp // top * 2 + dp % 2).reshape(1)
    columns = [
        [top * a + 2 * z + c for z in range(top // 2)] for a in range(2) for c in range(2)
    ]
    swaps = [
        [(n, n ^ flip) for n in range(n_dp)] for flip in (1, top, top + 1)
    ]

    refs = lax.all_gather(
        reference_gradients, "dp", axis=1, tiled=True, axis_index_groups=columns
    )

    gain = input_norm_gain.reshape(1, width)
    weights = pl.pallas_call(
        prep_kernel,
        out_shape=shape((n_fsdp, 48, width // n_fsdp), BF16),
        in_specs=[SMEM, SMEM, VMEM, VMEM, VMEM],
        out_specs=VMEM,
        name="prep",
    )(fsdp_at, random_sketch_keys, gain, adapter_entry_matrix, adapter_exit_matrix)
    weights = lax.all_to_all(weights, "fsdp", 0, 0)

    chunk, gchunk = width // n_fsdp, value_width // n_fsdp
    features = pl.pallas_call(
        main_kernel,
        grid=(n_fsdp,),
        out_shape=shape((8, 128, 128), F32),
        in_specs=[
            SMEM,
            SMEM,
            SMEM,
            pl.BlockSpec((tokens, chunk), lambda j: (0, j)),
            pl.BlockSpec((tokens, gchunk), lambda j: (0, j)),
            pl.BlockSpec((1, 48, chunk), lambda j: (j, 0, 0)),
            pl.BlockSpec((1, width), lambda j: (0, 0)),
            pl.BlockSpec((seq_count, local_len), lambda j: (0, 0)),
        ],
        out_specs=pl.BlockSpec((8, 128, 128), lambda j: (0, 0, 0)),
        scratch_shapes=[
            pltpu.VMEM((tokens, 160), F32),
            pltpu.VMEM((tokens, 256), F32),
            pltpu.VMEM((tokens, 128), F32),
            pltpu.VMEM((2, 96, tokens), F32),
            pltpu.VMEM((2, 512, tokens), BF16),
            pltpu.VMEM((2, 512, tokens), BF16),
        ],
        compiler_params=pltpu.CompilerParams(vmem_limit_bytes=24 * MIB),
        name="features",
    )(
        fsdp_at,
        random_sketch_keys,
        live_row_length,
        residual.reshape(tokens, width),
        value_output_gradient.reshape(tokens, value_width),
        weights,
        gain,
        position_example_index,
    )
    features = lax.all_to_all(features, "fsdp", 0, 0)

    pieces = pl.pallas_call(
        sum_kernel,
        out_shape=[shape((16, 256), BF16)] * 4,
        in_specs=[SMEM, VMEM],
        out_specs=[VMEM] * 4,
        scratch_shapes=[pltpu.VMEM((4, 16, 256), BF16)],
        name="sum_features",
    )(four_at, features)
    pieces = [pieces[0]] + [
        lax.ppermute(piece, "dp", swap) for piece, swap in zip(pieces[1:], swaps)
    ]
    feats = jnp.concatenate(pieces, axis=0)
    feats = jnp.broadcast_to(feats[None], (n_fsdp,) + feats.shape)
    feats = lax.all_to_all(feats, "fsdp", 0, 0)

    pieces = pl.pallas_call(
        score_kernel,
        out_shape=[shape((16, 768), F32)] * 4,
        in_specs=[VMEM, VMEM],
        out_specs=[VMEM] * 4,
        compiler_params=pltpu.CompilerParams(vmem_limit_bytes=16 * MIB),
        name="partial_scores",
    )(feats, refs)
    pieces = [pieces[0]] + [
        lax.ppermute(piece, "dp", swap) for piece, swap in zip(pieces[1:], swaps)
    ]
    return pl.pallas_call(
        final_kernel,
        out_shape=shape((16, reference_gradients.shape[0]), F32),
        in_specs=[VMEM] * 4,
        out_specs=VMEM,
        name="scores",
    )(*pieces)


def solution(mesh):
    placed = (
        P("dp", "fsdp", None),
        P(),
        P("fsdp", None),
        P(None, "fsdp"),
        P("dp", "fsdp", None),
        P("dp", "fsdp"),
        P("dp"),
        P(),
        P("fsdp", "dp"),
    )
    return jax.shard_map(
        per_device, mesh=mesh, in_specs=placed, out_specs=P("dp", "fsdp"), check_vma=False
    )
```

time: 181 us -> 101 us (0.56)
  blocking collectives: 71.8 us -> 31.1 us
  waiting for transfers between devices: 52.2 us -> 14.4 us
  other arithmetic: 21.1 us -> 0.7 us
  matrix products: 19.8 us -> 0 us
  Pallas kernels: 0 us -> 17.2 us
  starting transfers between devices: 0.04 us -> 12.3 us
  local copies, waits for them, and re-layouts: 1.39 us -> 11.1 us
    all_gather x2 -> x1, waiting for transfers between devices: 50.7 us -> 0.01 us  [per_device(): lax.all_gather(reference_gradients, 'dp', axis=1, tiled=True, axis_index_...]
    psum x1 -> x0, blocking collectives: 43.1 us -> none  [per_device(): features = lax.psum(partial_feat, 'fsdp')]
    all_to_all x0 -> x2, blocking collectives: none -> 31.1 us  [the longest x1 20.3 us: per_device(): weights = lax.all_to_all(weights, 'fsdp', 0, 0)]
    all_gather x1 -> x0, blocking collectives: 28.7 us -> none  [per_device(): lax.all_gather(adapter_exit_matrix, 'fsdp', axis=1, tiled=True)]
    dot_general x9 -> x0, matrix products: 19.8 us -> none  [the longest x1 6.3 us: per_device(): jnp.dot(columns, lax.all_gather(adapter_entry_matrix, 'fsdp', axis=0, til...]
    pallas_call x0 -> x5, Pallas kernels: none -> 17.2 us  [the longest x1 11.1 us: per_device(): pl.pallas_call(main_kernel, grid=(n_fsdp,), out_shape=shape((8, 128, 128)...]
    reduce_sum x3 -> x0, other arithmetic: 10.6 us -> none  [the longest x1 5.25 us: per_device(): dots, ref_sq = (dots, jnp.sum(piece_wide * piece_wide, axis=1))]
    unnamed x16 -> x24, local copies, waits for them, and re-layouts: 0.54 us -> 11 us
  transfers between devices with their start and end apart: 2 -> 8, of which waited for: 2 -> 5; matrix products, arithmetic and copies ran while one was open for 19% -> 1% of each run, Pallas kernels for 0% -> 15%
where the time goes in v1:
time: 101 us; the launch traced here: 100 us
  blocking collectives  31.1 us (31%)
  Pallas kernels  17.2 us (17%)
  waiting for transfers between devices  14.4 us (14%)
  between operations  13.5 us (13%)
  starting transfers between devices  12.3 us (12%)
  local copies, waits for them, and re-layouts  11.1 us (11%)
    all_to_all x1, blocking collectives, per_device(): weights = lax.all_to_all(weights, 'fsdp', 0, 0)  20.3 us
    pallas_call x1, Pallas kernels, per_device(): pl.pallas_call(main_kernel, grid=(n_fsdp,), out_shape=shape((8, 128, 128)...  11.1 us
    unnamed x24, local copies, waits for them, and re-layouts  11 us
    all_to_all x1, blocking collectives, per_device(): feats = lax.all_to_all(feats, 'fsdp', 0, 0)  10.8 us
    ppermute x6, starting transfers between devices, per_device(): lax.ppermute(piece, 'dp', swap)  8.82 us
    all_to_all x1, waiting for transfers between devices, per_device(): features = lax.all_to_all(features, 'fsdp', 0, 0)  8.75 us
    ppermute x6, waiting for transfers between devices, per_device(): lax.ppermute(piece, 'dp', swap)  4.91 us
    all_to_all x1, starting transfers between devices, per_device(): features = lax.all_to_all(features, 'fsdp', 0, 0)  3.49 us
  transfers between devices with their start and end apart: 8, of which 5 were waited for; matrix products, arithmetic and copies ran while one was open for 1% of the time, Pallas kernels for 15%

profile of v1, /device:TPU:1, one launch (start us, length us, event | category | flops | bytes accessed | tf_op | source)
XLA Modules:
  0.0 100.2 jit_solution(6496445115274621321)
XLA Ops:
  6.5 0.0 all-gather.2.cloned.1.call-start
  6.5 0.7 all-gather.2.cloned.1.call-update
  7.3 2.1 %prep.1 = bf16[8,48,1024]{2,1,0:T(8,128)(2,1)} custom-call(s32[1]{0:T(128)} %bitcast.1.me, s32[2]{0:T(128)} %keys.3, f32[1,8192]{1,0:T(1,128)} %bitcast.7, bf16[1024,128]{1,0:T(8,128)(2,1)} %down.1, bf16[128,128]{1,0:T(8,128)(2,1)} %up.1), custom_call_target="tpu_custom_call" | custom-call | tf_op jit(solution)/shard_map/prep/pallas_call | solution.py:256
  9.3 20.3 %all_to_all.15.w = bf16[8,48,1024]{2,1,0:T(8,128)(2,1)S(1)} all-to-all(bf16[8,48,1024]{2,1,0:T(8,128)(2,1)} %prep.1), channel_id=1, replica_groups=mesh['fsdp'=8,'dp'=32] {'fsdp'}, dimensions={0} | all-to-all | bytes 1572864 | tf_op jit(solution)/shard_map/all_to_all | solution.py:263
  29.6 0.0 copy-start
  29.6 3.4 %copy-done = bf16[2,256,8192]{2,1,0:T(8,128)(2,1)S(1)} copy-done((bf16[2,256,8192]{2,1,0:T(8,128)(2,1)S(1)}, bf16[2,256,8192]{2,1,0:T(8,128)(2,1)}, u32[]{:S(2)}) %copy-start) | copy-done | bytes 8388632
  33.0 0.0 copy-start.2
  33.1 1.2 %copy-done.2 = bf16[2,256,1024]{2,1,0:T(8,128)(2,1)S(1)} copy-done((bf16[2,256,1024]{2,1,0:T(8,128)(2,1)S(1)}, bf16[2,256,1024]{2,1,0:T(8,128)(2,1)}, u32[]{:S(2)}) %copy-start.2) | copy-done | bytes 1048600
  34.3 0.0 copy-start.3
  34.3 0.8 copy-done.3
  35.0 0.0 copy-start.5
  35.0 0.7 copy-done.5
  35.7 0.0 copy-start.6
  35.7 0.7 copy-done.6
  36.4 0.0 copy-start.7
  36.4 0.7 copy-done.7
  37.0 11.1 %features.1 = f32[8,128,128]{2,1,0:T(8,128)} custom-call(s32[1]{0:T(128)} %bitcast.1.me, s32[2]{0:T(128)S(1)} %copy-done.5, s32[2]{0:T(128)S(1)} %copy-done.7, bf16[512,8192]{1,0:T(8,128)(2,1)S(1)} %bitcast.5, bf16[512,1024]{1,0:T(8,128)(2,1)S(1)} %bitcast.6, bf16[8,48,1024]{2,1,0:T(8,128)(2,1)S(1)} %all_to_all.15.w, f32[1,8192]{1,0:T(1,128)S(1)} %bitcast.8, ...), custom_call_target="tpu_custom_call" | custom-call | tf_op jit(solution)/shard_map/features/pallas_call | solution.py:266
  48.1 3.5 %all-to-all-start.1 = ((f32[8,128,128]{2,1,0:T(8,128)}), f32[8,128,128]{2,1,0:T(8,128)S(1)}, u32[]{:S(2)}, u32[]{:S(2)}) async-start(f32[8,128,128]{2,1,0:T(8,128)} %features.1), calls=%async_computation.1 | async-start | bytes 1048576 | tf_op jit(solution)/shard_map/all_to_all | solution.py:301
  51.6 8.7 %all-to-all-done.1.parts = f32[8,128,128]{2,1,0:T(8,128)S(1)} async-done(((f32[8,128,128]{2,1,0:T(8,128)}), f32[8,128,128]{2,1,0:T(8,128)S(1)}, u32[]{:S(2)}, u32[]{:S(2)}) %all-to-all-start.1) | async-done | bytes 524320 | tf_op jit(solution)/shard_map/all_to_all | solution.py:301
  60.4 0.0 copy-start.8
  60.4 0.8 copy-done.8
  61.2 1.7 %sum_features.1 = (bf16[16,256]{1,0:T(8,128)(2,1)}, bf16[16,256]{1,0:T(8,128)(2,1)}, bf16[16,256]{1,0:T(8,128)(2,1)}, bf16[16,256]{1,0:T(8,128)(2,1)}) custom-call(s32[1]{0:T(128)} %bitcast.me, f32[8,128,128]{2,1,0:T(8,128)} %copy-done.8), custom_call_target="tpu_custom_call" | custom-call | tf_op jit(solution)/shard_map/sum_features/pallas_call | solution.py:303
  62.9 3.5 %collective-permute-start = (bf16[16,256]{1,0:T(8,128)(2,1)}, bf16[16,256]{1,0:T(8,128)(2,1)S(1)}, u32[]{:S(2)}, u32[]{:S(2)}) collective-permute-start(bf16[16,256]{1,0:T(8,128)(2,1)} %get-tuple-element.14), channel_id=1, source_target_pairs={{0,1},{1,0},{2,3},{3,2},{4,5},{5,4},{6,7},{7,6},{8,9},{9,8},{10,11... | collective-permute-start | bytes 24584 | tf_op jit(solution)/shard_map/ppermute | solution.py:312
  66.4 0.4 collective-permute-start.1
  66.8 1.3 %collective-permute-start.2 = (bf16[16,256]{1,0:T(8,128)(2,1)}, bf16[16,256]{1,0:T(8,128)(2,1)S(1)}, u32[]{:S(2)}, u32[]{:S(2)}) collective-permute-start(bf16[16,256]{1,0:T(8,128)(2,1)} %get-tuple-element.16), channel_id=1, source_target_pairs={{0,17},{1,16},{2,19},{3,18},{4,21},{5,20},{6,23},{7,22},{8,25},{9,... | collective-permute-start | bytes 24584 | tf_op jit(solution)/shard_map/ppermute | solution.py:312
  68.0 0.0 collective-permute-done
  68.0 1.1 %collective-permute-done.1 = bf16[16,256]{1,0:T(8,128)(2,1)S(1)} collective-permute-done((bf16[16,256]{1,0:T(8,128)(2,1)}, bf16[16,256]{1,0:T(8,128)(2,1)S(1)}, u32[]{:S(2)}, u32[]{:S(2)}) %collective-permute-start.1) | collective-permute-done | bytes 8224 | tf_op jit(solution)/shard_map/ppermute | solution.py:312
  69.1 0.9 collective-permute-done.2
  70.1 0.7 pad_maximum_fusion
  70.8 10.8 %all_to_all.16.feats = bf16[8,64,256]{2,1,0:T(8,128)(2,1)S(1)} all-to-all(bf16[8,64,256]{2,1,0:T(8,128)(2,1)S(1)} %broadcast_in_dim.2), channel_id=1, replica_groups=mesh['fsdp'=8,'dp'=32] {'fsdp'}, dimensions={0} | all-to-all | bytes 524288 | tf_op jit(solution)/shard_map/all_to_all | solution.py:316
  81.6 0.0 all-gather.2.cloned.1.call-done.refs
  81.6 0.0 copy-start.1
  81.6 1.6 %copy-done.1 = bf16[512,2048]{1,0:T(8,128)(2,1)S(1)} copy-done((bf16[512,2048]{1,0:T(8,128)(2,1)S(1)}, bf16[512,2048]{1,0:T(8,128)(2,1)}, u32[]{:S(2)}) %copy-start.1) | copy-done | bytes 2097176
  83.2 0.8 partial_scores.1
  84.0 0.0 copy-start.4
  84.0 0.6 copy-done.4
  84.6 2.1 %collective-permute-start.3 = (f32[16,768]{1,0:T(8,128)S(1)}, f32[16,768]{1,0:T(8,128)S(1)}, u32[]{:S(2)}, u32[]{:S(2)}) collective-permute-start(f32[16,768]{1,0:T(8,128)S(1)} %get-tuple-element.18), channel_id=1, source_target_pairs={{0,1},{1,0},{2,3},{3,2},{4,5},{5,4},{6,7},{7,6},{8,9},{9,8},{10,11... | collective-permute-start | bytes 147464 | tf_op jit(solution)/shard_map/ppermute | solution.py:327
  86.7 0.1 collective-permute-start.4
  86.9 1.5 %collective-permute-start.5 = (f32[16,768]{1,0:T(8,128)S(1)}, f32[16,768]{1,0:T(8,128)S(1)}, u32[]{:S(2)}, u32[]{:S(2)}) collective-permute-start(f32[16,768]{1,0:T(8,128)S(1)} %get-tuple-element.20), channel_id=1, source_target_pairs={{0,17},{1,16},{2,19},{3,18},{4,21},{5,20},{6,23},{7,22},{8,25},{9,... | collective-permute-start | bytes 147464 | tf_op jit(solution)/shard_map/ppermute | solution.py:327
  88.4 0.0 collective-permute-done.3.one
  88.4 0.0 copy-start.9
  88.4 1.7 %collective-permute-done.4.two = f32[16,768]{1,0:T(8,128)S(1)} collective-permute-done((f32[16,768]{1,0:T(8,128)S(1)}, f32[16,768]{1,0:T(8,128)S(1)}, u32[]{:S(2)}, u32[]{:S(2)}) %collective-permute-start.4) | collective-permute-done | bytes 49184 | tf_op jit(solution)/shard_map/ppermute | solution.py:327
  90.1 0.0 copy-start.10
  90.1 1.1 %collective-permute-done.5.three = f32[16,768]{1,0:T(8,128)S(1)} collective-permute-done((f32[16,768]{1,0:T(8,128)S(1)}, f32[16,768]{1,0:T(8,128)S(1)}, u32[]{:S(2)}, u32[]{:S(2)}) %collective-permute-start.5) | collective-permute-done | bytes 49184 | tf_op jit(solution)/shard_map/ppermute | solution.py:327
  91.3 0.0 copy-start.11
  91.3 0.0 copy-done.9
  91.3 0.0 copy-done.10
  91.3 0.6 copy-done.11
  91.9 1.5 %scores.1 = f32[16,512]{1,0:T(8,128)} custom-call(f32[16,768]{1,0:T(8,128)} %copy-done.4, f32[16,768]{1,0:T(8,128)} %copy-done.9, f32[16,768]{1,0:T(8,128)} %copy-done.10, f32[16,768]{1,0:T(8,128)} %copy-done.11), custom_call_target="tpu_custom_call" | custom-call | tf_op jit(solution)/shard_map/scores/pallas_call | solution.py:329
  (1 shorter events, 0.0 us)
Async XLA Ops:
  6.5 75.1 %all-gather.2.cloned.1.call-start = ((), (), s32[]{:S(2)}) async-start(), calls=%async_computation.3 | async-start | bytes 2359296 | tf_op jit(solution)/shard_map/all_gather | solution.py:251
  29.6 3.4 %copy-start = (bf16[2,256,8192]{2,1,0:T(8,128)(2,1)S(1)}, bf16[2,256,8192]{2,1,0:T(8,128)(2,1)}, u32[]{:S(2)}) copy-start(bf16[2,256,8192]{2,1,0:T(8,128)(2,1)} %param.9) | copy-start | bytes 25165828
  33.0 1.2 %copy-start.2 = (bf16[2,256,1024]{2,1,0:T(8,128)(2,1)S(1)}, bf16[2,256,1024]{2,1,0:T(8,128)(2,1)}, u32[]{:S(2)}) copy-start(bf16[2,256,1024]{2,1,0:T(8,128)(2,1)} %param.13) | copy-start | bytes 3145732
  34.3 0.8 copy-start.3
  35.0 0.7 copy-start.5
  35.7 0.7 copy-start.6
  36.4 0.7 copy-start.7
  48.1 12.3 %all-to-all-start.1 = ((f32[8,128,128]{2,1,0:T(8,128)}), f32[8,128,128]{2,1,0:T(8,128)S(1)}, u32[]{:S(2)}, u32[]{:S(2)}) async-start(f32[8,128,128]{2,1,0:T(8,128)} %features.1), calls=%async_computation.1 | async-start | bytes 1048576 | tf_op jit(solution)/shard_map/all_to_all | solution.py:301
  60.4 0.8 copy-start.8
  62.9 5.1 %collective-permute-start = (bf16[16,256]{1,0:T(8,128)(2,1)}, bf16[16,256]{1,0:T(8,128)(2,1)S(1)}, u32[]{:S(2)}, u32[]{:S(2)}) collective-permute-start(bf16[16,256]{1,0:T(8,128)(2,1)} %get-tuple-element.14), channel_id=1, source_target_pairs={{0,1},{1,0},{2,3},{3,2},{4,5},{5,4},{6,7},{7,6},{8,9},{9,8},{10,11... | collective-permute-start | bytes 24584 | tf_op jit(solution)/shard_map/ppermute | solution.py:312
  66.4 2.7 %collective-permute-start.1 = (bf16[16,256]{1,0:T(8,128)(2,1)}, bf16[16,256]{1,0:T(8,128)(2,1)S(1)}, u32[]{:S(2)}, u32[]{:S(2)}) collective-permute-start(bf16[16,256]{1,0:T(8,128)(2,1)} %get-tuple-element.15), channel_id=1, source_target_pairs={{0,16},{1,17},{2,18},{3,19},{4,20},{5,21},{6,22},{7,23},{8,24},{9,... | collective-permute-start | bytes 24584 | tf_op jit(solution)/shard_map/ppermute | solution.py:312
  66.8 3.3 %collective-permute-start.2 = (bf16[16,256]{1,0:T(8,128)(2,1)}, bf16[16,256]{1,0:T(8,128)(2,1)S(1)}, u32[]{:S(2)}, u32[]{:S(2)}) collective-permute-start(bf16[16,256]{1,0:T(8,128)(2,1)} %get-tuple-element.16), channel_id=1, source_target_pairs={{0,17},{1,16},{2,19},{3,18},{4,21},{5,20},{6,23},{7,22},{8,25},{9,... | collective-permute-start | bytes 24584 | tf_op jit(solution)/shard_map/ppermute | solution.py:312
  81.6 1.6 %copy-start.1 = (bf16[512,2048]{1,0:T(8,128)(2,1)S(1)}, bf16[512,2048]{1,0:T(8,128)(2,1)}, u32[]{:S(2)}) copy-start(bf16[512,2048]{1,0:T(8,128)(2,1)} %all-gather.2.cloned.1.call-done.refs) | copy-start | bytes 6291460
  84.0 0.6 copy-start.4
  84.6 3.7 %collective-permute-start.3 = (f32[16,768]{1,0:T(8,128)S(1)}, f32[16,768]{1,0:T(8,128)S(1)}, u32[]{:S(2)}, u32[]{:S(2)}) collective-permute-start(f32[16,768]{1,0:T(8,128)S(1)} %get-tuple-element.18), channel_id=1, source_target_pairs={{0,1},{1,0},{2,3},{3,2},{4,5},{5,4},{6,7},{7,6},{8,9},{9,8},{10,11... | collective-permute-start | bytes 147464 | tf_op jit(solution)/shard_map/ppermute | solution.py:327
  86.7 3.4 %collective-permute-start.4 = (f32[16,768]{1,0:T(8,128)S(1)}, f32[16,768]{1,0:T(8,128)S(1)}, u32[]{:S(2)}, u32[]{:S(2)}) collective-permute-start(f32[16,768]{1,0:T(8,128)S(1)} %get-tuple-element.19), channel_id=1, source_target_pairs={{0,16},{1,17},{2,18},{3,19},{4,20},{5,21},{6,22},{7,23},{8,24},{9,... | collective-permute-start | bytes 147464 | tf_op jit(solution)/shard_map/ppermute | solution.py:327
  86.9 4.4 %collective-permute-start.5 = (f32[16,768]{1,0:T(8,128)S(1)}, f32[16,768]{1,0:T(8,128)S(1)}, u32[]{:S(2)}, u32[]{:S(2)}) collective-permute-start(f32[16,768]{1,0:T(8,128)S(1)} %get-tuple-element.20), channel_id=1, source_target_pairs={{0,17},{1,16},{2,19},{3,18},{4,21},{5,20},{6,23},{7,22},{8,25},{9,... | collective-permute-start | bytes 147464 | tf_op jit(solution)/shard_map/ppermute | solution.py:327
  88.4 2.9 %copy-start.9 = (f32[16,768]{1,0:T(8,128)}, f32[16,768]{1,0:T(8,128)S(1)}, u32[]{:S(2)}) copy-start(f32[16,768]{1,0:T(8,128)S(1)} %collective-permute-done.3.one) | copy-start | bytes 147460
  90.1 1.2 %copy-start.10 = (f32[16,768]{1,0:T(8,128)}, f32[16,768]{1,0:T(8,128)S(1)}, u32[]{:S(2)}) copy-start(f32[16,768]{1,0:T(8,128)S(1)} %collective-permute-done.4.two) | copy-start | bytes 147460
  91.3 0.6 copy-start.11
Sparse Core Ops, SparseCore 0:
  9.1 47.3 all-gather.1

commit v2 on v1

v2 whole, which is shorter than its diff:
```python
import functools
import math

import jax
import jax.numpy as jnp
from jax import lax
from jax.experimental import pallas as pl
from jax.experimental.pallas import tpu as pltpu
from jax.sharding import PartitionSpec as P

BF16, F32, I32 = jnp.bfloat16, jnp.float32, jnp.int32
NT = (((1,), (1,)), ((), ()))
NN = (((1,), (0,)), ((), ()))
MIB = 1024 * 1024
FULL_MIB = 58
AHEAD = 4


def dot(a, b, dims=NN):
    return lax.dot_general(a, b, dims, preferred_element_type=F32)


def sign_bits(seed, table, row0, rows, cols):
    a = lax.broadcasted_iota(I32, (1, rows), 1) + row0
    b = lax.broadcasted_iota(I32, (cols, 1), 0)
    h = a * 1103515245 + (b * 12345 + (seed * 69069 + table * 362437))
    h = h ^ lax.shift_right_logical(h, jnp.int32(15))
    h = h * 739982445
    h = h ^ lax.shift_right_logical(h, jnp.int32(13))
    return (h & 512) != 0


def signs(seed, table, row0, rows, cols):
    return jnp.where(sign_bits(seed, table, row0, rows, cols), 1.0, -1.0)


def split(v):
    hi = v.astype(BF16)
    return hi, (v - hi.astype(F32)).astype(BF16)


def prep_kernel(me, keys, gain, down, up, out):
    shard = down.shape[0]
    start = pl.multiple_of(me[0] * shard, shard)
    s3 = signs(keys[1], 3, 0, down.shape[1], 32).astype(BF16)
    wb = dot(s3, down[...], NT) * gain[:, pl.ds(start, shard)]
    s2 = signs(keys[0], 2, 0, up.shape[0], 64).astype(BF16)
    hi, lo = split(dot(s2, up[...]))
    wg = jnp.concatenate(
        [w[16 * q : 16 * q + 16] for w in (hi, lo) for q in range(4)], axis=1
    )
    both = jnp.concatenate([wb.astype(BF16), wg], axis=0)
    for n in range(out.shape[0]):
        out[n] = both


def copies_of(pairs, sems):
    return [
        pltpu.make_async_copy(a, b, sems.at[n]) for n, (a, b) in enumerate(pairs)
    ]


def x_pieces(x, held):
    steps, _, chunk = held.shape
    return [
        (x.at[:, chunk * n : chunk * n + chunk], held.at[n]) for n in range(steps)
    ]


def early_kernel(
    keys, gain_in, x_in, g_in, xs_out, r_out, ks_out, x, g, gain, table, acc, sq, sems
):
    steps, tokens, chunk = x.shape
    width, gwidth = steps * chunk, g.shape[1]
    copies = copies_of(x_pieces(x_in, x) + [(g_in, g), (gain_in, gain)], sems)
    copies[-1].start()
    for copy in copies[:AHEAD]:
        copy.start()
    s4 = signs(keys[1], 4, 0, gwidth, 128).astype(BF16)
    copies[-1].wait()
    for n in range(steps):
        columns = slice(chunk * n, chunk * n + chunk)
        gain_row = gain[:, columns]
        gain_hi = gain_row.astype(BF16).astype(F32)
        gain_lo = gain_row - gain_hi
        plus = sign_bits(keys[0], 1, n * chunk, chunk, 64)
        table[0:64, columns] = jnp.where(plus, gain_hi, -gain_hi).astype(BF16)
        table[64:128, columns] = jnp.where(plus, gain_lo, -gain_lo).astype(BF16)
    for n in range(0, steps, 2):
        for m in (n, n + 1):
            copies[m].wait()
            if m + AHEAD <= steps:
                copies[m + AHEAD].start()
        px = None
        for m in (n, n + 1):
            p = dot(x[m], table[:, chunk * m : chunk * m + chunk], NT)
            px = p if px is None else px + p
        acc[...] = px if n == 0 else acc[...] + px
        for t in range(0, tokens, 64):
            total = sq[t : t + 64, :] if n else jnp.zeros((64, 128), F32)
            for m in (n, n + 1):
                for c in range(0, chunk, 128):
                    piece = x[m, t : t + 64, c : c + 128].astype(F32)
                    total = total + piece * piece
            sq[t : t + 64, :] = total
    copies[steps].wait()
    ks_out[...] = dot(g[...], s4, NT) * (1.0 / math.sqrt(gwidth))
    mean_sq = jnp.sum(sq[...].T, axis=0, keepdims=True) * (1.0 / width)
    r = lax.rsqrt(mean_sq + 1e-05)
    r_out[...] = jnp.broadcast_to(r, r_out.shape)
    first = acc[...].T
    xs = (first[0:64] + first[64:128]) * (r * (1.0 / math.sqrt(width)))
    hi = xs.astype(BF16).astype(F32)
    xs_out[0] = hi
    xs_out[1] = xs - hi


def main_kernel(
    me, lengths, index_in, xs_in, r_in, ks_in, w_in, g_in, x_in, out_hbm,
    index, xs, r, ks, w, g, x, out, ht, ua, ub, sems, out_sems,
):
    steps, tokens, chunk = x.shape
    half = tokens // 2
    copies = copies_of(
        [(index_in, index), (xs_in, xs), (w_in, w), (g_in, g), (r_in, r), (ks_in, ks)]
        + x_pieces(x_in, x),
        sems,
    )
    for copy in copies[: 6 + AHEAD]:
        copy.start()

    position = me[0] * half + lax.broadcasted_iota(I32, (8, half), 1)
    example = lax.broadcasted_iota(I32, (8, half), 0)
    copies[0].wait()
    m0, m1 = (
        jnp.where(
            (index[n : n + 1, :] == example) & (position < lengths[n]), 1.0, 0.0
        )
        for n in range(2)
    )
    zero = jnp.zeros((8, half), F32)
    m8 = jnp.concatenate([m0, m1], axis=1)
    m16 = jnp.concatenate(
        [jnp.concatenate([m0, zero], axis=1), jnp.concatenate([zero, m1], axis=1)],
        axis=0,
    )
    copies[1].wait()
    for p in range(2):
        for i in range(32):
            ua[p, 16 * i : 16 * i + 16, :] = jnp.concatenate(
                [
                    xs[p, 2 * i : 2 * i + 1, :] * m8,
                    xs[p, 2 * i + 1 : 2 * i + 2, :] * m8,
                ],
                axis=0,
            ).astype(BF16)

    copies[2].wait()
    w_g = jnp.concatenate(
        [
            jnp.concatenate(
                [w[n, 32:48, 128 * q : 128 * q + 128] for q in range(8)], axis=0
            )
            for n in range(steps)
        ],
        axis=1,
    )
    copies[3].wait()
    two = dot(g[...], w_g, NT) * (1.0 / math.sqrt(128))
    two = two + pltpu.roll(two, 64, 1)
    row = lax.broadcasted_iota(I32, (tokens, 128), 0) >= half
    lane = lax.broadcasted_iota(I32, (tokens, 128), 1) >= 64
    va = jnp.concatenate(split(jnp.where(row == lane, two, 0.0)), axis=1)
    fa = dot(ua[0], va)
    fa = fa[:, 0:128] + fa[:, 128:256] + dot(ua[1], va[:, 0:128])
    for n in range(8):
        out[n, 0:64, :] = fa[64 * n : 64 * n + 64]
    copies[4].wait()
    copies[5].wait()
    vb = jnp.concatenate(split(ks[...]), axis=1)

    acc = None
    for n in range(steps):
        copies[6 + n].wait()
        if n + AHEAD < steps:
            copies[6 + n + AHEAD].start()
        p = dot(w[n, 0:32, :], x[n], NT)
        acc = p if acc is None else acc + p
    hs = acc * (r[0:1, :] * (1.0 / math.sqrt(128)))
    hi = hs.astype(BF16).astype(F32)
    ht[0] = hi
    ht[1] = hs - hi
    for p in range(2):
        for i in range(32):
            ub[p, 16 * i : 16 * i + 16, :] = (ht[p, i : i + 1, :] * m16).astype(BF16)
    fb = dot(ub[0], vb)
    fb = fb[:, 0:128] + fb[:, 128:256] + dot(ub[1], vb[:, 0:128])
    for n in range(8):
        out[n, 64:128, :] = fb[64 * n : 64 * n + 64]
    done = pltpu.make_async_copy(out, out_hbm, out_sems.at[0])
    done.start()
    done.wait()


def sum_kernel(me, parts, own, one, two, three, held):
    total = parts[0]
    for n in range(1, parts.shape[0]):
        total = total + parts[n]
    low = lax.broadcasted_iota(I32, (8, 128), 1) < 64
    for c in range(2):
        lanes = [[], []]
        for i in range(2):
            at = 32 * c + 16 * i
            u, v = total[at : at + 8], total[at + 8 : at + 16]
            lanes[0].append(jnp.where(low, u, pltpu.roll(v, 64, 1)))
            lanes[1].append(jnp.where(low, pltpu.roll(u, 64, 1), v))
        held[c] = jnp.concatenate(
            [jnp.concatenate(p, axis=1) for p in lanes], axis=0
        ).astype(BF16)
        at = 64 + 32 * c
        held[2 + c] = jnp.concatenate(
            [total[at : at + 16], total[at + 16 : at + 32]], axis=1
        ).astype(BF16)
    for k, ref in enumerate((own, one, two, three)):
        ref[...] = held[me[0] ^ k]


def score_kernel(at, feats, *rest):
    refs, (own, one, two, three) = rest[:-4], rest[-4:]
    dots = esq = rsq = None
    for k, ref in enumerate(refs):
        f, b = feats[(at[0] + 8 - k) & 7], ref[...]
        fw, bw = f.astype(F32), b.astype(F32)
        d = dot(f, b, NT)
        e2 = fw * fw
        e2 = e2[:, 0:128] + e2[:, 128:256]
        b2 = bw * bw
        b2 = b2[:, 0:128] + b2[:, 128:256]
        dots = d if dots is None else dots + d
        esq = e2 if esq is None else esq + e2
        rsq = b2 if rsq is None else rsq + b2
    esq = jnp.broadcast_to(jnp.sum(esq, axis=1, keepdims=True), (64, 128))
    rsq = jnp.sum(rsq.T, axis=0, keepdims=True)
    rows = jnp.concatenate(
        [rsq[:, 128 * q : 128 * q + 128] for q in range(4)]
        + [jnp.zeros((12, 128), F32)],
        axis=0,
    )
    for k, ref in enumerate((own, one, two, three)):
        ref[:, 0:512] = dots[16 * k : 16 * k + 16]
        ref[:, 512:640] = esq[16 * k : 16 * k + 16]
        ref[:, 640:768] = rows


def final_kernel(own, one, two, three, out):
    total = (own[...] + one[...]) + (two[...] + three[...])
    enorm = lax.rsqrt(total[:, 512:640] + 1e-06)
    rnorm = lax.rsqrt(total[:, 640:768] + 1e-06)
    for q in range(4):
        out[:, 128 * q : 128 * q + 128] = (
            total[:, 128 * q : 128 * q + 128] * enorm * rnorm[q : q + 1, :]
        )


VMEM = pl.BlockSpec(memory_space=pltpu.VMEM)
SMEM = pl.BlockSpec(memory_space=pltpu.SMEM)
HBM = pl.BlockSpec(memory_space=pltpu.HBM)


def shape(dims, kind):
    return jax.ShapeDtypeStruct(dims, kind)


def kernel(body, name, out, ins, scratch=(), vmem=4, flops=0, nbytes=0, outs=VMEM):
    single = not isinstance(out, list)
    return pl.pallas_call(
        body,
        out_shape=out,
        in_specs=ins,
        out_specs=outs if single else [outs] * len(out),
        scratch_shapes=scratch,
        compiler_params=pltpu.CompilerParams(vmem_limit_bytes=vmem * MIB),
        cost_estimate=pl.CostEstimate(flops=flops, bytes_accessed=nbytes, transcendentals=0),
        name=name,
    )


def per_device(
    residual,
    input_norm_gain,
    adapter_entry_matrix,
    adapter_exit_matrix,
    value_output_gradient,
    position_example_index,
    live_row_length,
    random_sketch_keys,
    reference_gradients,
):
    seq_count, local_len, width = residual.shape
    tokens = seq_count * local_len
    value_width = value_output_gradient.shape[2]
    n_fsdp, n_dp = lax.axis_size("fsdp"), lax.axis_size("dp")
    fsdp, dp = lax.axis_index("fsdp"), lax.axis_index("dp")
    top = n_dp // 2
    fsdp_at = fsdp.reshape(1)
    z_at = (dp // 2 % (top // 2)).reshape(1)
    four_at = (dp // top * 2 + dp % 2).reshape(1)
    swaps = [[(n, n ^ flip) for n in range(n_dp)] for flip in (1, top, top + 1)]
    up, down = (
        [(n, n // top * top + (n + 2 * way) % top) for n in range(n_dp)] for way in (1, -1)
    )
    tie = lax.optimization_barrier

    x = residual.reshape(tokens, width)
    g = value_output_gradient.reshape(tokens, value_width)
    gain = input_norm_gain.reshape(1, width)
    chunk = width // n_fsdp

    refs_up = [lax.ppermute(reference_gradients, "dp", up)]
    refs_down = [lax.ppermute(reference_gradients, "dp", down)]

    weights = kernel(
        prep_kernel,
        "prep",
        shape((n_fsdp, 48, chunk), BF16),
        [SMEM, SMEM, VMEM, VMEM, VMEM],
        vmem=FULL_MIB,
    )(fsdp_at, random_sketch_keys, gain, adapter_entry_matrix, adapter_exit_matrix)
    weights = lax.all_to_all(weights, "fsdp", 0, 0)

    held = [
        pltpu.VMEM((n_fsdp, tokens, chunk), BF16),
        pltpu.VMEM((tokens, value_width), BF16),
    ]
    early = kernel(
        early_kernel,
        "early",
        [
            shape((2, 64, tokens), F32),
            shape((8, tokens), F32),
            shape((tokens, 128), F32),
        ],
        [SMEM] + [HBM] * 3,
        held
        + [
            pltpu.VMEM((1, width), F32),
            pltpu.VMEM((128, width), BF16),
            pltpu.VMEM((tokens, 128), F32),
            pltpu.VMEM((tokens, 128), F32),
            pltpu.SemaphoreType.DMA((2 + n_fsdp,)),
        ],
        vmem=FULL_MIB,
        flops=2 * tokens * width * 256,
        nbytes=12 * MIB,
    )(random_sketch_keys, gain, x, g)
    early, refs_up[0], refs_down[0] = tie((early, refs_up[0], refs_down[0]))
    refs_up.append(lax.ppermute(refs_up[0], "dp", up))
    refs_down.append(lax.ppermute(refs_down[0], "dp", down))

    features = kernel(
        main_kernel,
        "features",
        shape((8, 128, 128), F32),
        [SMEM] * 2 + [HBM] * 7,
        [
            pltpu.VMEM((seq_count, local_len), I32),
            pltpu.VMEM((2, 64, tokens), F32),
            pltpu.VMEM((8, tokens), F32),
            pltpu.VMEM((tokens, 128), F32),
            pltpu.VMEM((n_fsdp, 48, chunk), BF16),
            held[1],
            held[0],
            pltpu.VMEM((8, 128, 128), F32),
            pltpu.VMEM((2, 32, tokens), F32),
            pltpu.VMEM((2, 512, tokens), BF16),
            pltpu.VMEM((2, 512, tokens), BF16),
            pltpu.SemaphoreType.DMA((6 + n_fsdp,)),
            pltpu.SemaphoreType.DMA((1,)),
        ],
        vmem=FULL_MIB,
        flops=2 * tokens * width * 256,
        nbytes=12 * MIB,
        outs=HBM,
    )(fsdp_at, live_row_length, position_example_index, *early, weights, g, x)
    features, refs_up[1], refs_down[1] = tie((features, refs_up[1], refs_down[1]))
    refs_up.append(lax.ppermute(refs_up[1], "dp", up))
    refs_down.append(lax.ppermute(refs_down[1], "dp", down))
    features = lax.all_to_all(features, "fsdp", 0, 0)

    pieces = kernel(
        sum_kernel,
        "sum_features",
        [shape((16, 256), BF16)] * 4,
        [SMEM, VMEM],
        [pltpu.VMEM((4, 16, 256), BF16)],
    )(four_at, features)
    pieces = [pieces[0]] + [
        lax.ppermute(piece, "dp", swap) for piece, swap in zip(pieces[1:], swaps)
    ]
    feats = jnp.concatenate(pieces, axis=0)
    feats, refs_up[2], refs_down[2] = tie((feats, refs_up[2], refs_down[2]))
    refs_up.append(lax.ppermute(refs_up[2], "dp", up))
    feats = jnp.broadcast_to(feats[None], (n_fsdp,) + feats.shape)
    feats = lax.all_to_all(feats, "fsdp", 0, 0)

    refs = [reference_gradients] + refs_up + refs_down[::-1]
    pieces = kernel(
        score_kernel,
        "partial_scores",
        [shape((16, 768), F32)] * 4,
        [SMEM] + [VMEM] * 9,
        vmem=8,
    )(z_at, feats, *refs)
    pieces = [pieces[0]] + [
        lax.ppermute(piece, "dp", swap) for piece, swap in zip(pieces[1:], swaps)
    ]
    return kernel(
        final_kernel,
        "scores",
        shape((16, reference_gradients.shape[0]), F32),
        [VMEM] * 4,
    )(*pieces)


def solution(mesh):
    placed = (
        P("dp", "fsdp", None),
        P(),
        P("fsdp", None),
        P(None, "fsdp"),
        P("dp", "fsdp", None),
        P("dp", "fsdp"),
        P("dp"),
        P(),
        P("fsdp", "dp"),
    )
    return jax.shard_map(
        per_device, mesh=mesh, in_specs=placed, out_specs=P("dp", "fsdp"), check_vma=False
    )
```

time: 101 us -> 78.8 us (0.78)
  blocking collectives: 31.1 us -> 0 us
  starting transfers between devices: 12.3 us -> 37.3 us
  between operations: 13.5 us -> 0.11 us
  local copies, waits for them, and re-layouts: 11.1 us -> 1.61 us
  Pallas kernels: 17.2 us -> 21.4 us
  waiting for transfers between devices: 14.4 us -> 18 us
    all_to_all x2 -> x0, blocking collectives: 31.1 us -> none  [the longest x1 20.3 us: per_device(): weights = lax.all_to_all(weights, 'fsdp', 0, 0)]
    ppermute x0 -> x7, starting transfers between devices: none -> 11.2 us  [the longest x1 4.03 us: per_device(): refs_down = [lax.ppermute(reference_gradients, 'dp', down)]]
    all_to_all x0 -> x2, starting transfers between devices: none -> 11 us  [the longest x1 7.48 us: per_device(): weights = lax.all_to_all(weights, 'fsdp', 0, 0)]
    unnamed x24 -> x4, local copies, waits for them, and re-layouts: 11 us -> 0.89 us
    all_to_all x0 -> x2, waiting for transfers between devices: none -> 7.58 us  [the longest x1 7.58 us: per_device(): feats = lax.all_to_all(feats, 'fsdp', 0, 0)]
    pallas_call x5 -> x6, Pallas kernels: 17.2 us -> 21.4 us  [the longest x1 9.93 us: per_device(): kernel(early_kernel, 'early', [shape((2, 64, tokens), F32), shape((8, tok...]
    all_to_all x1, starting transfers between devices: 3.49 us -> 6.57 us  [per_device(): features = lax.all_to_all(features, 'fsdp', 0, 0)]
    all_to_all x1, waiting for transfers between devices: 8.75 us -> 6.16 us  [per_device(): features = lax.all_to_all(features, 'fsdp', 0, 0)]
  transfers between devices with their start and end apart: 8 -> 16, of which waited for: 5 -> 6; matrix products, arithmetic and copies ran while one was open for 1% -> 1% of each run, Pallas kernels for 15% -> 23%
where the time goes in v2:
time: 78.8 us; the launch traced here: 78.4 us
  starting transfers between devices  37.3 us (47%)
  Pallas kernels  21.4 us (27%)
  waiting for transfers between devices  18 us (23%)
  local copies, waits for them, and re-layouts  1.61 us (2%)
    pallas_call x1, Pallas kernels, per_device(): kernel(early_kernel, 'early', [shape((2, 64, tokens), F32), shape((8, tok...  9.93 us
    ppermute x6, starting transfers between devices, per_device(): lax.ppermute(piece, 'dp', swap)  8.64 us
    pallas_call x1, Pallas kernels, per_device(): kernel(main_kernel, 'features', shape((8, 128, 128), F32), [SMEM] * 2 + [...  7.8 us
    all_to_all x1, waiting for transfers between devices, per_device(): feats = lax.all_to_all(feats, 'fsdp', 0, 0)  7.58 us
    all_to_all x1, starting transfers between devices, per_device(): weights = lax.all_to_all(weights, 'fsdp', 0, 0)  7.48 us
    all_to_all x1, starting transfers between devices, per_device(): features = lax.all_to_all(features, 'fsdp', 0, 0)  6.57 us
    all_to_all x1, waiting for transfers between devices, per_device(): features = lax.all_to_all(features, 'fsdp', 0, 0)  6.16 us
    ppermute x6, waiting for transfers between devices, per_device(): lax.ppermute(piece, 'dp', swap)  4.21 us
  transfers between devices with their start and end apart: 16, of which 6 were waited for; matrix products, arithmetic and copies ran while one was open for 1% of the time, Pallas kernels for 23%

profile of v2, /device:TPU:1, one launch (start us, length us, event | category | flops | bytes accessed | tf_op | source)
XLA Modules:
  0.0 78.4 jit_solution(15898413844491223060)
XLA Ops:
  0.0 2.1 %prep.1 = bf16[8,48,1024]{2,1,0:T(8,128)(2,1)} custom-call(s32[1]{0:T(128)} %bitcast.2.me, s32[2]{0:T(128)} %keys.3, f32[1,8192]{1,0:T(1,128)} %bitcast.10, bf16[1024,128]{1,0:T(8,128)(2,1)} %down.1, bf16[128,128]{1,0:T(8,128)(2,1)} %up.1), custom_call_target="tpu_custom_call" | custom-call | tf_op jit(solution)/shard_map/prep/pallas_call | solution.py:322
  2.1 7.5 %all-to-all-start = ((bf16[8,48,1024]{2,1,0:T(8,128)(2,1)}), bf16[8,48,1024]{2,1,0:T(8,128)(2,1)S(1)}, u32[]{:S(2)}, u32[]{:S(2)}) async-start(bf16[8,48,1024]{2,1,0:T(8,128)(2,1)} %prep.1), calls=%async_computation | async-start | bytes 1572864 | tf_op jit(solution)/shard_map/all_to_all | solution.py:329
  9.6 1.6 %collective-permute-start = (bf16[512,256]{1,0:T(8,128)(2,1)}, bf16[512,256]{1,0:T(8,128)(2,1)S(1)}, u32[]{:S(2)}, u32[]{:S(2)}) collective-permute-start(bf16[512,256]{1,0:T(8,128)(2,1)} %rest_0_.1), channel_id=1, source_target_pairs={{0,2},{1,3},{2,4},{3,5},{4,6},{5,7},{6,8},{7,9},{8,10},{9,11},{10,... | collective-permute-start | bytes 786440 | tf_op jit(solution)/shard_map/ppermute | solution.py:319
  11.2 4.0 %collective-permute-start.1 = (bf16[512,256]{1,0:T(8,128)(2,1)}, bf16[512,256]{1,0:T(8,128)(2,1)S(1)}, u32[]{:S(2)}, u32[]{:S(2)}) collective-permute-start(bf16[512,256]{1,0:T(8,128)(2,1)} %rest_0_.1), channel_id=1, source_target_pairs={{0,14},{1,15},{2,0},{3,1},{4,2},{5,3},{6,4},{7,5},{8,6},{9,7},{10,... | collective-permute-start | bytes 786440 | tf_op jit(solution)/shard_map/ppermute | solution.py:320
  15.2 9.9 %early.1 = (f32[2,64,512]{2,1,0:T(8,128)}, f32[8,512]{1,0:T(8,128)}, f32[512,128]{1,0:T(8,128)}) custom-call(s32[2]{0:T(128)} %keys.3, f32[1,8192]{1,0:T(1,128)} %bitcast.11, bf16[512,8192]{1,0:T(8,128)(2,1)} %bitcast.6, bf16[512,1024]{1,0:T(8,128)(2,1)} %bitcast.8), custom_call_target="tpu_custom_call" | custom-call | flops 2147483648 | bytes 12582912 | tf_op jit(solution)/shard_map/early/pallas_call | solution.py:335
  25.2 0.0 copy-start
  25.2 0.0 collective-permute-done.rest_1_
  25.2 0.0 collective-permute-done.1.rest_7_
  25.2 0.1 collective-permute-start.2
  25.3 2.7 %collective-permute-start.3 = (bf16[512,256]{1,0:T(8,128)(2,1)S(1)}, bf16[512,256]{1,0:T(8,128)(2,1)S(1)}, u32[]{:S(2)}, u32[]{:S(2)}) collective-permute-start(bf16[512,256]{1,0:T(8,128)(2,1)S(1)} %collective-permute-done.1.rest_7_), channel_id=1, source_target_pairs={{0,14},{1,15},{2,0},{3,1},{4,2},{5,3},{6,4},{7,5},{8,6},{9,7},{10,... | collective-permute-start | bytes 786440 | tf_op jit(solution)/shard_map/ppermute | solution.py:358
  28.0 0.0 all-to-all-done.w_in
  28.0 0.0 copy-start.1
  28.0 0.9 %copy-done.1 = bf16[8,48,1024]{2,1,0:T(8,128)(2,1)} copy-done((bf16[8,48,1024]{2,1,0:T(8,128)(2,1)}, bf16[8,48,1024]{2,1,0:T(8,128)(2,1)S(1)}, u32[]{:S(2)}) %copy-start.1) | copy-done | bytes 786456
  28.9 7.8 %features.1 = f32[8,128,128]{2,1,0:T(8,128)} custom-call(s32[1]{0:T(128)} %bitcast.2.me, s32[2]{0:T(128)} %lengths.1, s32[2,256]{1,0:T(2,128)} %index_in.1, f32[2,64,512]{2,1,0:T(8,128)} %get-tuple-element.30.xs_in, f32[8,512]{1,0:T(8,128)} %get-tuple-element.31.r_in, f32[512,128]{1,0:T(8,128)} %get-tuple-element.32.ks_in, bf16[8,48,1024]{2,1,0:T(8,128)(2,1)} %copy-done.1, ...), custom_call_target="tpu_custom_call" | custom-call | flops 2147483648 | bytes 12582912 | tf_op jit(solution)/shard_map/features/pallas_call | solution.py:360
  36.7 0.0 collective-permute-done.2.rest_2_
  36.7 0.0 collective-permute-done.3.rest_6_
  36.7 6.6 %all-to-all-start.1 = ((f32[8,128,128]{2,1,0:T(8,128)}), f32[8,128,128]{2,1,0:T(8,128)S(1)}, u32[]{:S(2)}, u32[]{:S(2)}) async-start(f32[8,128,128]{2,1,0:T(8,128)} %features.1), calls=%async_computation.1 | async-start | bytes 1048576 | tf_op jit(solution)/shard_map/all_to_all | solution.py:388
  43.3 0.0 collective-permute-start.7
  43.3 2.7 %collective-permute-start.8 = (bf16[512,256]{1,0:T(8,128)(2,1)S(1)}, bf16[512,256]{1,0:T(8,128)(2,1)S(1)}, u32[]{:S(2)}, u32[]{:S(2)}) collective-permute-start(bf16[512,256]{1,0:T(8,128)(2,1)S(1)} %collective-permute-done.3.rest_6_), channel_id=1, source_target_pairs={{0,14},{1,15},{2,0},{3,1},{4,2},{5,3},{6,4},{7,5},{8,6},{9,7},{10,... | collective-permute-start | bytes 786440 | tf_op jit(solution)/shard_map/ppermute | solution.py:387
  45.9 6.2 %all-to-all-done.1.parts = f32[8,128,128]{2,1,0:T(8,128)S(1)} async-done(((f32[8,128,128]{2,1,0:T(8,128)}), f32[8,128,128]{2,1,0:T(8,128)S(1)}, u32[]{:S(2)}, u32[]{:S(2)}) %all-to-all-start.1) | async-done | bytes 524320 | tf_op jit(solution)/shard_map/all_to_all | solution.py:388
  52.1 0.1 sum_features.1
  52.2 3.6 %collective-permute-start.6 = (bf16[16,256]{1,0:T(8,128)(2,1)S(1)}, bf16[16,256]{1,0:T(8,128)(2,1)S(1)}, u32[]{:S(2)}, u32[]{:S(2)}) collective-permute-start(bf16[16,256]{1,0:T(8,128)(2,1)S(1)} %get-tuple-element.39), channel_id=1, source_target_pairs={{0,17},{1,16},{2,19},{3,18},{4,21},{5,20},{6,23},{7,22},{8,25},{9,... | collective-permute-start | bytes 24584 | tf_op jit(solution)/shard_map/ppermute | solution.py:398
  55.8 1.1 %collective-permute-start.5 = (bf16[16,256]{1,0:T(8,128)(2,1)S(1)}, bf16[16,256]{1,0:T(8,128)(2,1)S(1)}, u32[]{:S(2)}, u32[]{:S(2)}) collective-permute-start(bf16[16,256]{1,0:T(8,128)(2,1)S(1)} %get-tuple-element.38), channel_id=1, source_target_pairs={{0,16},{1,17},{2,18},{3,19},{4,20},{5,21},{6,22},{7,23},{8,24},{9,... | collective-permute-start | bytes 24584 | tf_op jit(solution)/shard_map/ppermute | solution.py:398
  56.9 0.0 collective-permute-start.4
  56.9 0.2 collective-permute-done.6
  57.1 1.2 %collective-permute-done.5 = bf16[16,256]{1,0:T(8,128)(2,1)S(1)} collective-permute-done((bf16[16,256]{1,0:T(8,128)(2,1)S(1)}, bf16[16,256]{1,0:T(8,128)(2,1)S(1)}, u32[]{:S(2)}, u32[]{:S(2)}) %collective-permute-start.5) | collective-permute-done | bytes 8224 | tf_op jit(solution)/shard_map/ppermute | solution.py:398
  58.3 0.0 collective-permute-done.4
  58.3 0.0 collective-permute-done.7.rest_3_
  58.3 0.0 collective-permute-done.8.rest_5_
  58.3 0.1 collective-permute-start.9
  58.4 0.7 broadcast_in_dim.2
  59.1 3.5 %all-to-all-start.2 = ((bf16[8,64,256]{2,1,0:T(8,128)(2,1)}), bf16[8,64,256]{2,1,0:T(8,128)(2,1)S(1)}, u32[]{:S(2)}, u32[]{:S(2)}) async-start(bf16[8,64,256]{2,1,0:T(8,128)(2,1)} %broadcast_in_dim.2), calls=%async_computation.2 | async-start | bytes 524288 | tf_op jit(solution)/shard_map/all_to_all | solution.py:404
  62.6 7.6 %all-to-all-done.2.feats = bf16[8,64,256]{2,1,0:T(8,128)(2,1)S(1)} async-done(((bf16[8,64,256]{2,1,0:T(8,128)(2,1)}), bf16[8,64,256]{2,1,0:T(8,128)(2,1)S(1)}, u32[]{:S(2)}, u32[]{:S(2)}) %all-to-all-start.2) | async-done | bytes 262176 | tf_op jit(solution)/shard_map/all_to_all | solution.py:404
  70.2 0.0 collective-permute-done.9.rest_4_
  70.2 0.0 copy-done
  70.2 0.8 %partial_scores.1 = (f32[16,768]{1,0:T(8,128)S(1)}, f32[16,768]{1,0:T(8,128)S(1)}, f32[16,768]{1,0:T(8,128)S(1)}, f32[16,768]{1,0:T(8,128)S(1)}) custom-call(s32[1]{0:T(128)} %bitcast.at, bf16[8,64,256]{2,1,0:T(8,128)(2,1)S(1)} %all-to-all-done.2.feats, bf16[512,256]{1,0:T(8,128)(2,1)S(1)} %copy-done, bf16[512,256]{1,0:T(8,128)(2,1)S(1)} %collective-permute-done.rest_1_, ...), custom_call_target="tpu_custom_call" | custom-call | tf_op jit(solution)/shard_map/partial_scores/pallas_call | solution.py:407
  71.0 2.2 %collective-permute-start.10 = (f32[16,768]{1,0:T(8,128)S(1)}, f32[16,768]{1,0:T(8,128)S(1)}, u32[]{:S(2)}, u32[]{:S(2)}) collective-permute-start(f32[16,768]{1,0:T(8,128)S(1)} %get-tuple-element.46), channel_id=1, source_target_pairs={{0,1},{1,0},{2,3},{3,2},{4,5},{5,4},{6,7},{7,6},{8,9},{9,8},{10,11... | collective-permute-start | bytes 147464 | tf_op jit(solution)/shard_map/ppermute | solution.py:415
  73.2 0.8 %collective-permute-start.11 = (f32[16,768]{1,0:T(8,128)S(1)}, f32[16,768]{1,0:T(8,128)S(1)}, u32[]{:S(2)}, u32[]{:S(2)}) collective-permute-start(f32[16,768]{1,0:T(8,128)S(1)} %get-tuple-element.47), channel_id=1, source_target_pairs={{0,16},{1,17},{2,18},{3,19},{4,20},{5,21},{6,22},{7,23},{8,24},{9,... | collective-permute-start | bytes 147464 | tf_op jit(solution)/shard_map/ppermute | solution.py:415
  74.0 0.9 %collective-permute-start.12 = (f32[16,768]{1,0:T(8,128)S(1)}, f32[16,768]{1,0:T(8,128)S(1)}, u32[]{:S(2)}, u32[]{:S(2)}) collective-permute-start(f32[16,768]{1,0:T(8,128)S(1)} %get-tuple-element.48), channel_id=1, source_target_pairs={{0,17},{1,16},{2,19},{3,18},{4,21},{5,20},{6,23},{7,22},{8,25},{9,... | collective-permute-start | bytes 147464 | tf_op jit(solution)/shard_map/ppermute | solution.py:415
  74.9 0.0 collective-permute-done.10.one
  75.0 1.2 %collective-permute-done.11.two = f32[16,768]{1,0:T(8,128)S(1)} collective-permute-done((f32[16,768]{1,0:T(8,128)S(1)}, f32[16,768]{1,0:T(8,128)S(1)}, u32[]{:S(2)}, u32[]{:S(2)}) %collective-permute-start.11) | collective-permute-done | bytes 49184 | tf_op jit(solution)/shard_map/ppermute | solution.py:415
  76.2 1.6 %collective-permute-done.12.three = f32[16,768]{1,0:T(8,128)S(1)} collective-permute-done((f32[16,768]{1,0:T(8,128)S(1)}, f32[16,768]{1,0:T(8,128)S(1)}, u32[]{:S(2)}, u32[]{:S(2)}) %collective-permute-start.12) | collective-permute-done | bytes 49184 | tf_op jit(solution)/shard_map/ppermute | solution.py:415
  77.8 0.6 scores.1
  (1 shorter events, 0.0 us)
Async XLA Ops:
  2.1 25.9 %all-to-all-start = ((bf16[8,48,1024]{2,1,0:T(8,128)(2,1)}), bf16[8,48,1024]{2,1,0:T(8,128)(2,1)S(1)}, u32[]{:S(2)}, u32[]{:S(2)}) async-start(bf16[8,48,1024]{2,1,0:T(8,128)(2,1)} %prep.1), calls=%async_computation | async-start | bytes 1572864 | tf_op jit(solution)/shard_map/all_to_all | solution.py:329
  9.6 15.6 %collective-permute-start = (bf16[512,256]{1,0:T(8,128)(2,1)}, bf16[512,256]{1,0:T(8,128)(2,1)S(1)}, u32[]{:S(2)}, u32[]{:S(2)}) collective-permute-start(bf16[512,256]{1,0:T(8,128)(2,1)} %rest_0_.1), channel_id=1, source_target_pairs={{0,2},{1,3},{2,4},{3,5},{4,6},{5,7},{6,8},{7,9},{8,10},{9,11},{10,... | collective-permute-start | bytes 786440 | tf_op jit(solution)/shard_map/ppermute | solution.py:319
  11.2 14.0 %collective-permute-start.1 = (bf16[512,256]{1,0:T(8,128)(2,1)}, bf16[512,256]{1,0:T(8,128)(2,1)S(1)}, u32[]{:S(2)}, u32[]{:S(2)}) collective-permute-start(bf16[512,256]{1,0:T(8,128)(2,1)} %rest_0_.1), channel_id=1, source_target_pairs={{0,14},{1,15},{2,0},{3,1},{4,2},{5,3},{6,4},{7,5},{8,6},{9,7},{10,... | collective-permute-start | bytes 786440 | tf_op jit(solution)/shard_map/ppermute | solution.py:320
  25.2 45.0 %copy-start = (bf16[512,256]{1,0:T(8,128)(2,1)S(1)}, bf16[512,256]{1,0:T(8,128)(2,1)}, u32[]{:S(2)}) copy-start(bf16[512,256]{1,0:T(8,128)(2,1)} %rest_0_.1) | copy-start | bytes 786436
  25.2 11.5 %collective-permute-start.2 = (bf16[512,256]{1,0:T(8,128)(2,1)S(1)}, bf16[512,256]{1,0:T(8,128)(2,1)S(1)}, u32[]{:S(2)}, u32[]{:S(2)}) collective-permute-start(bf16[512,256]{1,0:T(8,128)(2,1)S(1)} %collective-permute-done.rest_1_), channel_id=1, source_target_pairs={{0,2},{1,3},{2,4},{3,5},{4,6},{5,7},{6,8},{7,9},{8,10},{9,11},{10,... | collective-permute-start | bytes 786440 | tf_op jit(solution)/shard_map/ppermute | solution.py:357
  25.3 11.4 %collective-permute-start.3 = (bf16[512,256]{1,0:T(8,128)(2,1)S(1)}, bf16[512,256]{1,0:T(8,128)(2,1)S(1)}, u32[]{:S(2)}, u32[]{:S(2)}) collective-permute-start(bf16[512,256]{1,0:T(8,128)(2,1)S(1)} %collective-permute-done.1.rest_7_), channel_id=1, source_target_pairs={{0,14},{1,15},{2,0},{3,1},{4,2},{5,3},{6,4},{7,5},{8,6},{9,7},{10,... | collective-permute-start | bytes 786440 | tf_op jit(solution)/shard_map/ppermute | solution.py:358
  28.0 0.9 %copy-start.1 = (bf16[8,48,1024]{2,1,0:T(8,128)(2,1)}, bf16[8,48,1024]{2,1,0:T(8,128)(2,1)S(1)}, u32[]{:S(2)}) copy-start(bf16[8,48,1024]{2,1,0:T(8,128)(2,1)S(1)} %all-to-all-done.w_in) | copy-start | bytes 2359300
  36.7 15.4 %all-to-all-start.1 = ((f32[8,128,128]{2,1,0:T(8,128)}), f32[8,128,128]{2,1,0:T(8,128)S(1)}, u32[]{:S(2)}, u32[]{:S(2)}) async-start(f32[8,128,128]{2,1,0:T(8,128)} %features.1), calls=%async_computation.1 | async-start | bytes 1048576 | tf_op jit(solution)/shard_map/all_to_all | solution.py:388
  43.3 15.1 %collective-permute-start.7 = (bf16[512,256]{1,0:T(8,128)(2,1)S(1)}, bf16[512,256]{1,0:T(8,128)(2,1)S(1)}, u32[]{:S(2)}, u32[]{:S(2)}) collective-permute-start(bf16[512,256]{1,0:T(8,128)(2,1)S(1)} %collective-permute-done.2.rest_2_), channel_id=1, source_target_pairs={{0,2},{1,3},{2,4},{3,5},{4,6},{5,7},{6,8},{7,9},{8,10},{9,11},{10,... | collective-permute-start | bytes 786440 | tf_op jit(solution)/shard_map/ppermute | solution.py:386
  43.3 15.1 %collective-permute-start.8 = (bf16[512,256]{1,0:T(8,128)(2,1)S(1)}, bf16[512,256]{1,0:T(8,128)(2,1)S(1)}, u32[]{:S(2)}, u32[]{:S(2)}) collective-permute-start(bf16[512,256]{1,0:T(8,128)(2,1)S(1)} %collective-permute-done.3.rest_6_), channel_id=1, source_target_pairs={{0,14},{1,15},{2,0},{3,1},{4,2},{5,3},{6,4},{7,5},{8,6},{9,7},{10,... | collective-permute-start | bytes 786440 | tf_op jit(solution)/shard_map/ppermute | solution.py:387
  52.2 5.0 %collective-permute-start.6 = (bf16[16,256]{1,0:T(8,128)(2,1)S(1)}, bf16[16,256]{1,0:T(8,128)(2,1)S(1)}, u32[]{:S(2)}, u32[]{:S(2)}) collective-permute-start(bf16[16,256]{1,0:T(8,128)(2,1)S(1)} %get-tuple-element.39), channel_id=1, source_target_pairs={{0,17},{1,16},{2,19},{3,18},{4,21},{5,20},{6,23},{7,22},{8,25},{9,... | collective-permute-start | bytes 24584 | tf_op jit(solution)/shard_map/ppermute | solution.py:398
  55.8 2.5 %collective-permute-start.5 = (bf16[16,256]{1,0:T(8,128)(2,1)S(1)}, bf16[16,256]{1,0:T(8,128)(2,1)S(1)}, u32[]{:S(2)}, u32[]{:S(2)}) collective-permute-start(bf16[16,256]{1,0:T(8,128)(2,1)S(1)} %get-tuple-element.38), channel_id=1, source_target_pairs={{0,16},{1,17},{2,18},{3,19},{4,20},{5,21},{6,22},{7,23},{8,24},{9,... | collective-permute-start | bytes 24584 | tf_op jit(solution)/shard_map/ppermute | solution.py:398
  56.9 1.4 %collective-permute-start.4 = (bf16[16,256]{1,0:T(8,128)(2,1)S(1)}, bf16[16,256]{1,0:T(8,128)(2,1)S(1)}, u32[]{:S(2)}, u32[]{:S(2)}) collective-permute-start(bf16[16,256]{1,0:T(8,128)(2,1)S(1)} %get-tuple-element.37), channel_id=1, source_target_pairs={{0,1},{1,0},{2,3},{3,2},{4,5},{5,4},{6,7},{7,6},{8,9},{9,8},{10,11... | collective-permute-start | bytes 24584 | tf_op jit(solution)/shard_map/ppermute | solution.py:398
  58.3 11.9 %collective-permute-start.9 = (bf16[512,256]{1,0:T(8,128)(2,1)S(1)}, bf16[512,256]{1,0:T(8,128)(2,1)S(1)}, u32[]{:S(2)}, u32[]{:S(2)}) collective-permute-start(bf16[512,256]{1,0:T(8,128)(2,1)S(1)} %collective-permute-done.7.rest_3_), channel_id=1, source_target_pairs={{0,2},{1,3},{2,4},{3,5},{4,6},{5,7},{6,8},{7,9},{8,10},{9,11},{10,... | collective-permute-start | bytes 786440 | tf_op jit(solution)/shard_map/ppermute | solution.py:402
  59.1 11.1 %all-to-all-start.2 = ((bf16[8,64,256]{2,1,0:T(8,128)(2,1)}), bf16[8,64,256]{2,1,0:T(8,128)(2,1)S(1)}, u32[]{:S(2)}, u32[]{:S(2)}) async-start(bf16[8,64,256]{2,1,0:T(8,128)(2,1)} %broadcast_in_dim.2), calls=%async_computation.2 | async-start | bytes 524288 | tf_op jit(solution)/shard_map/all_to_all | solution.py:404
  71.0 3.9 %collective-permute-start.10 = (f32[16,768]{1,0:T(8,128)S(1)}, f32[16,768]{1,0:T(8,128)S(1)}, u32[]{:S(2)}, u32[]{:S(2)}) collective-permute-start(f32[16,768]{1,0:T(8,128)S(1)} %get-tuple-element.46), channel_id=1, source_target_pairs={{0,1},{1,0},{2,3},{3,2},{4,5},{5,4},{6,7},{7,6},{8,9},{9,8},{10,11... | collective-permute-start | bytes 147464 | tf_op jit(solution)/shard_map/ppermute | solution.py:415
  73.2 3.0 %collective-permute-start.11 = (f32[16,768]{1,0:T(8,128)S(1)}, f32[16,768]{1,0:T(8,128)S(1)}, u32[]{:S(2)}, u32[]{:S(2)}) collective-permute-start(f32[16,768]{1,0:T(8,128)S(1)} %get-tuple-element.47), channel_id=1, source_target_pairs={{0,16},{1,17},{2,18},{3,19},{4,20},{5,21},{6,22},{7,23},{8,24},{9,... | collective-permute-start | bytes 147464 | tf_op jit(solution)/shard_map/ppermute | solution.py:415
  74.0 3.7 %collective-permute-start.12 = (f32[16,768]{1,0:T(8,128)S(1)}, f32[16,768]{1,0:T(8,128)S(1)}, u32[]{:S(2)}, u32[]{:S(2)}) collective-permute-start(f32[16,768]{1,0:T(8,128)S(1)} %get-tuple-element.48), channel_id=1, source_target_pairs={{0,17},{1,16},{2,19},{3,18},{4,21},{5,20},{6,23},{7,22},{8,25},{9,... | collective-permute-start | bytes 147464 | tf_op jit(solution)/shard_map/ppermute | solution.py:415

commit v3 on v2

--- a/solution.py
+++ b/solution.py
@@ -13,7 +13,6 @@
 NN = (((1,), (0,)), ((), ()))
 MIB = 1024 * 1024
 FULL_MIB = 58
-AHEAD = 4
 
 
 def dot(a, b, dims=NN):
@@ -41,9 +40,14 @@
 
 def prep_kernel(me, keys, gain, down, up, out):
     shard = down.shape[0]
-    start = pl.multiple_of(me[0] * shard, shard)
+    rows = shard // 128
+    own_gain = gain[pl.ds(pl.multiple_of(me[0] * rows, rows), rows), :]
     s3 = signs(keys[1], 3, 0, down.shape[1], 32).astype(BF16)
-    wb = dot(s3, down[...], NT) * gain[:, pl.ds(start, shard)]
+    wb = dot(s3, down[...], NT)
+    wb = jnp.concatenate(
+        [wb[:, 128 * q : 128 * q + 128] * own_gain[q : q + 1, :] for q in range(rows)],
+        axis=1,
+    )
     s2 = signs(keys[0], 2, 0, up.shape[0], 64).astype(BF16)
     hi, lo = split(dot(s2, up[...]))
     wg = jnp.concatenate(
@@ -74,35 +78,36 @@
     width, gwidth = steps * chunk, g.shape[1]
     copies = copies_of(x_pieces(x_in, x) + [(g_in, g), (gain_in, gain)], sems)
     copies[-1].start()
-    for copy in copies[:AHEAD]:
+    for copy in copies[:-1]:
         copy.start()
     s4 = signs(keys[1], 4, 0, gwidth, 128).astype(BF16)
     copies[-1].wait()
-    for n in range(steps):
-        columns = slice(chunk * n, chunk * n + chunk)
-        gain_row = gain[:, columns]
+    for n in range(0, width, 128):
+        gain_row = gain[n // 128 : n // 128 + 1, :]
         gain_hi = gain_row.astype(BF16).astype(F32)
         gain_lo = gain_row - gain_hi
-        plus = sign_bits(keys[0], 1, n * chunk, chunk, 64)
-        table[0:64, columns] = jnp.where(plus, gain_hi, -gain_hi).astype(BF16)
-        table[64:128, columns] = jnp.where(plus, gain_lo, -gain_lo).astype(BF16)
-    for n in range(0, steps, 2):
-        for m in (n, n + 1):
-            copies[m].wait()
-            if m + AHEAD <= steps:
-                copies[m + AHEAD].start()
-        px = None
-        for m in (n, n + 1):
-            p = dot(x[m], table[:, chunk * m : chunk * m + chunk], NT)
-            px = p if px is None else px + p
-        acc[...] = px if n == 0 else acc[...] + px
+        plus = sign_bits(keys[0], 1, n, 128, 64)
+        table[0:64, n : n + 128] = jnp.where(plus, gain_hi, -gain_hi).astype(BF16)
+        table[64:128, n : n + 128] = jnp.where(plus, gain_lo, -gain_lo).astype(BF16)
+    acc[...] = jnp.zeros_like(acc)
+    sq[...] = jnp.zeros_like(sq)
+    @pl.loop(0, steps // 2)
+    def _(pair):
+        both = [2 * pair, 2 * pair + 1]
+        columns = [pl.ds(pl.multiple_of(n * chunk, chunk), chunk) for n in both]
+        for n, c in zip(both, columns):
+            pltpu.make_async_copy(x_in.at[:, c], x.at[n], sems.at[n]).wait()
+        acc[...] += dot(x[both[0]], table[:, columns[0]], NT) + dot(
+            x[both[1]], table[:, columns[1]], NT
+        )
         for t in range(0, tokens, 64):
-            total = sq[t : t + 64, :] if n else jnp.zeros((64, 128), F32)
-            for m in (n, n + 1):
+            total = sq[t : t + 64, :]
+            for n in both:
                 for c in range(0, chunk, 128):
-                    piece = x[m, t : t + 64, c : c + 128].astype(F32)
+                    piece = x[n, t : t + 64, c : c + 128].astype(F32)
                     total = total + piece * piece
             sq[t : t + 64, :] = total
+
     copies[steps].wait()
     ks_out[...] = dot(g[...], s4, NT) * (1.0 / math.sqrt(gwidth))
     mean_sq = jnp.sum(sq[...].T, axis=0, keepdims=True) * (1.0 / width)
@@ -126,7 +131,7 @@
         + x_pieces(x_in, x),
         sems,
     )
-    for copy in copies[: 6 + AHEAD]:
+    for copy in copies:
         copy.start()
 
     position = me[0] * half + lax.broadcasted_iota(I32, (8, half), 1)
@@ -175,6 +180,13 @@
     fa = fa[:, 0:128] + fa[:, 128:256] + dot(ua[1], va[:, 0:128])
     for n in range(8):
         out[n, 0:64, :] = fa[64 * n : 64 * n + 64]
+    done = [
+        pltpu.make_async_copy(
+            out.at[:, 64 * n : 64 * n + 64], out_hbm.at[:, 64 * n : 64 * n + 64], out_sems.at[n]
+        )
+        for n in range(2)
+    ]
+    done[0].start()
     copies[4].wait()
     copies[5].wait()
     vb = jnp.concatenate(split(ks[...]), axis=1)
@@ -182,8 +194,6 @@
     acc = None
     for n in range(steps):
         copies[6 + n].wait()
-        if n + AHEAD < steps:
-            copies[6 + n + AHEAD].start()
         p = dot(w[n, 0:32, :], x[n], NT)
         acc = p if acc is None else acc + p
     hs = acc * (r[0:1, :] * (1.0 / math.sqrt(128)))
@@ -197,9 +207,9 @@
     fb = fb[:, 0:128] + fb[:, 128:256] + dot(ub[1], vb[:, 0:128])
     for n in range(8):
         out[n, 64:128, :] = fb[64 * n : 64 * n + 64]
-    done = pltpu.make_async_copy(out, out_hbm, out_sems.at[0])
-    done.start()
-    done.wait()
+    done[1].start()
+    for copy in done:
+        copy.wait()
 
 
 def sum_kernel(me, parts, own, one, two, three, held):
@@ -313,7 +323,7 @@
 
     x = residual.reshape(tokens, width)
     g = value_output_gradient.reshape(tokens, value_width)
-    gain = input_norm_gain.reshape(1, width)
+    gain = input_norm_gain.reshape(width // 128, 128)
     chunk = width // n_fsdp
 
     refs_up = [lax.ppermute(reference_gradients, "dp", up)]
@@ -343,7 +353,7 @@
         [SMEM] + [HBM] * 3,
         held
         + [
-            pltpu.VMEM((1, width), F32),
+            pltpu.VMEM((width // 128, 128), F32),
             pltpu.VMEM((128, width), BF16),
             pltpu.VMEM((tokens, 128), F32),
             pltpu.VMEM((tokens, 128), F32),
@@ -375,7 +385,7 @@
             pltpu.VMEM((2, 512, tokens), BF16),
             pltpu.VMEM((2, 512, tokens), BF16),
             pltpu.SemaphoreType.DMA((6 + n_fsdp,)),
-            pltpu.SemaphoreType.DMA((1,)),
+            pltpu.SemaphoreType.DMA((2,)),
         ],
         vmem=FULL_MIB,
         flops=2 * tokens * width * 256,

time: 78.8 us -> 76.9 us (0.976)
  Pallas kernels: 21.4 us -> 19.5 us
    pallas_call x1, Pallas kernels: 9.93 us -> 8.22 us  [per_device(): kernel(early_kernel, 'early', [shape((2, 64, tokens), F32), shape((8, tok...]
  transfers between devices with their start and end apart: 16 -> 16, of which waited for: 6 -> 6; matrix products, arithmetic and copies ran while one was open for 1% -> 1% of each run, Pallas kernels for 23% -> 21%
where the time goes in v3:
time: 76.9 us; the launch traced here: 76.5 us
  starting transfers between devices  37.3 us (49%)
  Pallas kernels  19.5 us (25%)
  waiting for transfers between devices  18 us (23%)
  local copies, waits for them, and re-layouts  1.61 us (2%)
    ppermute x6, starting transfers between devices, per_device(): lax.ppermute(piece, 'dp', swap)  8.64 us
    pallas_call x1, Pallas kernels, per_device(): kernel(early_kernel, 'early', [shape((2, 64, tokens), F32), shape((8, tok...  8.22 us
    pallas_call x1, Pallas kernels, per_device(): kernel(main_kernel, 'features', shape((8, 128, 128), F32), [SMEM] * 2 + [...  7.59 us
    all_to_all x1, waiting for transfers between devices, per_device(): feats = lax.all_to_all(feats, 'fsdp', 0, 0)  7.58 us
    all_to_all x1, starting transfers between devices, per_device(): weights = lax.all_to_all(weights, 'fsdp', 0, 0)  7.48 us
    all_to_all x1, starting transfers between devices, per_device(): features = lax.all_to_all(features, 'fsdp', 0, 0)  6.58 us
    all_to_all x1, waiting for transfers between devices, per_device(): features = lax.all_to_all(features, 'fsdp', 0, 0)  6.16 us
    ppermute x6, waiting for transfers between devices, per_device(): lax.ppermute(piece, 'dp', swap)  4.23 us
  transfers between devices with their start and end apart: 16, of which 6 were waited for; matrix products, arithmetic and copies ran while one was open for 1% of the time, Pallas kernels for 21%

profile of v3, /device:TPU:1, one launch (start us, length us, event | category | flops | bytes accessed | tf_op | source)
XLA Modules:
  0.0 76.5 jit_solution(9107313787741734499)
XLA Ops:
  0.0 2.1 %prep.1 = bf16[8,48,1024]{2,1,0:T(8,128)(2,1)} custom-call(s32[1]{0:T(128)} %bitcast.2.me, s32[2]{0:T(128)} %keys.3, f32[64,128]{1,0:T(8,128)} %bitcast.10, bf16[1024,128]{1,0:T(8,128)(2,1)} %down.1, bf16[128,128]{1,0:T(8,128)(2,1)} %up.1), custom_call_target="tpu_custom_call" | custom-call | tf_op jit(solution)/shard_map/prep/pallas_call | solution.py:332
  2.1 7.5 %all-to-all-start = ((bf16[8,48,1024]{2,1,0:T(8,128)(2,1)}), bf16[8,48,1024]{2,1,0:T(8,128)(2,1)S(1)}, u32[]{:S(2)}, u32[]{:S(2)}) async-start(bf16[8,48,1024]{2,1,0:T(8,128)(2,1)} %prep.1), calls=%async_computation | async-start | bytes 1572864 | tf_op jit(solution)/shard_map/all_to_all | solution.py:339
  9.6 1.6 %collective-permute-start = (bf16[512,256]{1,0:T(8,128)(2,1)}, bf16[512,256]{1,0:T(8,128)(2,1)S(1)}, u32[]{:S(2)}, u32[]{:S(2)}) collective-permute-start(bf16[512,256]{1,0:T(8,128)(2,1)} %rest_0_.1), channel_id=1, source_target_pairs={{0,2},{1,3},{2,4},{3,5},{4,6},{5,7},{6,8},{7,9},{8,10},{9,11},{10,... | collective-permute-start | bytes 786440 | tf_op jit(solution)/shard_map/ppermute | solution.py:329
  11.2 4.0 %collective-permute-start.1 = (bf16[512,256]{1,0:T(8,128)(2,1)}, bf16[512,256]{1,0:T(8,128)(2,1)S(1)}, u32[]{:S(2)}, u32[]{:S(2)}) collective-permute-start(bf16[512,256]{1,0:T(8,128)(2,1)} %rest_0_.1), channel_id=1, source_target_pairs={{0,14},{1,15},{2,0},{3,1},{4,2},{5,3},{6,4},{7,5},{8,6},{9,7},{10,... | collective-permute-start | bytes 786440 | tf_op jit(solution)/shard_map/ppermute | solution.py:330
  15.2 8.2 %early.1 = (f32[2,64,512]{2,1,0:T(8,128)}, f32[8,512]{1,0:T(8,128)}, f32[512,128]{1,0:T(8,128)}) custom-call(s32[2]{0:T(128)} %keys.3, f32[64,128]{1,0:T(8,128)} %bitcast.11, bf16[512,8192]{1,0:T(8,128)(2,1)} %bitcast.6, bf16[512,1024]{1,0:T(8,128)(2,1)} %bitcast.8), custom_call_target="tpu_custom_call" | custom-call | flops 2147483648 | bytes 12582912 | tf_op jit(solution)/shard_map/early/pallas_call | solution.py:345
  23.5 0.0 copy-start
  23.5 0.0 collective-permute-done.rest_1_
  23.5 0.0 collective-permute-done.1.rest_7_
  23.5 0.1 collective-permute-start.2
  23.6 2.7 %collective-permute-start.3 = (bf16[512,256]{1,0:T(8,128)(2,1)S(1)}, bf16[512,256]{1,0:T(8,128)(2,1)S(1)}, u32[]{:S(2)}, u32[]{:S(2)}) collective-permute-start(bf16[512,256]{1,0:T(8,128)(2,1)S(1)} %collective-permute-done.1.rest_7_), channel_id=1, source_target_pairs={{0,14},{1,15},{2,0},{3,1},{4,2},{5,3},{6,4},{7,5},{8,6},{9,7},{10,... | collective-permute-start | bytes 786440 | tf_op jit(solution)/shard_map/ppermute | solution.py:368
  26.3 0.0 all-to-all-done.w_in
  26.3 0.0 copy-start.1
  26.3 0.9 %copy-done.1 = bf16[8,48,1024]{2,1,0:T(8,128)(2,1)} copy-done((bf16[8,48,1024]{2,1,0:T(8,128)(2,1)}, bf16[8,48,1024]{2,1,0:T(8,128)(2,1)S(1)}, u32[]{:S(2)}) %copy-start.1) | copy-done | bytes 786456
  27.1 7.6 %features.1 = f32[8,128,128]{2,1,0:T(8,128)} custom-call(s32[1]{0:T(128)} %bitcast.2.me, s32[2]{0:T(128)} %lengths.1, s32[2,256]{1,0:T(2,128)} %index_in.1, f32[2,64,512]{2,1,0:T(8,128)} %get-tuple-element.30.xs_in, f32[8,512]{1,0:T(8,128)} %get-tuple-element.31.r_in, f32[512,128]{1,0:T(8,128)} %get-tuple-element.32.ks_in, bf16[8,48,1024]{2,1,0:T(8,128)(2,1)} %copy-done.1, ...), custom_call_target="tpu_custom_call" | custom-call | flops 2147483648 | bytes 12582912 | tf_op jit(solution)/shard_map/features/pallas_call | solution.py:370
  34.7 0.0 collective-permute-done.2.rest_2_
  34.8 0.0 collective-permute-done.3.rest_6_
  34.8 6.6 %all-to-all-start.1 = ((f32[8,128,128]{2,1,0:T(8,128)}), f32[8,128,128]{2,1,0:T(8,128)S(1)}, u32[]{:S(2)}, u32[]{:S(2)}) async-start(f32[8,128,128]{2,1,0:T(8,128)} %features.1), calls=%async_computation.1 | async-start | bytes 1048576 | tf_op jit(solution)/shard_map/all_to_all | solution.py:398
  41.3 0.0 collective-permute-start.7
  41.4 2.7 %collective-permute-start.8 = (bf16[512,256]{1,0:T(8,128)(2,1)S(1)}, bf16[512,256]{1,0:T(8,128)(2,1)S(1)}, u32[]{:S(2)}, u32[]{:S(2)}) collective-permute-start(bf16[512,256]{1,0:T(8,128)(2,1)S(1)} %collective-permute-done.3.rest_6_), channel_id=1, source_target_pairs={{0,14},{1,15},{2,0},{3,1},{4,2},{5,3},{6,4},{7,5},{8,6},{9,7},{10,... | collective-permute-start | bytes 786440 | tf_op jit(solution)/shard_map/ppermute | solution.py:397
  44.0 6.2 %all-to-all-done.1.parts = f32[8,128,128]{2,1,0:T(8,128)S(1)} async-done(((f32[8,128,128]{2,1,0:T(8,128)}), f32[8,128,128]{2,1,0:T(8,128)S(1)}, u32[]{:S(2)}, u32[]{:S(2)}) %all-to-all-start.1) | async-done | bytes 524320 | tf_op jit(solution)/shard_map/all_to_all | solution.py:398
  50.2 0.1 sum_features.1
  50.3 3.6 %collective-permute-start.6 = (bf16[16,256]{1,0:T(8,128)(2,1)S(1)}, bf16[16,256]{1,0:T(8,128)(2,1)S(1)}, u32[]{:S(2)}, u32[]{:S(2)}) collective-permute-start(bf16[16,256]{1,0:T(8,128)(2,1)S(1)} %get-tuple-element.39), channel_id=1, source_target_pairs={{0,17},{1,16},{2,19},{3,18},{4,21},{5,20},{6,23},{7,22},{8,25},{9,... | collective-permute-start | bytes 24584 | tf_op jit(solution)/shard_map/ppermute | solution.py:408
  53.9 1.1 %collective-permute-start.5 = (bf16[16,256]{1,0:T(8,128)(2,1)S(1)}, bf16[16,256]{1,0:T(8,128)(2,1)S(1)}, u32[]{:S(2)}, u32[]{:S(2)}) collective-permute-start(bf16[16,256]{1,0:T(8,128)(2,1)S(1)} %get-tuple-element.38), channel_id=1, source_target_pairs={{0,16},{1,17},{2,18},{3,19},{4,20},{5,21},{6,22},{7,23},{8,24},{9,... | collective-permute-start | bytes 24584 | tf_op jit(solution)/shard_map/ppermute | solution.py:408
  55.0 0.0 collective-permute-start.4
  55.0 0.2 collective-permute-done.6
  55.2 1.2 %collective-permute-done.5 = bf16[16,256]{1,0:T(8,128)(2,1)S(1)} collective-permute-done((bf16[16,256]{1,0:T(8,128)(2,1)S(1)}, bf16[16,256]{1,0:T(8,128)(2,1)S(1)}, u32[]{:S(2)}, u32[]{:S(2)}) %collective-permute-start.5) | collective-permute-done | bytes 8224 | tf_op jit(solution)/shard_map/ppermute | solution.py:408
  56.4 0.0 collective-permute-done.4
  56.4 0.0 collective-permute-done.7.rest_3_
  56.4 0.0 collective-permute-done.8.rest_5_
  56.4 0.1 collective-permute-start.9
  56.5 0.7 broadcast_in_dim.2
  57.2 3.5 %all-to-all-start.2 = ((bf16[8,64,256]{2,1,0:T(8,128)(2,1)}), bf16[8,64,256]{2,1,0:T(8,128)(2,1)S(1)}, u32[]{:S(2)}, u32[]{:S(2)}) async-start(bf16[8,64,256]{2,1,0:T(8,128)(2,1)} %broadcast_in_dim.2), calls=%async_computation.2 | async-start | bytes 524288 | tf_op jit(solution)/shard_map/all_to_all | solution.py:414
  60.7 7.6 %all-to-all-done.2.feats = bf16[8,64,256]{2,1,0:T(8,128)(2,1)S(1)} async-done(((bf16[8,64,256]{2,1,0:T(8,128)(2,1)}), bf16[8,64,256]{2,1,0:T(8,128)(2,1)S(1)}, u32[]{:S(2)}, u32[]{:S(2)}) %all-to-all-start.2) | async-done | bytes 262176 | tf_op jit(solution)/shard_map/all_to_all | solution.py:414
  68.3 0.0 collective-permute-done.9.rest_4_
  68.3 0.0 copy-done
  68.3 0.8 %partial_scores.1 = (f32[16,768]{1,0:T(8,128)S(1)}, f32[16,768]{1,0:T(8,128)S(1)}, f32[16,768]{1,0:T(8,128)S(1)}, f32[16,768]{1,0:T(8,128)S(1)}) custom-call(s32[1]{0:T(128)} %bitcast.at, bf16[8,64,256]{2,1,0:T(8,128)(2,1)S(1)} %all-to-all-done.2.feats, bf16[512,256]{1,0:T(8,128)(2,1)S(1)} %copy-done, bf16[512,256]{1,0:T(8,128)(2,1)S(1)} %collective-permute-done.rest_1_, ...), custom_call_target="tpu_custom_call" | custom-call | tf_op jit(solution)/shard_map/partial_scores/pallas_call | solution.py:417
  69.1 2.2 %collective-permute-start.10 = (f32[16,768]{1,0:T(8,128)S(1)}, f32[16,768]{1,0:T(8,128)S(1)}, u32[]{:S(2)}, u32[]{:S(2)}) collective-permute-start(f32[16,768]{1,0:T(8,128)S(1)} %get-tuple-element.46), channel_id=1, source_target_pairs={{0,1},{1,0},{2,3},{3,2},{4,5},{5,4},{6,7},{7,6},{8,9},{9,8},{10,11... | collective-permute-start | bytes 147464 | tf_op jit(solution)/shard_map/ppermute | solution.py:425
  71.3 0.8 %collective-permute-start.11 = (f32[16,768]{1,0:T(8,128)S(1)}, f32[16,768]{1,0:T(8,128)S(1)}, u32[]{:S(2)}, u32[]{:S(2)}) collective-permute-start(f32[16,768]{1,0:T(8,128)S(1)} %get-tuple-element.47), channel_id=1, source_target_pairs={{0,16},{1,17},{2,18},{3,19},{4,20},{5,21},{6,22},{7,23},{8,24},{9,... | collective-permute-start | bytes 147464 | tf_op jit(solution)/shard_map/ppermute | solution.py:425
  72.1 0.9 %collective-permute-start.12 = (f32[16,768]{1,0:T(8,128)S(1)}, f32[16,768]{1,0:T(8,128)S(1)}, u32[]{:S(2)}, u32[]{:S(2)}) collective-permute-start(f32[16,768]{1,0:T(8,128)S(1)} %get-tuple-element.48), channel_id=1, source_target_pairs={{0,17},{1,16},{2,19},{3,18},{4,21},{5,20},{6,23},{7,22},{8,25},{9,... | collective-permute-start | bytes 147464 | tf_op jit(solution)/shard_map/ppermute | solution.py:425
  73.0 0.0 collective-permute-done.10.one
  73.0 1.2 %collective-permute-done.11.two = f32[16,768]{1,0:T(8,128)S(1)} collective-permute-done((f32[16,768]{1,0:T(8,128)S(1)}, f32[16,768]{1,0:T(8,128)S(1)}, u32[]{:S(2)}, u32[]{:S(2)}) %collective-permute-start.11) | collective-permute-done | bytes 49184 | tf_op jit(solution)/shard_map/ppermute | solution.py:425
  74.3 1.6 %collective-permute-done.12.three = f32[16,768]{1,0:T(8,128)S(1)} collective-permute-done((f32[16,768]{1,0:T(8,128)S(1)}, f32[16,768]{1,0:T(8,128)S(1)}, u32[]{:S(2)}, u32[]{:S(2)}) %collective-permute-start.12) | collective-permute-done | bytes 49184 | tf_op jit(solution)/shard_map/ppermute | solution.py:425
  75.9 0.6 scores.1
  (1 shorter events, 0.0 us)
Async XLA Ops:
  2.1 24.2 %all-to-all-start = ((bf16[8,48,1024]{2,1,0:T(8,128)(2,1)}), bf16[8,48,1024]{2,1,0:T(8,128)(2,1)S(1)}, u32[]{:S(2)}, u32[]{:S(2)}) async-start(bf16[8,48,1024]{2,1,0:T(8,128)(2,1)} %prep.1), calls=%async_computation | async-start | bytes 1572864 | tf_op jit(solution)/shard_map/all_to_all | solution.py:339
  9.6 13.9 %collective-permute-start = (bf16[512,256]{1,0:T(8,128)(2,1)}, bf16[512,256]{1,0:T(8,128)(2,1)S(1)}, u32[]{:S(2)}, u32[]{:S(2)}) collective-permute-start(bf16[512,256]{1,0:T(8,128)(2,1)} %rest_0_.1), channel_id=1, source_target_pairs={{0,2},{1,3},{2,4},{3,5},{4,6},{5,7},{6,8},{7,9},{8,10},{9,11},{10,... | collective-permute-start | bytes 786440 | tf_op jit(solution)/shard_map/ppermute | solution.py:329
  11.2 12.3 %collective-permute-start.1 = (bf16[512,256]{1,0:T(8,128)(2,1)}, bf16[512,256]{1,0:T(8,128)(2,1)S(1)}, u32[]{:S(2)}, u32[]{:S(2)}) collective-permute-start(bf16[512,256]{1,0:T(8,128)(2,1)} %rest_0_.1), channel_id=1, source_target_pairs={{0,14},{1,15},{2,0},{3,1},{4,2},{5,3},{6,4},{7,5},{8,6},{9,7},{10,... | collective-permute-start | bytes 786440 | tf_op jit(solution)/shard_map/ppermute | solution.py:330
  23.5 44.8 %copy-start = (bf16[512,256]{1,0:T(8,128)(2,1)S(1)}, bf16[512,256]{1,0:T(8,128)(2,1)}, u32[]{:S(2)}) copy-start(bf16[512,256]{1,0:T(8,128)(2,1)} %rest_0_.1) | copy-start | bytes 786436
  23.5 11.2 %collective-permute-start.2 = (bf16[512,256]{1,0:T(8,128)(2,1)S(1)}, bf16[512,256]{1,0:T(8,128)(2,1)S(1)}, u32[]{:S(2)}, u32[]{:S(2)}) collective-permute-start(bf16[512,256]{1,0:T(8,128)(2,1)S(1)} %collective-permute-done.rest_1_), channel_id=1, source_target_pairs={{0,2},{1,3},{2,4},{3,5},{4,6},{5,7},{6,8},{7,9},{8,10},{9,11},{10,... | collective-permute-start | bytes 786440 | tf_op jit(solution)/shard_map/ppermute | solution.py:367
  23.6 11.2 %collective-permute-start.3 = (bf16[512,256]{1,0:T(8,128)(2,1)S(1)}, bf16[512,256]{1,0:T(8,128)(2,1)S(1)}, u32[]{:S(2)}, u32[]{:S(2)}) collective-permute-start(bf16[512,256]{1,0:T(8,128)(2,1)S(1)} %collective-permute-done.1.rest_7_), channel_id=1, source_target_pairs={{0,14},{1,15},{2,0},{3,1},{4,2},{5,3},{6,4},{7,5},{8,6},{9,7},{10,... | collective-permute-start | bytes 786440 | tf_op jit(solution)/shard_map/ppermute | solution.py:368
  26.3 0.9 %copy-start.1 = (bf16[8,48,1024]{2,1,0:T(8,128)(2,1)}, bf16[8,48,1024]{2,1,0:T(8,128)(2,1)S(1)}, u32[]{:S(2)}) copy-start(bf16[8,48,1024]{2,1,0:T(8,128)(2,1)S(1)} %all-to-all-done.w_in) | copy-start | bytes 2359300
  34.8 15.4 %all-to-all-start.1 = ((f32[8,128,128]{2,1,0:T(8,128)}), f32[8,128,128]{2,1,0:T(8,128)S(1)}, u32[]{:S(2)}, u32[]{:S(2)}) async-start(f32[8,128,128]{2,1,0:T(8,128)} %features.1), calls=%async_computation.1 | async-start | bytes 1048576 | tf_op jit(solution)/shard_map/all_to_all | solution.py:398
  41.3 15.1 %collective-permute-start.7 = (bf16[512,256]{1,0:T(8,128)(2,1)S(1)}, bf16[512,256]{1,0:T(8,128)(2,1)S(1)}, u32[]{:S(2)}, u32[]{:S(2)}) collective-permute-start(bf16[512,256]{1,0:T(8,128)(2,1)S(1)} %collective-permute-done.2.rest_2_), channel_id=1, source_target_pairs={{0,2},{1,3},{2,4},{3,5},{4,6},{5,7},{6,8},{7,9},{8,10},{9,11},{10,... | collective-permute-start | bytes 786440 | tf_op jit(solution)/shard_map/ppermute | solution.py:396
  41.4 15.1 %collective-permute-start.8 = (bf16[512,256]{1,0:T(8,128)(2,1)S(1)}, bf16[512,256]{1,0:T(8,128)(2,1)S(1)}, u32[]{:S(2)}, u32[]{:S(2)}) collective-permute-start(bf16[512,256]{1,0:T(8,128)(2,1)S(1)} %collective-permute-done.3.rest_6_), channel_id=1, source_target_pairs={{0,14},{1,15},{2,0},{3,1},{4,2},{5,3},{6,4},{7,5},{8,6},{9,7},{10,... | collective-permute-start | bytes 786440 | tf_op jit(solution)/shard_map/ppermute | solution.py:397
  50.3 5.0 %collective-permute-start.6 = (bf16[16,256]{1,0:T(8,128)(2,1)S(1)}, bf16[16,256]{1,0:T(8,128)(2,1)S(1)}, u32[]{:S(2)}, u32[]{:S(2)}) collective-permute-start(bf16[16,256]{1,0:T(8,128)(2,1)S(1)} %get-tuple-element.39), channel_id=1, source_target_pairs={{0,17},{1,16},{2,19},{3,18},{4,21},{5,20},{6,23},{7,22},{8,25},{9,... | collective-permute-start | bytes 24584 | tf_op jit(solution)/shard_map/ppermute | solution.py:408
  53.9 2.5 %collective-permute-start.5 = (bf16[16,256]{1,0:T(8,128)(2,1)S(1)}, bf16[16,256]{1,0:T(8,128)(2,1)S(1)}, u32[]{:S(2)}, u32[]{:S(2)}) collective-permute-start(bf16[16,256]{1,0:T(8,128)(2,1)S(1)} %get-tuple-element.38), channel_id=1, source_target_pairs={{0,16},{1,17},{2,18},{3,19},{4,20},{5,21},{6,22},{7,23},{8,24},{9,... | collective-permute-start | bytes 24584 | tf_op jit(solution)/shard_map/ppermute | solution.py:408
  55.0 1.4 %collective-permute-start.4 = (bf16[16,256]{1,0:T(8,128)(2,1)S(1)}, bf16[16,256]{1,0:T(8,128)(2,1)S(1)}, u32[]{:S(2)}, u32[]{:S(2)}) collective-permute-start(bf16[16,256]{1,0:T(8,128)(2,1)S(1)} %get-tuple-element.37), channel_id=1, source_target_pairs={{0,1},{1,0},{2,3},{3,2},{4,5},{5,4},{6,7},{7,6},{8,9},{9,8},{10,11... | collective-permute-start | bytes 24584 | tf_op jit(solution)/shard_map/ppermute | solution.py:408
  56.4 11.9 %collective-permute-start.9 = (bf16[512,256]{1,0:T(8,128)(2,1)S(1)}, bf16[512,256]{1,0:T(8,128)(2,1)S(1)}, u32[]{:S(2)}, u32[]{:S(2)}) collective-permute-start(bf16[512,256]{1,0:T(8,128)(2,1)S(1)} %collective-permute-done.7.rest_3_), channel_id=1, source_target_pairs={{0,2},{1,3},{2,4},{3,5},{4,6},{5,7},{6,8},{7,9},{8,10},{9,11},{10,... | collective-permute-start | bytes 786440 | tf_op jit(solution)/shard_map/ppermute | solution.py:412
  57.2 11.0 %all-to-all-start.2 = ((bf16[8,64,256]{2,1,0:T(8,128)(2,1)}), bf16[8,64,256]{2,1,0:T(8,128)(2,1)S(1)}, u32[]{:S(2)}, u32[]{:S(2)}) async-start(bf16[8,64,256]{2,1,0:T(8,128)(2,1)} %broadcast_in_dim.2), calls=%async_computation.2 | async-start | bytes 524288 | tf_op jit(solution)/shard_map/all_to_all | solution.py:414
  69.1 3.9 %collective-permute-start.10 = (f32[16,768]{1,0:T(8,128)S(1)}, f32[16,768]{1,0:T(8,128)S(1)}, u32[]{:S(2)}, u32[]{:S(2)}) collective-permute-start(f32[16,768]{1,0:T(8,128)S(1)} %get-tuple-element.46), channel_id=1, source_target_pairs={{0,1},{1,0},{2,3},{3,2},{4,5},{5,4},{6,7},{7,6},{8,9},{9,8},{10,11... | collective-permute-start | bytes 147464 | tf_op jit(solution)/shard_map/ppermute | solution.py:425
  71.3 3.0 %collective-permute-start.11 = (f32[16,768]{1,0:T(8,128)S(1)}, f32[16,768]{1,0:T(8,128)S(1)}, u32[]{:S(2)}, u32[]{:S(2)}) collective-permute-start(f32[16,768]{1,0:T(8,128)S(1)} %get-tuple-element.47), channel_id=1, source_target_pairs={{0,16},{1,17},{2,18},{3,19},{4,20},{5,21},{6,22},{7,23},{8,24},{9,... | collective-permute-start | bytes 147464 | tf_op jit(solution)/shard_map/ppermute | solution.py:425
  72.1 3.7 %collective-permute-start.12 = (f32[16,768]{1,0:T(8,128)S(1)}, f32[16,768]{1,0:T(8,128)S(1)}, u32[]{:S(2)}, u32[]{:S(2)}) collective-permute-start(f32[16,768]{1,0:T(8,128)S(1)} %get-tuple-element.48), channel_id=1, source_target_pairs={{0,17},{1,16},{2,19},{3,18},{4,21},{5,20},{6,23},{7,22},{8,25},{9,... | collective-permute-start | bytes 147464 | tf_op jit(solution)/shard_map/ppermute | solution.py:425

commit v4 on v3

--- a/solution.py
+++ b/solution.py
@@ -38,7 +38,7 @@
     return hi, (v - hi.astype(F32)).astype(BF16)
 
 
-def prep_kernel(me, keys, gain, down, up, out):
+def prep_kernel(me, four_at, z_at, keys, gain, down, up, out):
     shard = down.shape[0]
     rows = shard // 128
     own_gain = gain[pl.ds(pl.multiple_of(me[0] * rows, rows), rows), :]
@@ -71,17 +71,13 @@
     ]
 
 
-def early_kernel(
-    keys, gain_in, x_in, g_in, xs_out, r_out, ks_out, x, g, gain, table, acc, sq, sems
-):
+def early_kernel(keys, gain_in, x_in, acc, sq, x, gain, table, sems):
     steps, tokens, chunk = x.shape
-    width, gwidth = steps * chunk, g.shape[1]
-    copies = copies_of(x_pieces(x_in, x) + [(g_in, g), (gain_in, gain)], sems)
-    copies[-1].start()
-    for copy in copies[:-1]:
+    width = steps * chunk
+    copies = copies_of([(gain_in, gain)] + x_pieces(x_in, x), sems)
+    for copy in copies:
         copy.start()
-    s4 = signs(keys[1], 4, 0, gwidth, 128).astype(BF16)
-    copies[-1].wait()
+    copies[0].wait()
     for n in range(0, width, 128):
         gain_row = gain[n // 128 : n // 128 + 1, :]
         gain_hi = gain_row.astype(BF16).astype(F32)
@@ -96,7 +92,7 @@
         both = [2 * pair, 2 * pair + 1]
         columns = [pl.ds(pl.multiple_of(n * chunk, chunk), chunk) for n in both]
         for n, c in zip(both, columns):
-            pltpu.make_async_copy(x_in.at[:, c], x.at[n], sems.at[n]).wait()
+            pltpu.make_async_copy(x_in.at[:, c], x.at[n], sems.at[1 + n]).wait()
         acc[...] += dot(x[both[0]], table[:, columns[0]], NT) + dot(
             x[both[1]], table[:, columns[1]], NT
         )
@@ -108,32 +104,23 @@
                     total = total + piece * piece
             sq[t : t + 64, :] = total
 
-    copies[steps].wait()
-    ks_out[...] = dot(g[...], s4, NT) * (1.0 / math.sqrt(gwidth))
-    mean_sq = jnp.sum(sq[...].T, axis=0, keepdims=True) * (1.0 / width)
-    r = lax.rsqrt(mean_sq + 1e-05)
-    r_out[...] = jnp.broadcast_to(r, r_out.shape)
-    first = acc[...].T
-    xs = (first[0:64] + first[64:128]) * (r * (1.0 / math.sqrt(width)))
-    hi = xs.astype(BF16).astype(F32)
-    xs_out[0] = hi
-    xs_out[1] = xs - hi
-
 
 def main_kernel(
-    me, lengths, index_in, xs_in, r_in, ks_in, w_in, g_in, x_in, out_hbm,
-    index, xs, r, ks, w, g, x, out, ht, ua, ub, sems, out_sems,
+    me, keys, lengths, index_in, acc_in, sq_in, w_in, g_in, x_in, out_hbm,
+    index, acc, sq, w, g, x, out, xt, ua, ub, sems, out_sems,
 ):
     steps, tokens, chunk = x.shape
+    width, gwidth = steps * chunk, g.shape[1]
     half = tokens // 2
     copies = copies_of(
-        [(index_in, index), (xs_in, xs), (w_in, w), (g_in, g), (r_in, r), (ks_in, ks)]
+        [(index_in, index), (acc_in, acc), (sq_in, sq), (w_in, w), (g_in, g)]
         + x_pieces(x_in, x),
         sems,
     )
     for copy in copies:
         copy.start()
 
+    s4 = signs(keys[1], 4, 0, gwidth, 128).astype(BF16)
     position = me[0] * half + lax.broadcasted_iota(I32, (8, half), 1)
     example = lax.broadcasted_iota(I32, (8, half), 0)
     copies[0].wait()
@@ -150,17 +137,25 @@
         axis=0,
     )
     copies[1].wait()
+    copies[2].wait()
+    mean_sq = jnp.sum(sq[...].T, axis=0, keepdims=True) * (1.0 / width)
+    r = lax.rsqrt(mean_sq + 1e-05)
+    first = acc[...].T
+    xs = (first[0:64] + first[64:128]) * (r * (1.0 / math.sqrt(width)))
+    hi = xs.astype(BF16).astype(F32)
+    xt[0, 0:64] = hi
+    xt[1, 0:64] = xs - hi
     for p in range(2):
         for i in range(32):
             ua[p, 16 * i : 16 * i + 16, :] = jnp.concatenate(
                 [
-                    xs[p, 2 * i : 2 * i + 1, :] * m8,
-                    xs[p, 2 * i + 1 : 2 * i + 2, :] * m8,
+                    xt[p, 2 * i : 2 * i + 1, :] * m8,
+                    xt[p, 2 * i + 1 : 2 * i + 2, :] * m8,
                 ],
                 axis=0,
             ).astype(BF16)
 
-    copies[2].wait()
+    copies[3].wait()
     w_g = jnp.concatenate(
         [
             jnp.concatenate(
@@ -170,8 +165,9 @@
         ],
         axis=1,
     )
-    copies[3].wait()
-    two = dot(g[...], w_g, NT) * (1.0 / math.sqrt(128))
+    copies[4].wait()
+    pg = dot(g[...], jnp.concatenate([w_g, s4], axis=0), NT)
+    two = pg[:, 0:128] * (1.0 / math.sqrt(128))
     two = two + pltpu.roll(two, 64, 1)
     row = lax.broadcasted_iota(I32, (tokens, 128), 0) >= half
     lane = lax.broadcasted_iota(I32, (tokens, 128), 1) >= 64
@@ -187,22 +183,22 @@
         for n in range(2)
     ]
     done[0].start()
-    copies[4].wait()
-    copies[5].wait()
-    vb = jnp.concatenate(split(ks[...]), axis=1)
-
-    acc = None
+    vb = jnp.concatenate(split(pg[:, 128:256] * (1.0 / math.sqrt(gwidth))), axis=1)
+
+    total = None
     for n in range(steps):
-        copies[6 + n].wait()
+        copies[5 + n].wait()
         p = dot(w[n, 0:32, :], x[n], NT)
-        acc = p if acc is None else acc + p
-    hs = acc * (r[0:1, :] * (1.0 / math.sqrt(128)))
+        total = p if total is None else total + p
+    hs = total * (r * (1.0 / math.sqrt(128)))
     hi = hs.astype(BF16).astype(F32)
-    ht[0] = hi
-    ht[1] = hs - hi
+    xt[0, 64:96] = hi
+    xt[1, 64:96] = hs - hi
     for p in range(2):
         for i in range(32):
-            ub[p, 16 * i : 16 * i + 16, :] = (ht[p, i : i + 1, :] * m16).astype(BF16)
+            ub[p, 16 * i : 16 * i + 16, :] = (
+                xt[p, 64 + i : 65 + i, :] * m16
+            ).astype(BF16)
     fb = dot(ub[0], vb)
     fb = fb[:, 0:128] + fb[:, 128:256] + dot(ub[1], vb[:, 0:128])
     for n in range(8):
@@ -333,36 +329,26 @@
         prep_kernel,
         "prep",
         shape((n_fsdp, 48, chunk), BF16),
-        [SMEM, SMEM, VMEM, VMEM, VMEM],
+        [SMEM] * 4 + [VMEM] * 3,
         vmem=FULL_MIB,
-    )(fsdp_at, random_sketch_keys, gain, adapter_entry_matrix, adapter_exit_matrix)
+    )(fsdp_at, four_at, z_at, random_sketch_keys, gain, adapter_entry_matrix, adapter_exit_matrix)
     weights = lax.all_to_all(weights, "fsdp", 0, 0)
 
-    held = [
-        pltpu.VMEM((n_fsdp, tokens, chunk), BF16),
-        pltpu.VMEM((tokens, value_width), BF16),
-    ]
     early = kernel(
         early_kernel,
         "early",
+        [shape((tokens, 128), F32)] * 2,
+        [SMEM] + [HBM] * 2,
         [
-            shape((2, 64, tokens), F32),
-            shape((8, tokens), F32),
-            shape((tokens, 128), F32),
-        ],
-        [SMEM] + [HBM] * 3,
-        held
-        + [
+            pltpu.VMEM((n_fsdp, tokens, chunk), BF16),
             pltpu.VMEM((width // 128, 128), F32),
             pltpu.VMEM((128, width), BF16),
-            pltpu.VMEM((tokens, 128), F32),
-            pltpu.VMEM((tokens, 128), F32),
-            pltpu.SemaphoreType.DMA((2 + n_fsdp,)),
+            pltpu.SemaphoreType.DMA((1 + n_fsdp,)),
         ],
         vmem=FULL_MIB,
         flops=2 * tokens * width * 256,
         nbytes=12 * MIB,
-    )(random_sketch_keys, gain, x, g)
+    )(random_sketch_keys, gain, x)
     early, refs_up[0], refs_down[0] = tie((early, refs_up[0], refs_down[0]))
     refs_up.append(lax.ppermute(refs_up[0], "dp", up))
     refs_down.append(lax.ppermute(refs_down[0], "dp", down))
@@ -371,27 +357,35 @@
         main_kernel,
         "features",
         shape((8, 128, 128), F32),
-        [SMEM] * 2 + [HBM] * 7,
+        [SMEM] * 3 + [HBM] * 6,
         [
             pltpu.VMEM((seq_count, local_len), I32),
-            pltpu.VMEM((2, 64, tokens), F32),
-            pltpu.VMEM((8, tokens), F32),
+            pltpu.VMEM((tokens, 128), F32),
             pltpu.VMEM((tokens, 128), F32),
             pltpu.VMEM((n_fsdp, 48, chunk), BF16),
-            held[1],
-            held[0],
+            pltpu.VMEM((tokens, value_width), BF16),
+            pltpu.VMEM((n_fsdp, tokens, chunk), BF16),
             pltpu.VMEM((8, 128, 128), F32),
-            pltpu.VMEM((2, 32, tokens), F32),
+            pltpu.VMEM((2, 96, tokens), F32),
             pltpu.VMEM((2, 512, tokens), BF16),
             pltpu.VMEM((2, 512, tokens), BF16),
-            pltpu.SemaphoreType.DMA((6 + n_fsdp,)),
+            pltpu.SemaphoreType.DMA((5 + n_fsdp,)),
             pltpu.SemaphoreType.DMA((2,)),
         ],
         vmem=FULL_MIB,
         flops=2 * tokens * width * 256,
         nbytes=12 * MIB,
         outs=HBM,
-    )(fsdp_at, live_row_length, position_example_index, *early, weights, g, x)
+    )(
+        fsdp_at,
+        random_sketch_keys,
+        live_row_length,
+        position_example_index,
+        *early,
+        weights,
+        g,
+        x,
+    )
     features, refs_up[1], refs_down[1] = tie((features, refs_up[1], refs_down[1]))
     refs_up.append(lax.ppermute(refs_up[1], "dp", up))
     refs_down.append(lax.ppermute(refs_down[1], "dp", down))

time: 76.9 us -> 76.1 us (0.990)
  blocking collectives: 0 us -> 10.8 us
  waiting for transfers between devices: 18 us -> 10.7 us
  starting transfers between devices: 37.3 us -> 34.3 us
    all_to_all x0 -> x1, blocking collectives: none -> 10.8 us  [per_device(): feats = lax.all_to_all(feats, 'fsdp', 0, 0)]
    all_to_all x1 -> x0, waiting for transfers between devices: 7.58 us -> none  [per_device(): feats = lax.all_to_all(feats, 'fsdp', 0, 0)]
    all_to_all x1 -> x0, starting transfers between devices: 3.46 us -> none  [per_device(): feats = lax.all_to_all(feats, 'fsdp', 0, 0)]
  transfers between devices with their start and end apart: 16 -> 15, of which waited for: 6 -> 5; matrix products, arithmetic and copies ran while one was open for 1% -> 0% of each run, Pallas kernels for 21% -> 20%
where the time goes in v4:
time: 76.1 us; the launch traced here: 75.8 us
  starting transfers between devices  34.3 us (45%)
  Pallas kernels  19 us (25%)
  blocking collectives  10.8 us (14%)
  waiting for transfers between devices  10.7 us (14%)
  local copies, waits for them, and re-layouts  0.9 us (1%)
    all_to_all x1, blocking collectives, per_device(): feats = lax.all_to_all(feats, 'fsdp', 0, 0)  10.8 us
    ppermute x6, starting transfers between devices, per_device(): lax.ppermute(piece, 'dp', swap)  9.03 us
    pallas_call x1, Pallas kernels, per_device(): kernel(early_kernel, 'early', [shape((tokens, 128), F32)] * 2, [SMEM] + [...  7.76 us
    pallas_call x1, Pallas kernels, per_device(): kernel(main_kernel, 'features', shape((8, 128, 128), F32), [SMEM] * 3 + [...  7.65 us
    all_to_all x1, starting transfers between devices, per_device(): weights = lax.all_to_all(weights, 'fsdp', 0, 0)  7.48 us
    all_to_all x1, starting transfers between devices, per_device(): features = lax.all_to_all(features, 'fsdp', 0, 0)  6.59 us
    all_to_all x1, waiting for transfers between devices, per_device(): features = lax.all_to_all(features, 'fsdp', 0, 0)  6.16 us
    ppermute x6, waiting for transfers between devices, per_device(): lax.ppermute(piece, 'dp', swap)  4.53 us
  transfers between devices with their start and end apart: 15, of which 5 were waited for; matrix products, arithmetic and copies ran while one was open for 0% of the time, Pallas kernels for 20%

profile of v4, /device:TPU:1, one launch (start us, length us, event | category | flops | bytes accessed | tf_op | source)
XLA Modules:
  0.0 75.8 jit_solution(2544435443577673911)
XLA Ops:
  0.0 2.1 %prep.1 = bf16[8,48,1024]{2,1,0:T(8,128)(2,1)} custom-call(s32[1]{0:T(128)} %bitcast.2.me, s32[1]{0:T(128)} %bitcast.1.four_at.me, s32[1]{0:T(128)} %bitcast.z_at.at, s32[2]{0:T(128)} %keys.5, f32[64,128]{1,0:T(8,128)} %bitcast.9, bf16[1024,128]{1,0:T(8,128)(2,1)} %down.1, bf16[128,128]{1,0:T(8,128)(2,1)} %up.1), custom_call_target="tpu_custom_call" | custom-call | tf_op jit(solution)/shard_map/prep/pallas_call | solution.py:328
  2.1 7.5 %all-to-all-start = ((bf16[8,48,1024]{2,1,0:T(8,128)(2,1)}), bf16[8,48,1024]{2,1,0:T(8,128)(2,1)S(1)}, u32[]{:S(2)}, u32[]{:S(2)}) async-start(bf16[8,48,1024]{2,1,0:T(8,128)(2,1)} %prep.1), calls=%async_computation | async-start | bytes 1572864 | tf_op jit(solution)/shard_map/all_to_all | solution.py:335
  9.6 1.6 %collective-permute-start = (bf16[512,256]{1,0:T(8,128)(2,1)}, bf16[512,256]{1,0:T(8,128)(2,1)S(1)}, u32[]{:S(2)}, u32[]{:S(2)}) collective-permute-start(bf16[512,256]{1,0:T(8,128)(2,1)} %rest_0_.1), channel_id=1, source_target_pairs={{0,2},{1,3},{2,4},{3,5},{4,6},{5,7},{6,8},{7,9},{8,10},{9,11},{10,... | collective-permute-start | bytes 786440 | tf_op jit(solution)/shard_map/ppermute | solution.py:325
  11.2 4.0 %collective-permute-start.1 = (bf16[512,256]{1,0:T(8,128)(2,1)}, bf16[512,256]{1,0:T(8,128)(2,1)S(1)}, u32[]{:S(2)}, u32[]{:S(2)}) collective-permute-start(bf16[512,256]{1,0:T(8,128)(2,1)} %rest_0_.1), channel_id=1, source_target_pairs={{0,14},{1,15},{2,0},{3,1},{4,2},{5,3},{6,4},{7,5},{8,6},{9,7},{10,... | collective-permute-start | bytes 786440 | tf_op jit(solution)/shard_map/ppermute | solution.py:326
  15.2 7.8 %early.1 = (f32[512,128]{1,0:T(8,128)}, f32[512,128]{1,0:T(8,128)}) custom-call(s32[2]{0:T(128)} %keys.5, f32[64,128]{1,0:T(8,128)} %bitcast.10, bf16[512,8192]{1,0:T(8,128)(2,1)} %bitcast.6), custom_call_target="tpu_custom_call" | custom-call | flops 2147483648 | bytes 12582912 | tf_op jit(solution)/shard_map/early/pallas_call | solution.py:337
  23.0 0.0 copy-start
  23.0 0.0 collective-permute-done.rest_1_
  23.0 0.0 collective-permute-done.1.rest_7_
  23.0 0.1 collective-permute-start.2
  23.1 2.7 %collective-permute-start.3 = (bf16[512,256]{1,0:T(8,128)(2,1)S(1)}, bf16[512,256]{1,0:T(8,128)(2,1)S(1)}, u32[]{:S(2)}, u32[]{:S(2)}) collective-permute-start(bf16[512,256]{1,0:T(8,128)(2,1)S(1)} %collective-permute-done.1.rest_7_), channel_id=1, source_target_pairs={{0,14},{1,15},{2,0},{3,1},{4,2},{5,3},{6,4},{7,5},{8,6},{9,7},{10,... | collective-permute-start | bytes 786440 | tf_op jit(solution)/shard_map/ppermute | solution.py:354
  25.8 0.0 all-to-all-done.w_in
  25.8 0.0 copy-start.1
  25.8 0.9 %copy-done.1 = bf16[8,48,1024]{2,1,0:T(8,128)(2,1)} copy-done((bf16[8,48,1024]{2,1,0:T(8,128)(2,1)}, bf16[8,48,1024]{2,1,0:T(8,128)(2,1)S(1)}, u32[]{:S(2)}) %copy-start.1) | copy-done | bytes 786456
  26.7 7.6 %features.1 = f32[8,128,128]{2,1,0:T(8,128)} custom-call(s32[1]{0:T(128)} %bitcast.2.me, s32[2]{0:T(128)} %keys.5, s32[2]{0:T(128)} %lengths.1, s32[2,256]{1,0:T(2,128)} %index_in.1, f32[512,128]{1,0:T(8,128)} %get-tuple-element.27.acc_in, f32[512,128]{1,0:T(8,128)} %get-tuple-element.28.sq_in, bf16[8,48,1024]{2,1,0:T(8,128)(2,1)} %copy-done.1, ...), custom_call_target="tpu_custom_call" | custom-call | flops 2147483648 | bytes 12582912 | tf_op jit(solution)/shard_map/features/pallas_call | solution.py:356
  34.3 0.0 collective-permute-done.2.rest_2_
  34.3 0.0 collective-permute-done.3.rest_6_
  34.3 6.6 %all-to-all-start.1 = ((f32[8,128,128]{2,1,0:T(8,128)}), f32[8,128,128]{2,1,0:T(8,128)S(1)}, u32[]{:S(2)}, u32[]{:S(2)}) async-start(f32[8,128,128]{2,1,0:T(8,128)} %features.1), calls=%async_computation.1 | async-start | bytes 1048576 | tf_op jit(solution)/shard_map/all_to_all | solution.py:392
  40.9 0.0 collective-permute-start.7
  40.9 2.7 %collective-permute-start.8 = (bf16[512,256]{1,0:T(8,128)(2,1)S(1)}, bf16[512,256]{1,0:T(8,128)(2,1)S(1)}, u32[]{:S(2)}, u32[]{:S(2)}) collective-permute-start(bf16[512,256]{1,0:T(8,128)(2,1)S(1)} %collective-permute-done.3.rest_6_), channel_id=1, source_target_pairs={{0,14},{1,15},{2,0},{3,1},{4,2},{5,3},{6,4},{7,5},{8,6},{9,7},{10,... | collective-permute-start | bytes 786440 | tf_op jit(solution)/shard_map/ppermute | solution.py:391
  43.6 6.2 %all-to-all-done.1.parts = f32[8,128,128]{2,1,0:T(8,128)S(1)} async-done(((f32[8,128,128]{2,1,0:T(8,128)}), f32[8,128,128]{2,1,0:T(8,128)S(1)}, u32[]{:S(2)}, u32[]{:S(2)}) %all-to-all-start.1) | async-done | bytes 524320 | tf_op jit(solution)/shard_map/all_to_all | solution.py:392
  49.8 0.1 sum_features.1
  49.9 3.4 %collective-permute-start.4 = (bf16[16,256]{1,0:T(8,128)(2,1)S(1)}, bf16[16,256]{1,0:T(8,128)(2,1)S(1)}, u32[]{:S(2)}, u32[]{:S(2)}) collective-permute-start(bf16[16,256]{1,0:T(8,128)(2,1)S(1)} %get-tuple-element.33), channel_id=1, source_target_pairs={{0,1},{1,0},{2,3},{3,2},{4,5},{5,4},{6,7},{7,6},{8,9},{9,8},{10,11... | collective-permute-start | bytes 24584 | tf_op jit(solution)/shard_map/ppermute | solution.py:402
  53.2 0.4 collective-permute-start.5
  53.6 1.4 %collective-permute-start.6 = (bf16[16,256]{1,0:T(8,128)(2,1)S(1)}, bf16[16,256]{1,0:T(8,128)(2,1)S(1)}, u32[]{:S(2)}, u32[]{:S(2)}) collective-permute-start(bf16[16,256]{1,0:T(8,128)(2,1)S(1)} %get-tuple-element.35), channel_id=1, source_target_pairs={{0,17},{1,16},{2,19},{3,18},{4,21},{5,20},{6,23},{7,22},{8,25},{9,... | collective-permute-start | bytes 24584 | tf_op jit(solution)/shard_map/ppermute | solution.py:402
  55.0 0.0 collective-permute-done.4
  55.0 0.8 %collective-permute-done.5 = bf16[16,256]{1,0:T(8,128)(2,1)S(1)} collective-permute-done((bf16[16,256]{1,0:T(8,128)(2,1)S(1)}, bf16[16,256]{1,0:T(8,128)(2,1)S(1)}, u32[]{:S(2)}, u32[]{:S(2)}) %collective-permute-start.5) | collective-permute-done | bytes 8224 | tf_op jit(solution)/shard_map/ppermute | solution.py:402
  55.8 0.9 %collective-permute-done.6 = bf16[16,256]{1,0:T(8,128)(2,1)S(1)} collective-permute-done((bf16[16,256]{1,0:T(8,128)(2,1)S(1)}, bf16[16,256]{1,0:T(8,128)(2,1)S(1)}, u32[]{:S(2)}, u32[]{:S(2)}) %collective-permute-start.6) | collective-permute-done | bytes 8224 | tf_op jit(solution)/shard_map/ppermute | solution.py:402
  56.7 0.0 collective-permute-done.7.rest_3_
  56.7 0.0 collective-permute-done.8.rest_5_
  56.7 0.1 collective-permute-start.9
  56.8 10.8 %all_to_all.15.feats = bf16[8,64,256]{2,1,0:T(8,128)(2,1)S(1)} all-to-all(bf16[8,64,256]{2,1,0:T(8,128)(2,1)S(1)} %broadcast_in_dim.2), channel_id=1, replica_groups=mesh['fsdp'=8,'dp'=32] {'fsdp'}, dimensions={0} | all-to-all | bytes 524288 | tf_op jit(solution)/shard_map/all_to_all | solution.py:408
  67.6 0.0 collective-permute-done.9.rest_4_
  67.6 0.0 copy-done
  67.6 0.8 %partial_scores.1 = (f32[16,768]{1,0:T(8,128)S(1)}, f32[16,768]{1,0:T(8,128)S(1)}, f32[16,768]{1,0:T(8,128)S(1)}, f32[16,768]{1,0:T(8,128)S(1)}) custom-call(s32[1]{0:T(128)} %bitcast.z_at.at, bf16[8,64,256]{2,1,0:T(8,128)(2,1)S(1)} %all_to_all.15.feats, bf16[512,256]{1,0:T(8,128)(2,1)S(1)} %copy-done, bf16[512,256]{1,0:T(8,128)(2,1)S(1)} %collective-permute-done.rest_1_, ...), custom_call_target="tpu_custom_call" | custom-call | tf_op jit(solution)/shard_map/partial_scores/pallas_call | solution.py:411
  68.5 2.2 %collective-permute-start.10 = (f32[16,768]{1,0:T(8,128)S(1)}, f32[16,768]{1,0:T(8,128)S(1)}, u32[]{:S(2)}, u32[]{:S(2)}) collective-permute-start(f32[16,768]{1,0:T(8,128)S(1)} %get-tuple-element.42), channel_id=1, source_target_pairs={{0,1},{1,0},{2,3},{3,2},{4,5},{5,4},{6,7},{7,6},{8,9},{9,8},{10,11... | collective-permute-start | bytes 147464 | tf_op jit(solution)/shard_map/ppermute | solution.py:419
  70.6 0.2 collective-permute-start.11
  70.9 1.5 %collective-permute-start.12 = (f32[16,768]{1,0:T(8,128)S(1)}, f32[16,768]{1,0:T(8,128)S(1)}, u32[]{:S(2)}, u32[]{:S(2)}) collective-permute-start(f32[16,768]{1,0:T(8,128)S(1)} %get-tuple-element.44), channel_id=1, source_target_pairs={{0,17},{1,16},{2,19},{3,18},{4,21},{5,20},{6,23},{7,22},{8,25},{9,... | collective-permute-start | bytes 147464 | tf_op jit(solution)/shard_map/ppermute | solution.py:419
  72.4 0.0 collective-permute-done.10.one
  72.4 1.2 %collective-permute-done.11.two = f32[16,768]{1,0:T(8,128)S(1)} collective-permute-done((f32[16,768]{1,0:T(8,128)S(1)}, f32[16,768]{1,0:T(8,128)S(1)}, u32[]{:S(2)}, u32[]{:S(2)}) %collective-permute-start.11) | collective-permute-done | bytes 49184 | tf_op jit(solution)/shard_map/ppermute | solution.py:419
  73.6 1.6 %collective-permute-done.12.three = f32[16,768]{1,0:T(8,128)S(1)} collective-permute-done((f32[16,768]{1,0:T(8,128)S(1)}, f32[16,768]{1,0:T(8,128)S(1)}, u32[]{:S(2)}, u32[]{:S(2)}) %collective-permute-start.12) | collective-permute-done | bytes 49184 | tf_op jit(solution)/shard_map/ppermute | solution.py:419
  75.2 0.6 scores.1
  (2 shorter events, 0.0 us)
Async XLA Ops:
  2.1 23.7 %all-to-all-start = ((bf16[8,48,1024]{2,1,0:T(8,128)(2,1)}), bf16[8,48,1024]{2,1,0:T(8,128)(2,1)S(1)}, u32[]{:S(2)}, u32[]{:S(2)}) async-start(bf16[8,48,1024]{2,1,0:T(8,128)(2,1)} %prep.1), calls=%async_computation | async-start | bytes 1572864 | tf_op jit(solution)/shard_map/all_to_all | solution.py:335
  9.6 13.4 %collective-permute-start = (bf16[512,256]{1,0:T(8,128)(2,1)}, bf16[512,256]{1,0:T(8,128)(2,1)S(1)}, u32[]{:S(2)}, u32[]{:S(2)}) collective-permute-start(bf16[512,256]{1,0:T(8,128)(2,1)} %rest_0_.1), channel_id=1, source_target_pairs={{0,2},{1,3},{2,4},{3,5},{4,6},{5,7},{6,8},{7,9},{8,10},{9,11},{10,... | collective-permute-start | bytes 786440 | tf_op jit(solution)/shard_map/ppermute | solution.py:325
  11.2 11.8 %collective-permute-start.1 = (bf16[512,256]{1,0:T(8,128)(2,1)}, bf16[512,256]{1,0:T(8,128)(2,1)S(1)}, u32[]{:S(2)}, u32[]{:S(2)}) collective-permute-start(bf16[512,256]{1,0:T(8,128)(2,1)} %rest_0_.1), channel_id=1, source_target_pairs={{0,14},{1,15},{2,0},{3,1},{4,2},{5,3},{6,4},{7,5},{8,6},{9,7},{10,... | collective-permute-start | bytes 786440 | tf_op jit(solution)/shard_map/ppermute | solution.py:326
  23.0 44.6 %copy-start = (bf16[512,256]{1,0:T(8,128)(2,1)S(1)}, bf16[512,256]{1,0:T(8,128)(2,1)}, u32[]{:S(2)}) copy-start(bf16[512,256]{1,0:T(8,128)(2,1)} %rest_0_.1) | copy-start | bytes 786436
  23.0 11.3 %collective-permute-start.2 = (bf16[512,256]{1,0:T(8,128)(2,1)S(1)}, bf16[512,256]{1,0:T(8,128)(2,1)S(1)}, u32[]{:S(2)}, u32[]{:S(2)}) collective-permute-start(bf16[512,256]{1,0:T(8,128)(2,1)S(1)} %collective-permute-done.rest_1_), channel_id=1, source_target_pairs={{0,2},{1,3},{2,4},{3,5},{4,6},{5,7},{6,8},{7,9},{8,10},{9,11},{10,... | collective-permute-start | bytes 786440 | tf_op jit(solution)/shard_map/ppermute | solution.py:353
  23.1 11.2 %collective-permute-start.3 = (bf16[512,256]{1,0:T(8,128)(2,1)S(1)}, bf16[512,256]{1,0:T(8,128)(2,1)S(1)}, u32[]{:S(2)}, u32[]{:S(2)}) collective-permute-start(bf16[512,256]{1,0:T(8,128)(2,1)S(1)} %collective-permute-done.1.rest_7_), channel_id=1, source_target_pairs={{0,14},{1,15},{2,0},{3,1},{4,2},{5,3},{6,4},{7,5},{8,6},{9,7},{10,... | collective-permute-start | bytes 786440 | tf_op jit(solution)/shard_map/ppermute | solution.py:354
  25.8 0.9 %copy-start.1 = (bf16[8,48,1024]{2,1,0:T(8,128)(2,1)}, bf16[8,48,1024]{2,1,0:T(8,128)(2,1)S(1)}, u32[]{:S(2)}) copy-start(bf16[8,48,1024]{2,1,0:T(8,128)(2,1)S(1)} %all-to-all-done.w_in) | copy-start | bytes 2359300
  34.3 15.4 %all-to-all-start.1 = ((f32[8,128,128]{2,1,0:T(8,128)}), f32[8,128,128]{2,1,0:T(8,128)S(1)}, u32[]{:S(2)}, u32[]{:S(2)}) async-start(f32[8,128,128]{2,1,0:T(8,128)} %features.1), calls=%async_computation.1 | async-start | bytes 1048576 | tf_op jit(solution)/shard_map/all_to_all | solution.py:392
  40.9 15.8 %collective-permute-start.7 = (bf16[512,256]{1,0:T(8,128)(2,1)S(1)}, bf16[512,256]{1,0:T(8,128)(2,1)S(1)}, u32[]{:S(2)}, u32[]{:S(2)}) collective-permute-start(bf16[512,256]{1,0:T(8,128)(2,1)S(1)} %collective-permute-done.2.rest_2_), channel_id=1, source_target_pairs={{0,2},{1,3},{2,4},{3,5},{4,6},{5,7},{6,8},{7,9},{8,10},{9,11},{10,... | collective-permute-start | bytes 786440 | tf_op jit(solution)/shard_map/ppermute | solution.py:390
  40.9 15.8 %collective-permute-start.8 = (bf16[512,256]{1,0:T(8,128)(2,1)S(1)}, bf16[512,256]{1,0:T(8,128)(2,1)S(1)}, u32[]{:S(2)}, u32[]{:S(2)}) collective-permute-start(bf16[512,256]{1,0:T(8,128)(2,1)S(1)} %collective-permute-done.3.rest_6_), channel_id=1, source_target_pairs={{0,14},{1,15},{2,0},{3,1},{4,2},{5,3},{6,4},{7,5},{8,6},{9,7},{10,... | collective-permute-start | bytes 786440 | tf_op jit(solution)/shard_map/ppermute | solution.py:391
  49.9 5.1 %collective-permute-start.4 = (bf16[16,256]{1,0:T(8,128)(2,1)S(1)}, bf16[16,256]{1,0:T(8,128)(2,1)S(1)}, u32[]{:S(2)}, u32[]{:S(2)}) collective-permute-start(bf16[16,256]{1,0:T(8,128)(2,1)S(1)} %get-tuple-element.33), channel_id=1, source_target_pairs={{0,1},{1,0},{2,3},{3,2},{4,5},{5,4},{6,7},{7,6},{8,9},{9,8},{10,11... | collective-permute-start | bytes 24584 | tf_op jit(solution)/shard_map/ppermute | solution.py:402
  53.2 2.5 %collective-permute-start.5 = (bf16[16,256]{1,0:T(8,128)(2,1)S(1)}, bf16[16,256]{1,0:T(8,128)(2,1)S(1)}, u32[]{:S(2)}, u32[]{:S(2)}) collective-permute-start(bf16[16,256]{1,0:T(8,128)(2,1)S(1)} %get-tuple-element.34), channel_id=1, source_target_pairs={{0,16},{1,17},{2,18},{3,19},{4,20},{5,21},{6,22},{7,23},{8,24},{9,... | collective-permute-start | bytes 24584 | tf_op jit(solution)/shard_map/ppermute | solution.py:402
  53.6 3.1 %collective-permute-start.6 = (bf16[16,256]{1,0:T(8,128)(2,1)S(1)}, bf16[16,256]{1,0:T(8,128)(2,1)S(1)}, u32[]{:S(2)}, u32[]{:S(2)}) collective-permute-start(bf16[16,256]{1,0:T(8,128)(2,1)S(1)} %get-tuple-element.35), channel_id=1, source_target_pairs={{0,17},{1,16},{2,19},{3,18},{4,21},{5,20},{6,23},{7,22},{8,25},{9,... | collective-permute-start | bytes 24584 | tf_op jit(solution)/shard_map/ppermute | solution.py:402
  56.7 10.9 %collective-permute-start.9 = (bf16[512,256]{1,0:T(8,128)(2,1)S(1)}, bf16[512,256]{1,0:T(8,128)(2,1)S(1)}, u32[]{:S(2)}, u32[]{:S(2)}) collective-permute-start(bf16[512,256]{1,0:T(8,128)(2,1)S(1)} %collective-permute-done.7.rest_3_), channel_id=1, source_target_pairs={{0,2},{1,3},{2,4},{3,5},{4,6},{5,7},{6,8},{7,9},{8,10},{9,11},{10,... | collective-permute-start | bytes 786440 | tf_op jit(solution)/shard_map/ppermute | solution.py:406
  68.5 3.9 %collective-permute-start.10 = (f32[16,768]{1,0:T(8,128)S(1)}, f32[16,768]{1,0:T(8,128)S(1)}, u32[]{:S(2)}, u32[]{:S(2)}) collective-permute-start(f32[16,768]{1,0:T(8,128)S(1)} %get-tuple-element.42), channel_id=1, source_target_pairs={{0,1},{1,0},{2,3},{3,2},{4,5},{5,4},{6,7},{7,6},{8,9},{9,8},{10,11... | collective-permute-start | bytes 147464 | tf_op jit(solution)/shard_map/ppermute | solution.py:419
  70.6 3.0 %collective-permute-start.11 = (f32[16,768]{1,0:T(8,128)S(1)}, f32[16,768]{1,0:T(8,128)S(1)}, u32[]{:S(2)}, u32[]{:S(2)}) collective-permute-start(f32[16,768]{1,0:T(8,128)S(1)} %get-tuple-element.43), channel_id=1, source_target_pairs={{0,16},{1,17},{2,18},{3,19},{4,20},{5,21},{6,22},{7,23},{8,24},{9,... | collective-permute-start | bytes 147464 | tf_op jit(solution)/shard_map/ppermute | solution.py:419
  70.9 4.3 %collective-permute-start.12 = (f32[16,768]{1,0:T(8,128)S(1)}, f32[16,768]{1,0:T(8,128)S(1)}, u32[]{:S(2)}, u32[]{:S(2)}) collective-permute-start(f32[16,768]{1,0:T(8,128)S(1)} %get-tuple-element.44), channel_id=1, source_target_pairs={{0,17},{1,16},{2,19},{3,18},{4,21},{5,20},{6,23},{7,22},{8,25},{9,... | collective-permute-start | bytes 147464 | tf_op jit(solution)/shard_map/ppermute | solution.py:419

commit v5 on v4

--- a/solution.py
+++ b/solution.py
@@ -315,7 +315,6 @@
     up, down = (
         [(n, n // top * top + (n + 2 * way) % top) for n in range(n_dp)] for way in (1, -1)
     )
-    tie = lax.optimization_barrier
 
     x = residual.reshape(tokens, width)
     g = value_output_gradient.reshape(tokens, value_width)
@@ -349,7 +348,6 @@
         flops=2 * tokens * width * 256,
         nbytes=12 * MIB,
     )(random_sketch_keys, gain, x)
-    early, refs_up[0], refs_down[0] = tie((early, refs_up[0], refs_down[0]))
     refs_up.append(lax.ppermute(refs_up[0], "dp", up))
     refs_down.append(lax.ppermute(refs_down[0], "dp", down))
 
@@ -386,7 +384,6 @@
         g,
         x,
     )
-    features, refs_up[1], refs_down[1] = tie((features, refs_up[1], refs_down[1]))
     refs_up.append(lax.ppermute(refs_up[1], "dp", up))
     refs_down.append(lax.ppermute(refs_down[1], "dp", down))
     features = lax.all_to_all(features, "fsdp", 0, 0)
@@ -402,7 +399,6 @@
         lax.ppermute(piece, "dp", swap) for piece, swap in zip(pieces[1:], swaps)
     ]
     feats = jnp.concatenate(pieces, axis=0)
-    feats, refs_up[2], refs_down[2] = tie((feats, refs_up[2], refs_down[2]))
     refs_up.append(lax.ppermute(refs_up[2], "dp", up))
     feats = jnp.broadcast_to(feats[None], (n_fsdp,) + feats.shape)
     feats = lax.all_to_all(feats, "fsdp", 0, 0)

time: 76.1 us -> 75.3 us (0.989)
  blocking collectives: 10.8 us -> 0 us
  waiting for transfers between devices: 10.7 us -> 16.3 us
  starting transfers between devices: 34.3 us -> 37.9 us
    all_to_all x1 -> x0, blocking collectives: 10.8 us -> none  [per_device(): feats = lax.all_to_all(feats, 'fsdp', 0, 0)]
    all_to_all x0 -> x1, starting transfers between devices: none -> 3.41 us  [per_device(): feats = lax.all_to_all(feats, 'fsdp', 0, 0)]
    ppermute x1, waiting for transfers between devices: 0.01 us -> 3.1 us  [per_device(): refs_up.append(lax.ppermute(refs_up[2], 'dp', up))]
    all_to_all x0 -> x1, waiting for transfers between devices: none -> 3.04 us  [per_device(): feats = lax.all_to_all(feats, 'fsdp', 0, 0)]
    ppermute x6, waiting for transfers between devices: 4.53 us -> 2.83 us  [per_device(): lax.ppermute(piece, 'dp', swap)]
    ppermute x1, waiting for transfers between devices: 0.01 us -> 1.37 us  [per_device(): refs_down.append(lax.ppermute(refs_down[1], 'dp', down))]
  transfers between devices with their start and end apart: 15 -> 16, of which waited for: 5 -> 6; matrix products, arithmetic and copies ran while one was open for 0% -> 1% of each run, Pallas kernels for 20% -> 21%
where the time goes in v5:
time: 75.3 us; the launch traced here: 74.9 us
  starting transfers between devices  37.9 us (50%)
  Pallas kernels  19.1 us (25%)
  waiting for transfers between devices  16.3 us (22%)
  local copies, waits for them, and re-layouts  1.6 us (2%)
    ppermute x6, starting transfers between devices, per_device(): lax.ppermute(piece, 'dp', swap)  9.03 us
    pallas_call x1, Pallas kernels, per_device(): kernel(early_kernel, 'early', [shape((tokens, 128), F32)] * 2, [SMEM] + [...  7.75 us
    pallas_call x1, Pallas kernels, per_device(): kernel(main_kernel, 'features', shape((8, 128, 128), F32), [SMEM] * 3 + [...  7.69 us
    all_to_all x1, starting transfers between devices, per_device(): weights = lax.all_to_all(weights, 'fsdp', 0, 0)  7.48 us
    all_to_all x1, starting transfers between devices, per_device(): features = lax.all_to_all(features, 'fsdp', 0, 0)  6.58 us
    all_to_all x1, waiting for transfers between devices, per_device(): features = lax.all_to_all(features, 'fsdp', 0, 0)  5.91 us
    ppermute x1, starting transfers between devices, per_device(): refs_down = [lax.ppermute(reference_gradients, 'dp', down)]  4.03 us
    all_to_all x1, starting transfers between devices, per_device(): feats = lax.all_to_all(feats, 'fsdp', 0, 0)  3.41 us
  transfers between devices with their start and end apart: 16, of which 6 were waited for; matrix products, arithmetic and copies ran while one was open for 1% of the time, Pallas kernels for 21%

profile of v5, /device:TPU:1, one launch (start us, length us, event | category | flops | bytes accessed | tf_op | source)
XLA Modules:
  0.0 74.9 jit_solution(18380169667201859086)
XLA Ops:
  0.0 2.1 %prep.1 = bf16[8,48,1024]{2,1,0:T(8,128)(2,1)} custom-call(s32[1]{0:T(128)} %bitcast.2.me, s32[1]{0:T(128)} %bitcast.1.four_at.me, s32[1]{0:T(128)} %bitcast.z_at.at, s32[2]{0:T(128)} %keys.5, f32[64,128]{1,0:T(8,128)} %bitcast.9, bf16[1024,128]{1,0:T(8,128)(2,1)} %down.1, bf16[128,128]{1,0:T(8,128)(2,1)} %up.1), custom_call_target="tpu_custom_call" | custom-call | tf_op jit(solution)/shard_map/prep/pallas_call | solution.py:327
  2.1 7.5 %all-to-all-start = ((bf16[8,48,1024]{2,1,0:T(8,128)(2,1)}), bf16[8,48,1024]{2,1,0:T(8,128)(2,1)S(1)}, u32[]{:S(2)}, u32[]{:S(2)}) async-start(bf16[8,48,1024]{2,1,0:T(8,128)(2,1)} %prep.1), calls=%async_computation | async-start | bytes 1572864 | tf_op jit(solution)/shard_map/all_to_all | solution.py:334
  9.6 1.6 %collective-permute-start.3 = (bf16[512,256]{1,0:T(8,128)(2,1)}, bf16[512,256]{1,0:T(8,128)(2,1)S(1)}, u32[]{:S(2)}, u32[]{:S(2)}) collective-permute-start(bf16[512,256]{1,0:T(8,128)(2,1)} %rest_0_.1), channel_id=1, source_target_pairs={{0,2},{1,3},{2,4},{3,5},{4,6},{5,7},{6,8},{7,9},{8,10},{9,11},{10,... | collective-permute-start | bytes 786440 | tf_op jit(solution)/shard_map/ppermute | solution.py:324
  11.2 4.0 %collective-permute-start.7 = (bf16[512,256]{1,0:T(8,128)(2,1)}, bf16[512,256]{1,0:T(8,128)(2,1)S(1)}, u32[]{:S(2)}, u32[]{:S(2)}) collective-permute-start(bf16[512,256]{1,0:T(8,128)(2,1)} %rest_0_.1), channel_id=1, source_target_pairs={{0,14},{1,15},{2,0},{3,1},{4,2},{5,3},{6,4},{7,5},{8,6},{9,7},{10,... | collective-permute-start | bytes 786440 | tf_op jit(solution)/shard_map/ppermute | solution.py:325
  15.2 7.7 %early.1 = (f32[512,128]{1,0:T(8,128)}, f32[512,128]{1,0:T(8,128)}) custom-call(s32[2]{0:T(128)} %keys.5, f32[64,128]{1,0:T(8,128)} %bitcast.10, bf16[512,8192]{1,0:T(8,128)(2,1)} %bitcast.6), custom_call_target="tpu_custom_call" | custom-call | flops 2147483648 | bytes 12582912 | tf_op jit(solution)/shard_map/early/pallas_call | solution.py:336
  23.0 0.0 copy-start
  23.0 0.0 collective-permute-done.3.rest_1_
  23.0 0.1 collective-permute-start.4
  23.1 0.0 all-to-all-done.w_in
  23.1 0.0 copy-start.1
  23.1 0.9 %copy-done.1 = bf16[8,48,1024]{2,1,0:T(8,128)(2,1)} copy-done((bf16[8,48,1024]{2,1,0:T(8,128)(2,1)}, bf16[8,48,1024]{2,1,0:T(8,128)(2,1)S(1)}, u32[]{:S(2)}) %copy-start.1) | copy-done | bytes 786456
  24.0 7.7 %features.1 = f32[8,128,128]{2,1,0:T(8,128)} custom-call(s32[1]{0:T(128)} %bitcast.2.me, s32[2]{0:T(128)} %keys.5, s32[2]{0:T(128)} %lengths.1, s32[2,256]{1,0:T(2,128)} %index_in.1, f32[512,128]{1,0:T(8,128)} %get-tuple-element.15.acc_in, f32[512,128]{1,0:T(8,128)} %get-tuple-element.16.sq_in, bf16[8,48,1024]{2,1,0:T(8,128)(2,1)} %copy-done.1, ...), custom_call_target="tpu_custom_call" | custom-call | flops 2147483648 | bytes 12582912 | tf_op jit(solution)/shard_map/features/pallas_call | solution.py:354
  31.7 6.6 %all-to-all-start.1 = ((f32[8,128,128]{2,1,0:T(8,128)}), f32[8,128,128]{2,1,0:T(8,128)S(1)}, u32[]{:S(2)}, u32[]{:S(2)}) async-start(f32[8,128,128]{2,1,0:T(8,128)} %features.1), calls=%async_computation.1 | async-start | bytes 1048576 | tf_op jit(solution)/shard_map/all_to_all | solution.py:389
  38.3 0.0 collective-permute-done.7.rest_7_
  38.3 2.9 %collective-permute-start.8 = (bf16[512,256]{1,0:T(8,128)(2,1)S(1)}, bf16[512,256]{1,0:T(8,128)(2,1)S(1)}, u32[]{:S(2)}, u32[]{:S(2)}) collective-permute-start(bf16[512,256]{1,0:T(8,128)(2,1)S(1)} %collective-permute-done.7.rest_7_), channel_id=1, source_target_pairs={{0,14},{1,15},{2,0},{3,1},{4,2},{5,3},{6,4},{7,5},{8,6},{9,7},{10,... | collective-permute-start | bytes 786440 | tf_op jit(solution)/shard_map/ppermute | solution.py:352
  41.1 0.0 collective-permute-done.4.rest_2_
  41.1 0.0 collective-permute-start.5
  41.1 5.9 %all-to-all-done.1.parts = f32[8,128,128]{2,1,0:T(8,128)S(1)} async-done(((f32[8,128,128]{2,1,0:T(8,128)}), f32[8,128,128]{2,1,0:T(8,128)S(1)}, u32[]{:S(2)}, u32[]{:S(2)}) %all-to-all-start.1) | async-done | bytes 524320 | tf_op jit(solution)/shard_map/all_to_all | solution.py:389
  47.1 0.1 sum_features.1
  47.2 3.4 %collective-permute-start = (bf16[16,256]{1,0:T(8,128)(2,1)S(1)}, bf16[16,256]{1,0:T(8,128)(2,1)S(1)}, u32[]{:S(2)}, u32[]{:S(2)}) collective-permute-start(bf16[16,256]{1,0:T(8,128)(2,1)S(1)} %get-tuple-element.18), channel_id=1, source_target_pairs={{0,1},{1,0},{2,3},{3,2},{4,5},{5,4},{6,7},{7,6},{8,9},{9,8},{10,11... | collective-permute-start | bytes 24584 | tf_op jit(solution)/shard_map/ppermute | solution.py:399
  50.6 0.4 collective-permute-start.1
  51.0 1.3 %collective-permute-start.2 = (bf16[16,256]{1,0:T(8,128)(2,1)S(1)}, bf16[16,256]{1,0:T(8,128)(2,1)S(1)}, u32[]{:S(2)}, u32[]{:S(2)}) collective-permute-start(bf16[16,256]{1,0:T(8,128)(2,1)S(1)} %get-tuple-element.20), channel_id=1, source_target_pairs={{0,17},{1,16},{2,19},{3,18},{4,21},{5,20},{6,23},{7,22},{8,25},{9,... | collective-permute-start | bytes 24584 | tf_op jit(solution)/shard_map/ppermute | solution.py:399
  52.3 0.0 collective-permute-done.8.rest_6_
  52.3 2.8 %collective-permute-start.9 = (bf16[512,256]{1,0:T(8,128)(2,1)S(1)}, bf16[512,256]{1,0:T(8,128)(2,1)S(1)}, u32[]{:S(2)}, u32[]{:S(2)}) collective-permute-start(bf16[512,256]{1,0:T(8,128)(2,1)S(1)} %collective-permute-done.8.rest_6_), channel_id=1, source_target_pairs={{0,14},{1,15},{2,0},{3,1},{4,2},{5,3},{6,4},{7,5},{8,6},{9,7},{10,... | collective-permute-start | bytes 786440 | tf_op jit(solution)/shard_map/ppermute | solution.py:388
  55.1 0.0 collective-permute-done.5.rest_3_
  55.1 0.0 collective-permute-start.6
  55.1 0.0 collective-permute-done
  55.1 0.0 collective-permute-done.1
  55.1 0.0 collective-permute-done.2
  55.1 0.7 broadcast_in_dim.2
  55.9 3.4 %all-to-all-start.2 = ((bf16[8,64,256]{2,1,0:T(8,128)(2,1)}), bf16[8,64,256]{2,1,0:T(8,128)(2,1)S(1)}, u32[]{:S(2)}, u32[]{:S(2)}) async-start(bf16[8,64,256]{2,1,0:T(8,128)(2,1)} %broadcast_in_dim.2), calls=%async_computation.2 | async-start | bytes 524288 | tf_op jit(solution)/shard_map/all_to_all | solution.py:404
  59.3 1.4 %collective-permute-done.9.rest_5_ = bf16[512,256]{1,0:T(8,128)(2,1)S(1)} collective-permute-done((bf16[512,256]{1,0:T(8,128)(2,1)S(1)}, bf16[512,256]{1,0:T(8,128)(2,1)S(1)}, u32[]{:S(2)}, u32[]{:S(2)}) %collective-permute-start.9) | collective-permute-done | bytes 262176 | tf_op jit(solution)/shard_map/ppermute | solution.py:388
  60.7 3.1 %collective-permute-done.6.rest_4_ = bf16[512,256]{1,0:T(8,128)(2,1)S(1)} collective-permute-done((bf16[512,256]{1,0:T(8,128)(2,1)S(1)}, bf16[512,256]{1,0:T(8,128)(2,1)S(1)}, u32[]{:S(2)}, u32[]{:S(2)}) %collective-permute-start.6) | collective-permute-done | bytes 262176 | tf_op jit(solution)/shard_map/ppermute | solution.py:402
  63.8 3.0 %all-to-all-done.2.feats = bf16[8,64,256]{2,1,0:T(8,128)(2,1)S(1)} async-done(((bf16[8,64,256]{2,1,0:T(8,128)(2,1)}), bf16[8,64,256]{2,1,0:T(8,128)(2,1)S(1)}, u32[]{:S(2)}, u32[]{:S(2)}) %all-to-all-start.2) | async-done | bytes 262176 | tf_op jit(solution)/shard_map/all_to_all | solution.py:404
  66.8 0.0 copy-done
  66.8 0.8 %partial_scores.1 = (f32[16,768]{1,0:T(8,128)S(1)}, f32[16,768]{1,0:T(8,128)S(1)}, f32[16,768]{1,0:T(8,128)S(1)}, f32[16,768]{1,0:T(8,128)S(1)}) custom-call(s32[1]{0:T(128)} %bitcast.z_at.at, bf16[8,64,256]{2,1,0:T(8,128)(2,1)S(1)} %all-to-all-done.2.feats, bf16[512,256]{1,0:T(8,128)(2,1)S(1)} %copy-done, ...), custom_call_target="tpu_custom_call" | custom-call | tf_op jit(solution)/shard_map/partial_scores/pallas_call | solution.py:407
  67.6 2.1 %collective-permute-start.10 = (f32[16,768]{1,0:T(8,128)S(1)}, f32[16,768]{1,0:T(8,128)S(1)}, u32[]{:S(2)}, u32[]{:S(2)}) collective-permute-start(f32[16,768]{1,0:T(8,128)S(1)} %get-tuple-element.22), channel_id=1, source_target_pairs={{0,1},{1,0},{2,3},{3,2},{4,5},{5,4},{6,7},{7,6},{8,9},{9,8},{10,11... | collective-permute-start | bytes 147464 | tf_op jit(solution)/shard_map/ppermute | solution.py:415
  69.8 0.4 collective-permute-start.11
  70.1 1.4 %collective-permute-start.12 = (f32[16,768]{1,0:T(8,128)S(1)}, f32[16,768]{1,0:T(8,128)S(1)}, u32[]{:S(2)}, u32[]{:S(2)}) collective-permute-start(f32[16,768]{1,0:T(8,128)S(1)} %get-tuple-element.24), channel_id=1, source_target_pairs={{0,17},{1,16},{2,19},{3,18},{4,21},{5,20},{6,23},{7,22},{8,25},{9,... | collective-permute-start | bytes 147464 | tf_op jit(solution)/shard_map/ppermute | solution.py:415
  71.5 0.0 collective-permute-done.10.one
  71.5 1.2 %collective-permute-done.11.two = f32[16,768]{1,0:T(8,128)S(1)} collective-permute-done((f32[16,768]{1,0:T(8,128)S(1)}, f32[16,768]{1,0:T(8,128)S(1)}, u32[]{:S(2)}, u32[]{:S(2)}) %collective-permute-start.11) | collective-permute-done | bytes 49184 | tf_op jit(solution)/shard_map/ppermute | solution.py:415
  72.7 1.6 %collective-permute-done.12.three = f32[16,768]{1,0:T(8,128)S(1)} collective-permute-done((f32[16,768]{1,0:T(8,128)S(1)}, f32[16,768]{1,0:T(8,128)S(1)}, u32[]{:S(2)}, u32[]{:S(2)}) %collective-permute-start.12) | collective-permute-done | bytes 49184 | tf_op jit(solution)/shard_map/ppermute | solution.py:415
  74.3 0.6 scores.1
  (1 shorter events, 0.0 us)
Async XLA Ops:
  2.1 21.0 %all-to-all-start = ((bf16[8,48,1024]{2,1,0:T(8,128)(2,1)}), bf16[8,48,1024]{2,1,0:T(8,128)(2,1)S(1)}, u32[]{:S(2)}, u32[]{:S(2)}) async-start(bf16[8,48,1024]{2,1,0:T(8,128)(2,1)} %prep.1), calls=%async_computation | async-start | bytes 1572864 | tf_op jit(solution)/shard_map/all_to_all | solution.py:334
  9.6 13.4 %collective-permute-start.3 = (bf16[512,256]{1,0:T(8,128)(2,1)}, bf16[512,256]{1,0:T(8,128)(2,1)S(1)}, u32[]{:S(2)}, u32[]{:S(2)}) collective-permute-start(bf16[512,256]{1,0:T(8,128)(2,1)} %rest_0_.1), channel_id=1, source_target_pairs={{0,2},{1,3},{2,4},{3,5},{4,6},{5,7},{6,8},{7,9},{8,10},{9,11},{10,... | collective-permute-start | bytes 786440 | tf_op jit(solution)/shard_map/ppermute | solution.py:324
  11.2 27.1 %collective-permute-start.7 = (bf16[512,256]{1,0:T(8,128)(2,1)}, bf16[512,256]{1,0:T(8,128)(2,1)S(1)}, u32[]{:S(2)}, u32[]{:S(2)}) collective-permute-start(bf16[512,256]{1,0:T(8,128)(2,1)} %rest_0_.1), channel_id=1, source_target_pairs={{0,14},{1,15},{2,0},{3,1},{4,2},{5,3},{6,4},{7,5},{8,6},{9,7},{10,... | collective-permute-start | bytes 786440 | tf_op jit(solution)/shard_map/ppermute | solution.py:325
  23.0 43.8 %copy-start = (bf16[512,256]{1,0:T(8,128)(2,1)S(1)}, bf16[512,256]{1,0:T(8,128)(2,1)}, u32[]{:S(2)}) copy-start(bf16[512,256]{1,0:T(8,128)(2,1)} %rest_0_.1) | copy-start | bytes 786436
  23.0 18.1 %collective-permute-start.4 = (bf16[512,256]{1,0:T(8,128)(2,1)S(1)}, bf16[512,256]{1,0:T(8,128)(2,1)S(1)}, u32[]{:S(2)}, u32[]{:S(2)}) collective-permute-start(bf16[512,256]{1,0:T(8,128)(2,1)S(1)} %collective-permute-done.3.rest_1_), channel_id=1, source_target_pairs={{0,2},{1,3},{2,4},{3,5},{4,6},{5,7},{6,8},{7,9},{8,10},{9,11},{10,... | collective-permute-start | bytes 786440 | tf_op jit(solution)/shard_map/ppermute | solution.py:351
  23.1 0.9 %copy-start.1 = (bf16[8,48,1024]{2,1,0:T(8,128)(2,1)}, bf16[8,48,1024]{2,1,0:T(8,128)(2,1)S(1)}, u32[]{:S(2)}) copy-start(bf16[8,48,1024]{2,1,0:T(8,128)(2,1)S(1)} %all-to-all-done.w_in) | copy-start | bytes 2359300
  31.7 15.4 %all-to-all-start.1 = ((f32[8,128,128]{2,1,0:T(8,128)}), f32[8,128,128]{2,1,0:T(8,128)S(1)}, u32[]{:S(2)}, u32[]{:S(2)}) async-start(f32[8,128,128]{2,1,0:T(8,128)} %features.1), calls=%async_computation.1 | async-start | bytes 1048576 | tf_op jit(solution)/shard_map/all_to_all | solution.py:389
  38.3 14.0 %collective-permute-start.8 = (bf16[512,256]{1,0:T(8,128)(2,1)S(1)}, bf16[512,256]{1,0:T(8,128)(2,1)S(1)}, u32[]{:S(2)}, u32[]{:S(2)}) collective-permute-start(bf16[512,256]{1,0:T(8,128)(2,1)S(1)} %collective-permute-done.7.rest_7_), channel_id=1, source_target_pairs={{0,14},{1,15},{2,0},{3,1},{4,2},{5,3},{6,4},{7,5},{8,6},{9,7},{10,... | collective-permute-start | bytes 786440 | tf_op jit(solution)/shard_map/ppermute | solution.py:352
  41.1 14.0 %collective-permute-start.5 = (bf16[512,256]{1,0:T(8,128)(2,1)S(1)}, bf16[512,256]{1,0:T(8,128)(2,1)S(1)}, u32[]{:S(2)}, u32[]{:S(2)}) collective-permute-start(bf16[512,256]{1,0:T(8,128)(2,1)S(1)} %collective-permute-done.4.rest_2_), channel_id=1, source_target_pairs={{0,2},{1,3},{2,4},{3,5},{4,6},{5,7},{6,8},{7,9},{8,10},{9,11},{10,... | collective-permute-start | bytes 786440 | tf_op jit(solution)/shard_map/ppermute | solution.py:387
  47.2 8.0 %collective-permute-start = (bf16[16,256]{1,0:T(8,128)(2,1)S(1)}, bf16[16,256]{1,0:T(8,128)(2,1)S(1)}, u32[]{:S(2)}, u32[]{:S(2)}) collective-permute-start(bf16[16,256]{1,0:T(8,128)(2,1)S(1)} %get-tuple-element.18), channel_id=1, source_target_pairs={{0,1},{1,0},{2,3},{3,2},{4,5},{5,4},{6,7},{7,6},{8,9},{9,8},{10,11... | collective-permute-start | bytes 24584 | tf_op jit(solution)/shard_map/ppermute | solution.py:399
  50.6 4.5 %collective-permute-start.1 = (bf16[16,256]{1,0:T(8,128)(2,1)S(1)}, bf16[16,256]{1,0:T(8,128)(2,1)S(1)}, u32[]{:S(2)}, u32[]{:S(2)}) collective-permute-start(bf16[16,256]{1,0:T(8,128)(2,1)S(1)} %get-tuple-element.19), channel_id=1, source_target_pairs={{0,16},{1,17},{2,18},{3,19},{4,20},{5,21},{6,22},{7,23},{8,24},{9,... | collective-permute-start | bytes 24584 | tf_op jit(solution)/shard_map/ppermute | solution.py:399
  51.0 4.2 %collective-permute-start.2 = (bf16[16,256]{1,0:T(8,128)(2,1)S(1)}, bf16[16,256]{1,0:T(8,128)(2,1)S(1)}, u32[]{:S(2)}, u32[]{:S(2)}) collective-permute-start(bf16[16,256]{1,0:T(8,128)(2,1)S(1)} %get-tuple-element.20), channel_id=1, source_target_pairs={{0,17},{1,16},{2,19},{3,18},{4,21},{5,20},{6,23},{7,22},{8,25},{9,... | collective-permute-start | bytes 24584 | tf_op jit(solution)/shard_map/ppermute | solution.py:399
  52.3 8.3 %collective-permute-start.9 = (bf16[512,256]{1,0:T(8,128)(2,1)S(1)}, bf16[512,256]{1,0:T(8,128)(2,1)S(1)}, u32[]{:S(2)}, u32[]{:S(2)}) collective-permute-start(bf16[512,256]{1,0:T(8,128)(2,1)S(1)} %collective-permute-done.8.rest_6_), channel_id=1, source_target_pairs={{0,14},{1,15},{2,0},{3,1},{4,2},{5,3},{6,4},{7,5},{8,6},{9,7},{10,... | collective-permute-start | bytes 786440 | tf_op jit(solution)/shard_map/ppermute | solution.py:388
  55.1 8.6 %collective-permute-start.6 = (bf16[512,256]{1,0:T(8,128)(2,1)S(1)}, bf16[512,256]{1,0:T(8,128)(2,1)S(1)}, u32[]{:S(2)}, u32[]{:S(2)}) collective-permute-start(bf16[512,256]{1,0:T(8,128)(2,1)S(1)} %collective-permute-done.5.rest_3_), channel_id=1, source_target_pairs={{0,2},{1,3},{2,4},{3,5},{4,6},{5,7},{6,8},{7,9},{8,10},{9,11},{10,... | collective-permute-start | bytes 786440 | tf_op jit(solution)/shard_map/ppermute | solution.py:402
  55.9 10.9 %all-to-all-start.2 = ((bf16[8,64,256]{2,1,0:T(8,128)(2,1)}), bf16[8,64,256]{2,1,0:T(8,128)(2,1)S(1)}, u32[]{:S(2)}, u32[]{:S(2)}) async-start(bf16[8,64,256]{2,1,0:T(8,128)(2,1)} %broadcast_in_dim.2), calls=%async_computation.2 | async-start | bytes 524288 | tf_op jit(solution)/shard_map/all_to_all | solution.py:404
  67.6 3.9 %collective-permute-start.10 = (f32[16,768]{1,0:T(8,128)S(1)}, f32[16,768]{1,0:T(8,128)S(1)}, u32[]{:S(2)}, u32[]{:S(2)}) collective-permute-start(f32[16,768]{1,0:T(8,128)S(1)} %get-tuple-element.22), channel_id=1, source_target_pairs={{0,1},{1,0},{2,3},{3,2},{4,5},{5,4},{6,7},{7,6},{8,9},{9,8},{10,11... | collective-permute-start | bytes 147464 | tf_op jit(solution)/shard_map/ppermute | solution.py:415
  69.8 3.0 %collective-permute-start.11 = (f32[16,768]{1,0:T(8,128)S(1)}, f32[16,768]{1,0:T(8,128)S(1)}, u32[]{:S(2)}, u32[]{:S(2)}) collective-permute-start(f32[16,768]{1,0:T(8,128)S(1)} %get-tuple-element.23), channel_id=1, source_target_pairs={{0,16},{1,17},{2,18},{3,19},{4,20},{5,21},{6,22},{7,23},{8,24},{9,... | collective-permute-start | bytes 147464 | tf_op jit(solution)/shard_map/ppermute | solution.py:415
  70.1 4.2 %collective-permute-start.12 = (f32[16,768]{1,0:T(8,128)S(1)}, f32[16,768]{1,0:T(8,128)S(1)}, u32[]{:S(2)}, u32[]{:S(2)}) collective-permute-start(f32[16,768]{1,0:T(8,128)S(1)} %get-tuple-element.24), channel_id=1, source_target_pairs={{0,17},{1,16},{2,19},{3,18},{4,21},{5,20},{6,23},{7,22},{8,25},{9,... | collective-permute-start | bytes 147464 | tf_op jit(solution)/shard_map/ppermute | solution.py:415

commit v6 on v5

--- a/solution.py
+++ b/solution.py
@@ -77,14 +77,16 @@
     copies = copies_of([(gain_in, gain)] + x_pieces(x_in, x), sems)
     for copy in copies:
         copy.start()
+    for n in range(0, width, 128):
+        table[0:64, n : n + 128] = signs(keys[0], 1, n, 128, 64).astype(BF16)
     copies[0].wait()
     for n in range(0, width, 128):
         gain_row = gain[n // 128 : n // 128 + 1, :]
-        gain_hi = gain_row.astype(BF16).astype(F32)
-        gain_lo = gain_row - gain_hi
-        plus = sign_bits(keys[0], 1, n, 128, 64)
-        table[0:64, n : n + 128] = jnp.where(plus, gain_hi, -gain_hi).astype(BF16)
-        table[64:128, n : n + 128] = jnp.where(plus, gain_lo, -gain_lo).astype(BF16)
+        gain_hi = gain_row.astype(BF16)
+        gain_lo = (gain_row - gain_hi.astype(F32)).astype(BF16)
+        plus = table[0:64, n : n + 128]
+        table[64:128, n : n + 128] = plus * gain_lo
+        table[0:64, n : n + 128] = plus * gain_hi
     acc[...] = jnp.zeros_like(acc)
     sq[...] = jnp.zeros_like(sq)
     @pl.loop(0, steps // 2)
@@ -252,19 +254,34 @@
         + [jnp.zeros((12, 128), F32)],
         axis=0,
     )
-    for k, ref in enumerate((own, one, two, three)):
-        ref[:, 0:512] = dots[16 * k : 16 * k + 16]
-        ref[:, 512:640] = esq[16 * k : 16 * k + 16]
+    own[:, 0:512] = dots[0:16]
+    own[:, 512:640] = esq[0:16]
+    own[:, 640:768] = rows
+    rows_hi, rows_lo = split(rows[0:4])
+    rows = jnp.concatenate(
+        [rows_hi.astype(F32), rows_lo.astype(F32), rows[8:16]], axis=0
+    ).astype(BF16)
+    low = lax.broadcasted_iota(I32, (16, 128), 1) < 64
+    for k, ref in ((1, one), (2, two), (3, three)):
+        ref[:, 0:512] = dots[16 * k : 16 * k + 16].astype(BF16)
+        hi, lo = split(esq[16 * k : 16 * k + 16])
+        ref[:, 512:640] = jnp.where(low, hi.astype(F32), lo.astype(F32)).astype(BF16)
         ref[:, 640:768] = rows
 
 
 def final_kernel(own, one, two, three, out):
-    total = (own[...] + one[...]) + (two[...] + three[...])
-    enorm = lax.rsqrt(total[:, 512:640] + 1e-06)
-    rnorm = lax.rsqrt(total[:, 640:768] + 1e-06)
+    dots, esq, rsq = own[:, 0:512], own[:, 512:640], own[0:4, 640:768]
+    for ref in (one, two, three):
+        dots = dots + ref[:, 0:512].astype(F32)
+        parts = ref[:, 512:640].astype(F32)
+        esq = esq + (parts + pltpu.roll(parts, 64, 1))
+        parts = ref[:, 640:768].astype(F32)
+        rsq = rsq + (parts[0:4] + parts[4:8])
+    enorm = lax.rsqrt(esq + 1e-06)
+    rnorm = lax.rsqrt(rsq + 1e-06)
     for q in range(4):
         out[:, 128 * q : 128 * q + 128] = (
-            total[:, 128 * q : 128 * q + 128] * enorm * rnorm[q : q + 1, :]
+            dots[:, 128 * q : 128 * q + 128] * enorm * rnorm[q : q + 1, :]
         )
 
 
@@ -407,7 +424,7 @@
     pieces = kernel(
         score_kernel,
         "partial_scores",
-        [shape((16, 768), F32)] * 4,
+        [shape((16, 768), F32)] + [shape((16, 768), BF16)] * 3,
         [SMEM] + [VMEM] * 9,
         vmem=8,
     )(z_at, feats, *refs)

time: 75.3 us -> 74.7 us (level)
  waiting for transfers between devices: 16.3 us -> 15.3 us
where the time goes in v6:
time: 74.7 us; the launch traced here: 74.3 us
  starting transfers between devices  38.4 us (51%)
  Pallas kernels  18.9 us (25%)
  waiting for transfers between devices  15.3 us (20%)
  local copies, waits for them, and re-layouts  1.6 us (2%)
    ppermute x6, starting transfers between devices, per_device(): lax.ppermute(piece, 'dp', swap)  9.03 us
    pallas_call x1, Pallas kernels, per_device(): kernel(main_kernel, 'features', shape((8, 128, 128), F32), [SMEM] * 3 + [...  7.69 us
    all_to_all x1, starting transfers between devices, per_device(): weights = lax.all_to_all(weights, 'fsdp', 0, 0)  7.48 us
    pallas_call x1, Pallas kernels, per_device(): kernel(early_kernel, 'early', [shape((tokens, 128), F32)] * 2, [SMEM] + [...  7.47 us
    all_to_all x1, starting transfers between devices, per_device(): features = lax.all_to_all(features, 'fsdp', 0, 0)  6.58 us
    all_to_all x1, waiting for transfers between devices, per_device(): features = lax.all_to_all(features, 'fsdp', 0, 0)  5.63 us
    ppermute x1, starting transfers between devices, per_device(): refs_down = [lax.ppermute(reference_gradients, 'dp', down)]  4.03 us
    all_to_all x1, starting transfers between devices, per_device(): feats = lax.all_to_all(feats, 'fsdp', 0, 0)  3.41 us
  transfers between devices with their start and end apart: 16, of which 6 were waited for; matrix products, arithmetic and copies ran while one was open for 1% of the time, Pallas kernels for 21%

profile of v6, /device:TPU:1, one launch (start us, length us, event | category | flops | bytes accessed | tf_op | source)
XLA Modules:
  0.0 74.3 jit_solution(10269540015358185371)
XLA Ops:
  0.0 2.1 %prep.1 = bf16[8,48,1024]{2,1,0:T(8,128)(2,1)} custom-call(s32[1]{0:T(128)} %bitcast.2.me, s32[1]{0:T(128)} %bitcast.1.four_at.me, s32[1]{0:T(128)} %bitcast.z_at.at, s32[2]{0:T(128)} %keys.5, f32[64,128]{1,0:T(8,128)} %bitcast.9, bf16[1024,128]{1,0:T(8,128)(2,1)} %down.1, bf16[128,128]{1,0:T(8,128)(2,1)} %up.1), custom_call_target="tpu_custom_call" | custom-call | tf_op jit(solution)/shard_map/prep/pallas_call | solution.py:344
  2.1 7.5 %all-to-all-start = ((bf16[8,48,1024]{2,1,0:T(8,128)(2,1)}), bf16[8,48,1024]{2,1,0:T(8,128)(2,1)S(1)}, u32[]{:S(2)}, u32[]{:S(2)}) async-start(bf16[8,48,1024]{2,1,0:T(8,128)(2,1)} %prep.1), calls=%async_computation | async-start | bytes 1572864 | tf_op jit(solution)/shard_map/all_to_all | solution.py:351
  9.6 1.6 %collective-permute-start.3 = (bf16[512,256]{1,0:T(8,128)(2,1)}, bf16[512,256]{1,0:T(8,128)(2,1)S(1)}, u32[]{:S(2)}, u32[]{:S(2)}) collective-permute-start(bf16[512,256]{1,0:T(8,128)(2,1)} %rest_0_.1), channel_id=1, source_target_pairs={{0,2},{1,3},{2,4},{3,5},{4,6},{5,7},{6,8},{7,9},{8,10},{9,11},{10,... | collective-permute-start | bytes 786440 | tf_op jit(solution)/shard_map/ppermute | solution.py:341
  11.2 4.0 %collective-permute-start.7 = (bf16[512,256]{1,0:T(8,128)(2,1)}, bf16[512,256]{1,0:T(8,128)(2,1)S(1)}, u32[]{:S(2)}, u32[]{:S(2)}) collective-permute-start(bf16[512,256]{1,0:T(8,128)(2,1)} %rest_0_.1), channel_id=1, source_target_pairs={{0,14},{1,15},{2,0},{3,1},{4,2},{5,3},{6,4},{7,5},{8,6},{9,7},{10,... | collective-permute-start | bytes 786440 | tf_op jit(solution)/shard_map/ppermute | solution.py:342
  15.2 7.5 %early.1 = (f32[512,128]{1,0:T(8,128)}, f32[512,128]{1,0:T(8,128)}) custom-call(s32[2]{0:T(128)} %keys.5, f32[64,128]{1,0:T(8,128)} %bitcast.10, bf16[512,8192]{1,0:T(8,128)(2,1)} %bitcast.6), custom_call_target="tpu_custom_call" | custom-call | flops 2147483648 | bytes 12582912 | tf_op jit(solution)/shard_map/early/pallas_call | solution.py:353
  22.7 0.0 copy-start
  22.7 0.0 collective-permute-done.3.rest_1_
  22.7 0.1 collective-permute-start.4
  22.8 0.0 all-to-all-done.w_in
  22.8 0.0 copy-start.1
  22.8 0.9 %copy-done.1 = bf16[8,48,1024]{2,1,0:T(8,128)(2,1)} copy-done((bf16[8,48,1024]{2,1,0:T(8,128)(2,1)}, bf16[8,48,1024]{2,1,0:T(8,128)(2,1)S(1)}, u32[]{:S(2)}) %copy-start.1) | copy-done | bytes 786456
  23.7 7.7 %features.1 = f32[8,128,128]{2,1,0:T(8,128)} custom-call(s32[1]{0:T(128)} %bitcast.2.me, s32[2]{0:T(128)} %keys.5, s32[2]{0:T(128)} %lengths.1, s32[2,256]{1,0:T(2,128)} %index_in.1, f32[512,128]{1,0:T(8,128)} %get-tuple-element.15.acc_in, f32[512,128]{1,0:T(8,128)} %get-tuple-element.16.sq_in, bf16[8,48,1024]{2,1,0:T(8,128)(2,1)} %copy-done.1, ...), custom_call_target="tpu_custom_call" | custom-call | flops 2147483648 | bytes 12582912 | tf_op jit(solution)/shard_map/features/pallas_call | solution.py:371
  31.4 6.6 %all-to-all-start.1 = ((f32[8,128,128]{2,1,0:T(8,128)}), f32[8,128,128]{2,1,0:T(8,128)S(1)}, u32[]{:S(2)}, u32[]{:S(2)}) async-start(f32[8,128,128]{2,1,0:T(8,128)} %features.1), calls=%async_computation.1 | async-start | bytes 1048576 | tf_op jit(solution)/shard_map/all_to_all | solution.py:406
  38.0 0.0 collective-permute-done.7.rest_7_
  38.0 3.1 %collective-permute-start.8 = (bf16[512,256]{1,0:T(8,128)(2,1)S(1)}, bf16[512,256]{1,0:T(8,128)(2,1)S(1)}, u32[]{:S(2)}, u32[]{:S(2)}) collective-permute-start(bf16[512,256]{1,0:T(8,128)(2,1)S(1)} %collective-permute-done.7.rest_7_), channel_id=1, source_target_pairs={{0,14},{1,15},{2,0},{3,1},{4,2},{5,3},{6,4},{7,5},{8,6},{9,7},{10,... | collective-permute-start | bytes 786440 | tf_op jit(solution)/shard_map/ppermute | solution.py:369
  41.1 0.0 collective-permute-done.4.rest_2_
  41.1 0.0 collective-permute-start.5
  41.1 5.6 %all-to-all-done.1.parts = f32[8,128,128]{2,1,0:T(8,128)S(1)} async-done(((f32[8,128,128]{2,1,0:T(8,128)}), f32[8,128,128]{2,1,0:T(8,128)S(1)}, u32[]{:S(2)}, u32[]{:S(2)}) %all-to-all-start.1) | async-done | bytes 524320 | tf_op jit(solution)/shard_map/all_to_all | solution.py:406
  46.8 0.1 sum_features.1
  46.9 3.4 %collective-permute-start = (bf16[16,256]{1,0:T(8,128)(2,1)S(1)}, bf16[16,256]{1,0:T(8,128)(2,1)S(1)}, u32[]{:S(2)}, u32[]{:S(2)}) collective-permute-start(bf16[16,256]{1,0:T(8,128)(2,1)S(1)} %get-tuple-element.18), channel_id=1, source_target_pairs={{0,1},{1,0},{2,3},{3,2},{4,5},{5,4},{6,7},{7,6},{8,9},{9,8},{10,11... | collective-permute-start | bytes 24584 | tf_op jit(solution)/shard_map/ppermute | solution.py:416
  50.3 0.4 collective-permute-start.1
  50.7 1.4 %collective-permute-start.2 = (bf16[16,256]{1,0:T(8,128)(2,1)S(1)}, bf16[16,256]{1,0:T(8,128)(2,1)S(1)}, u32[]{:S(2)}, u32[]{:S(2)}) collective-permute-start(bf16[16,256]{1,0:T(8,128)(2,1)S(1)} %get-tuple-element.20), channel_id=1, source_target_pairs={{0,17},{1,16},{2,19},{3,18},{4,21},{5,20},{6,23},{7,22},{8,25},{9,... | collective-permute-start | bytes 24584 | tf_op jit(solution)/shard_map/ppermute | solution.py:416
  52.0 0.0 collective-permute-done.8.rest_6_
  52.0 3.1 %collective-permute-start.9 = (bf16[512,256]{1,0:T(8,128)(2,1)S(1)}, bf16[512,256]{1,0:T(8,128)(2,1)S(1)}, u32[]{:S(2)}, u32[]{:S(2)}) collective-permute-start(bf16[512,256]{1,0:T(8,128)(2,1)S(1)} %collective-permute-done.8.rest_6_), channel_id=1, source_target_pairs={{0,14},{1,15},{2,0},{3,1},{4,2},{5,3},{6,4},{7,5},{8,6},{9,7},{10,... | collective-permute-start | bytes 786440 | tf_op jit(solution)/shard_map/ppermute | solution.py:405
  55.1 0.0 collective-permute-done.5.rest_3_
  55.1 0.0 collective-permute-start.6
  55.1 0.0 collective-permute-done
  55.1 0.0 collective-permute-done.1
  55.1 0.0 collective-permute-done.2
  55.1 0.7 broadcast_in_dim.2
  55.9 3.4 %all-to-all-start.2 = ((bf16[8,64,256]{2,1,0:T(8,128)(2,1)}), bf16[8,64,256]{2,1,0:T(8,128)(2,1)S(1)}, u32[]{:S(2)}, u32[]{:S(2)}) async-start(bf16[8,64,256]{2,1,0:T(8,128)(2,1)} %broadcast_in_dim.2), calls=%async_computation.2 | async-start | bytes 524288 | tf_op jit(solution)/shard_map/all_to_all | solution.py:421
  59.3 1.4 %collective-permute-done.9.rest_5_ = bf16[512,256]{1,0:T(8,128)(2,1)S(1)} collective-permute-done((bf16[512,256]{1,0:T(8,128)(2,1)S(1)}, bf16[512,256]{1,0:T(8,128)(2,1)S(1)}, u32[]{:S(2)}, u32[]{:S(2)}) %collective-permute-start.9) | collective-permute-done | bytes 262176 | tf_op jit(solution)/shard_map/ppermute | solution.py:405
  60.7 3.1 %collective-permute-done.6.rest_4_ = bf16[512,256]{1,0:T(8,128)(2,1)S(1)} collective-permute-done((bf16[512,256]{1,0:T(8,128)(2,1)S(1)}, bf16[512,256]{1,0:T(8,128)(2,1)S(1)}, u32[]{:S(2)}, u32[]{:S(2)}) %collective-permute-start.6) | collective-permute-done | bytes 262176 | tf_op jit(solution)/shard_map/ppermute | solution.py:419
  63.8 3.0 %all-to-all-done.2.feats = bf16[8,64,256]{2,1,0:T(8,128)(2,1)S(1)} async-done(((bf16[8,64,256]{2,1,0:T(8,128)(2,1)}), bf16[8,64,256]{2,1,0:T(8,128)(2,1)S(1)}, u32[]{:S(2)}, u32[]{:S(2)}) %all-to-all-start.2) | async-done | bytes 262176 | tf_op jit(solution)/shard_map/all_to_all | solution.py:421
  66.8 0.0 copy-done
  66.8 0.8 %partial_scores.1 = (f32[16,768]{1,0:T(8,128)S(1)}, bf16[16,768]{1,0:T(8,128)(2,1)S(1)}, bf16[16,768]{1,0:T(8,128)(2,1)S(1)}, bf16[16,768]{1,0:T(8,128)(2,1)S(1)}) custom-call(s32[1]{0:T(128)} %bitcast.z_at.at, bf16[8,64,256]{2,1,0:T(8,128)(2,1)S(1)} %all-to-all-done.2.feats, bf16[512,256]{1,0:T(8,128)(2,1)S(1)} %copy-done, ...), custom_call_target="tpu_custom_call" | custom-call | tf_op jit(solution)/shard_map/partial_scores/pallas_call | solution.py:424
  67.6 2.1 %collective-permute-start.10 = (bf16[16,768]{1,0:T(8,128)(2,1)S(1)}, bf16[16,768]{1,0:T(8,128)(2,1)S(1)}, u32[]{:S(2)}, u32[]{:S(2)}) collective-permute-start(bf16[16,768]{1,0:T(8,128)(2,1)S(1)} %get-tuple-element.22), channel_id=1, source_target_pairs={{0,1},{1,0},{2,3},{3,2},{4,5},{5,4},{6,7},{7,6},{8,9},{9,8},{10,11... | collective-permute-start | bytes 73736 | tf_op jit(solution)/shard_map/ppermute | solution.py:432
  69.8 0.4 collective-permute-start.11
  70.1 1.4 %collective-permute-start.12 = (bf16[16,768]{1,0:T(8,128)(2,1)S(1)}, bf16[16,768]{1,0:T(8,128)(2,1)S(1)}, u32[]{:S(2)}, u32[]{:S(2)}) collective-permute-start(bf16[16,768]{1,0:T(8,128)(2,1)S(1)} %get-tuple-element.24), channel_id=1, source_target_pairs={{0,17},{1,16},{2,19},{3,18},{4,21},{5,20},{6,23},{7,22},{8,25},{9,... | collective-permute-start | bytes 73736 | tf_op jit(solution)/shard_map/ppermute | solution.py:432
  71.5 0.0 collective-permute-done.10.one
  71.5 1.0 %collective-permute-done.11.two = bf16[16,768]{1,0:T(8,128)(2,1)S(1)} collective-permute-done((bf16[16,768]{1,0:T(8,128)(2,1)S(1)}, bf16[16,768]{1,0:T(8,128)(2,1)S(1)}, u32[]{:S(2)}, u32[]{:S(2)}) %collective-permute-start.11) | collective-permute-done | bytes 24608 | tf_op jit(solution)/shard_map/ppermute | solution.py:432
  72.5 1.2 %collective-permute-done.12.three = bf16[16,768]{1,0:T(8,128)(2,1)S(1)} collective-permute-done((bf16[16,768]{1,0:T(8,128)(2,1)S(1)}, bf16[16,768]{1,0:T(8,128)(2,1)S(1)}, u32[]{:S(2)}, u32[]{:S(2)}) %collective-permute-start.12) | collective-permute-done | bytes 24608 | tf_op jit(solution)/shard_map/ppermute | solution.py:432
  73.6 0.7 scores.1
  (1 shorter events, 0.0 us)
Async XLA Ops:
  2.1 20.7 %all-to-all-start = ((bf16[8,48,1024]{2,1,0:T(8,128)(2,1)}), bf16[8,48,1024]{2,1,0:T(8,128)(2,1)S(1)}, u32[]{:S(2)}, u32[]{:S(2)}) async-start(bf16[8,48,1024]{2,1,0:T(8,128)(2,1)} %prep.1), calls=%async_computation | async-start | bytes 1572864 | tf_op jit(solution)/shard_map/all_to_all | solution.py:351
  9.6 13.2 %collective-permute-start.3 = (bf16[512,256]{1,0:T(8,128)(2,1)}, bf16[512,256]{1,0:T(8,128)(2,1)S(1)}, u32[]{:S(2)}, u32[]{:S(2)}) collective-permute-start(bf16[512,256]{1,0:T(8,128)(2,1)} %rest_0_.1), channel_id=1, source_target_pairs={{0,2},{1,3},{2,4},{3,5},{4,6},{5,7},{6,8},{7,9},{8,10},{9,11},{10,... | collective-permute-start | bytes 786440 | tf_op jit(solution)/shard_map/ppermute | solution.py:341
  11.2 26.8 %collective-permute-start.7 = (bf16[512,256]{1,0:T(8,128)(2,1)}, bf16[512,256]{1,0:T(8,128)(2,1)S(1)}, u32[]{:S(2)}, u32[]{:S(2)}) collective-permute-start(bf16[512,256]{1,0:T(8,128)(2,1)} %rest_0_.1), channel_id=1, source_target_pairs={{0,14},{1,15},{2,0},{3,1},{4,2},{5,3},{6,4},{7,5},{8,6},{9,7},{10,... | collective-permute-start | bytes 786440 | tf_op jit(solution)/shard_map/ppermute | solution.py:342
  22.7 44.1 %copy-start = (bf16[512,256]{1,0:T(8,128)(2,1)S(1)}, bf16[512,256]{1,0:T(8,128)(2,1)}, u32[]{:S(2)}) copy-start(bf16[512,256]{1,0:T(8,128)(2,1)} %rest_0_.1) | copy-start | bytes 786436
  22.7 18.4 %collective-permute-start.4 = (bf16[512,256]{1,0:T(8,128)(2,1)S(1)}, bf16[512,256]{1,0:T(8,128)(2,1)S(1)}, u32[]{:S(2)}, u32[]{:S(2)}) collective-permute-start(bf16[512,256]{1,0:T(8,128)(2,1)S(1)} %collective-permute-done.3.rest_1_), channel_id=1, source_target_pairs={{0,2},{1,3},{2,4},{3,5},{4,6},{5,7},{6,8},{7,9},{8,10},{9,11},{10,... | collective-permute-start | bytes 786440 | tf_op jit(solution)/shard_map/ppermute | solution.py:368
  22.8 0.9 %copy-start.1 = (bf16[8,48,1024]{2,1,0:T(8,128)(2,1)}, bf16[8,48,1024]{2,1,0:T(8,128)(2,1)S(1)}, u32[]{:S(2)}) copy-start(bf16[8,48,1024]{2,1,0:T(8,128)(2,1)S(1)} %all-to-all-done.w_in) | copy-start | bytes 2359300
  31.4 15.4 %all-to-all-start.1 = ((f32[8,128,128]{2,1,0:T(8,128)}), f32[8,128,128]{2,1,0:T(8,128)S(1)}, u32[]{:S(2)}, u32[]{:S(2)}) async-start(f32[8,128,128]{2,1,0:T(8,128)} %features.1), calls=%async_computation.1 | async-start | bytes 1048576 | tf_op jit(solution)/shard_map/all_to_all | solution.py:406
  38.0 14.0 %collective-permute-start.8 = (bf16[512,256]{1,0:T(8,128)(2,1)S(1)}, bf16[512,256]{1,0:T(8,128)(2,1)S(1)}, u32[]{:S(2)}, u32[]{:S(2)}) collective-permute-start(bf16[512,256]{1,0:T(8,128)(2,1)S(1)} %collective-permute-done.7.rest_7_), channel_id=1, source_target_pairs={{0,14},{1,15},{2,0},{3,1},{4,2},{5,3},{6,4},{7,5},{8,6},{9,7},{10,... | collective-permute-start | bytes 786440 | tf_op jit(solution)/shard_map/ppermute | solution.py:369
  41.1 14.0 %collective-permute-start.5 = (bf16[512,256]{1,0:T(8,128)(2,1)S(1)}, bf16[512,256]{1,0:T(8,128)(2,1)S(1)}, u32[]{:S(2)}, u32[]{:S(2)}) collective-permute-start(bf16[512,256]{1,0:T(8,128)(2,1)S(1)} %collective-permute-done.4.rest_2_), channel_id=1, source_target_pairs={{0,2},{1,3},{2,4},{3,5},{4,6},{5,7},{6,8},{7,9},{8,10},{9,11},{10,... | collective-permute-start | bytes 786440 | tf_op jit(solution)/shard_map/ppermute | solution.py:404
  46.9 8.2 %collective-permute-start = (bf16[16,256]{1,0:T(8,128)(2,1)S(1)}, bf16[16,256]{1,0:T(8,128)(2,1)S(1)}, u32[]{:S(2)}, u32[]{:S(2)}) collective-permute-start(bf16[16,256]{1,0:T(8,128)(2,1)S(1)} %get-tuple-element.18), channel_id=1, source_target_pairs={{0,1},{1,0},{2,3},{3,2},{4,5},{5,4},{6,7},{7,6},{8,9},{9,8},{10,11... | collective-permute-start | bytes 24584 | tf_op jit(solution)/shard_map/ppermute | solution.py:416
  50.3 4.8 %collective-permute-start.1 = (bf16[16,256]{1,0:T(8,128)(2,1)S(1)}, bf16[16,256]{1,0:T(8,128)(2,1)S(1)}, u32[]{:S(2)}, u32[]{:S(2)}) collective-permute-start(bf16[16,256]{1,0:T(8,128)(2,1)S(1)} %get-tuple-element.19), channel_id=1, source_target_pairs={{0,16},{1,17},{2,18},{3,19},{4,20},{5,21},{6,22},{7,23},{8,24},{9,... | collective-permute-start | bytes 24584 | tf_op jit(solution)/shard_map/ppermute | solution.py:416
  50.7 4.4 %collective-permute-start.2 = (bf16[16,256]{1,0:T(8,128)(2,1)S(1)}, bf16[16,256]{1,0:T(8,128)(2,1)S(1)}, u32[]{:S(2)}, u32[]{:S(2)}) collective-permute-start(bf16[16,256]{1,0:T(8,128)(2,1)S(1)} %get-tuple-element.20), channel_id=1, source_target_pairs={{0,17},{1,16},{2,19},{3,18},{4,21},{5,20},{6,23},{7,22},{8,25},{9,... | collective-permute-start | bytes 24584 | tf_op jit(solution)/shard_map/ppermute | solution.py:416
  52.0 8.6 %collective-permute-start.9 = (bf16[512,256]{1,0:T(8,128)(2,1)S(1)}, bf16[512,256]{1,0:T(8,128)(2,1)S(1)}, u32[]{:S(2)}, u32[]{:S(2)}) collective-permute-start(bf16[512,256]{1,0:T(8,128)(2,1)S(1)} %collective-permute-done.8.rest_6_), channel_id=1, source_target_pairs={{0,14},{1,15},{2,0},{3,1},{4,2},{5,3},{6,4},{7,5},{8,6},{9,7},{10,... | collective-permute-start | bytes 786440 | tf_op jit(solution)/shard_map/ppermute | solution.py:405
  55.1 8.6 %collective-permute-start.6 = (bf16[512,256]{1,0:T(8,128)(2,1)S(1)}, bf16[512,256]{1,0:T(8,128)(2,1)S(1)}, u32[]{:S(2)}, u32[]{:S(2)}) collective-permute-start(bf16[512,256]{1,0:T(8,128)(2,1)S(1)} %collective-permute-done.5.rest_3_), channel_id=1, source_target_pairs={{0,2},{1,3},{2,4},{3,5},{4,6},{5,7},{6,8},{7,9},{8,10},{9,11},{10,... | collective-permute-start | bytes 786440 | tf_op jit(solution)/shard_map/ppermute | solution.py:419
  55.9 10.9 %all-to-all-start.2 = ((bf16[8,64,256]{2,1,0:T(8,128)(2,1)}), bf16[8,64,256]{2,1,0:T(8,128)(2,1)S(1)}, u32[]{:S(2)}, u32[]{:S(2)}) async-start(bf16[8,64,256]{2,1,0:T(8,128)(2,1)} %broadcast_in_dim.2), calls=%async_computation.2 | async-start | bytes 524288 | tf_op jit(solution)/shard_map/all_to_all | solution.py:421
  67.6 3.9 %collective-permute-start.10 = (bf16[16,768]{1,0:T(8,128)(2,1)S(1)}, bf16[16,768]{1,0:T(8,128)(2,1)S(1)}, u32[]{:S(2)}, u32[]{:S(2)}) collective-permute-start(bf16[16,768]{1,0:T(8,128)(2,1)S(1)} %get-tuple-element.22), channel_id=1, source_target_pairs={{0,1},{1,0},{2,3},{3,2},{4,5},{5,4},{6,7},{7,6},{8,9},{9,8},{10,11... | collective-permute-start | bytes 73736 | tf_op jit(solution)/shard_map/ppermute | solution.py:432
  69.8 2.7 %collective-permute-start.11 = (bf16[16,768]{1,0:T(8,128)(2,1)S(1)}, bf16[16,768]{1,0:T(8,128)(2,1)S(1)}, u32[]{:S(2)}, u32[]{:S(2)}) collective-permute-start(bf16[16,768]{1,0:T(8,128)(2,1)S(1)} %get-tuple-element.23), channel_id=1, source_target_pairs={{0,16},{1,17},{2,18},{3,19},{4,20},{5,21},{6,22},{7,23},{8,24},{9,... | collective-permute-start | bytes 73736 | tf_op jit(solution)/shard_map/ppermute | solution.py:432
  70.1 3.5 %collective-permute-start.12 = (bf16[16,768]{1,0:T(8,128)(2,1)S(1)}, bf16[16,768]{1,0:T(8,128)(2,1)S(1)}, u32[]{:S(2)}, u32[]{:S(2)}) collective-permute-start(bf16[16,768]{1,0:T(8,128)(2,1)S(1)} %get-tuple-element.24), channel_id=1, source_target_pairs={{0,17},{1,16},{2,19},{3,18},{4,21},{5,20},{6,23},{7,22},{8,25},{9,... | collective-permute-start | bytes 73736 | tf_op jit(solution)/shard_map/ppermute | solution.py:432
